TPU v7x, 32 devices: a whole 2x2x4 slice. The times are simulated.
32 devices in a mesh: rep: 4 (over y, x), fsdp: 8 (over z, core).
Axes of the slice: x: 2, y: 2, z: 4, core: 2. Of those that a mesh axis runs over, the one named last changes fastest.
Arguments:
- tokens: bfloat16 [49152, 576], P(('rep', 'fsdp')), may hold values from -6 to 6
- segment: int32 [49152], P(('rep', 'fsdp')), may hold values from -1 to 767, as said below
- attn_gain: bfloat16 [2, 576], P(None, 'fsdp'), may hold values from 0.099609375 to 1.8984375
- w_query: bfloat16 [2, 576, 576], P(None, 'fsdp'), may hold values from -0.25 to 0.25
- key_weight: bfloat16 [2, 576, 192], P(None, 'fsdp'), may hold values from -0.25 to 0.25
- value_weight: bfloat16 [2, 576, 192], P(None, 'fsdp'), may hold values from -0.25 to 0.25
- w_out: bfloat16 [2, 576, 576], P(None, 'fsdp'), may hold values from -3 to 3
- mlp_gain: bfloat16 [2, 576], P(None, 'fsdp'), may hold values from 0.099609375 to 1.8984375
- gate_weight: bfloat16 [2, 576, 1536], P(None, 'fsdp'), may hold values from -0.25 to 0.25
- up_weight: bfloat16 [2, 576, 1536], P(None, 'fsdp'), may hold values from -0.25 to 0.25
- down_weight: bfloat16 [2, 1536, 576], P(None, 'fsdp'), may hold values from -0.15625 to 0.15625
- cotangent: bfloat16 [49152, 576], P(('rep', 'fsdp')), may hold values from -6 to 6
Outputs:
- out_tokens: bfloat16 [49152, 576], P(('rep', 'fsdp'))
- grad_tokens: float32 [49152, 576], P(('rep', 'fsdp'))
- grad_attn_gain: float32 [2, 576], P(None, 'fsdp')
- grad_query: float32 [2, 576, 576], P(None, 'fsdp')
- grad_key: float32 [2, 576, 192], P(None, 'fsdp')
- grad_value: float32 [2, 576, 192], P(None, 'fsdp')
- grad_out: float32 [2, 576, 576], P(None, 'fsdp')
- grad_mlp_gain: float32 [2, 576], P(None, 'fsdp')
- grad_gate: float32 [2, 576, 1536], P(None, 'fsdp')
- grad_up: float32 [2, 576, 1536], P(None, 'fsdp')
- grad_down: float32 [2, 1536, 576], P(None, 'fsdp')
Inputs may be any that keep to these rules, and one draw needn't show every extreme that they name: `segment`: each aligned block of 768 rows (one micro-batch of one device) holds whole sequences numbered 0, 1, 2, ... in order, then padding rows marked -1; no sequence has more than 512 rows and one has exactly 512; some block has no padding; some block holds 768 sequences of one row each.
All inputs are finite; a program needn't handle non-finite values.
Results may differ from a plain program's by a relative error of at most 0.025.
Values may be sent and summed in bfloat16 or wider, within the bound.
A program may use at most 384 MiB of HBM per device.

v0:
```python
import jax
import jax.numpy as jnp
from jax import lax
from jax.experimental import pallas as pl
from jax.experimental.pallas import tpu as pltpu
from jax.sharding import PartitionSpec as P

QUERY_HEADS = 9
KEY_VALUE_HEADS = 3
HEAD_WIDTH = 64
DECODER_LAYERS = 2
MICRO = 2


epsilon = 1e-05
rope_base = 100000.0
masked_fill = -1e30


def geometry(segment):
    count_of_rows = segment.shape[-1]
    row_index = jnp.arange(count_of_rows, dtype=jnp.int32)
    same_segment = segment[..., :, None] == segment[..., None, :]
    earlier = row_index[None, :] < row_index[:, None]
    position = jnp.sum(jnp.where(same_segment & earlier, 1, 0).astype(jnp.int32), axis=-1)
    allowed = same_segment & (row_index[None, :] <= row_index[:, None])
    active_rows = jnp.where(segment >= 0, 1.0, 0.0).astype(jnp.float32)[..., None]
    frequency = rope_base ** (-2.0 * jnp.arange(HEAD_WIDTH // 2, dtype=jnp.float32) / HEAD_WIDTH)
    angles = position.astype(jnp.float32)[..., None] * frequency
    return (allowed, active_rows, jnp.cos(angles)[..., None, :], jnp.sin(angles)[..., None, :])


def rotary_apply(vectors, cosine_table, sine_values):
    half_width = vectors.shape[-1] // 2
    first_half = vectors[..., :half_width]
    second_half = vectors[..., half_width:]
    return jnp.concatenate(
        [
            first_half * cosine_table - second_half * sine_values,
            second_half * cosine_table + first_half * sine_values,
        ],
        axis=-1,
    )


def rotary_inverse(vectors, cosine_table, sine_values):
    half_width = vectors.shape[-1] // 2
    first_half = vectors[..., :half_width]
    second_half = vectors[..., half_width:]
    return jnp.concatenate(
        [
            first_half * cosine_table + second_half * sine_values,
            second_half * cosine_table - first_half * sine_values,
        ],
        axis=-1,
    )


def norm_forward(value_rows, gain_row):
    factor = lax.rsqrt(jnp.mean(value_rows * value_rows, axis=-1, keepdims=True) + epsilon)
    return (value_rows * factor * gain_row, factor)


def norm_backward(value_rows, factor, gain_row, upstream):
    scaled = upstream * gain_row
    through = factor * scaled - value_rows * (factor * factor * factor) * jnp.mean(
        scaled * value_rows, axis=-1, keepdims=True
    )
    return (through, jnp.sum(upstream * value_rows * factor, axis=0))


def row_tile(count_of_rows):
    return 256 if count_of_rows % 256 == 0 else count_of_rows


def tile_mask(column_ref, row_ref, start, size):
    reach = start + size
    shape = (size, reach)
    row_number = lax.broadcasted_iota(jnp.int32, shape, 0) + start
    key_number = lax.broadcasted_iota(jnp.int32, shape, 1)
    same = column_ref[start : start + size, :] == row_ref[0, :, :reach]
    allowed = jnp.where(same & (key_number <= row_number), 1.0, 0.0)
    return jnp.concatenate([allowed] * (QUERY_HEADS // KEY_VALUE_HEADS), axis=0) > 0.5


def head_stack(ref, start, size, group):
    heads = QUERY_HEADS // KEY_VALUE_HEADS
    first = group * heads * HEAD_WIDTH
    piece = ref[start : start + size, first : first + heads * HEAD_WIDTH]
    return jnp.concatenate(
        [piece[:, j * HEAD_WIDTH : (j + 1) * HEAD_WIDTH] for j in range(heads)], axis=0
    )


def head_unstack(stacked, size):
    heads = QUERY_HEADS // KEY_VALUE_HEADS
    return [stacked[j * size : (j + 1) * size] for j in range(heads)]


def dot_rows(left, right):
    return lax.dot_general(
        left, right, (((0,), (0,)), ((), ())), preferred_element_type=jnp.float32
    )


def forward_kernel(column_ref, row_ref, query_ref, key_ref, value_ref, mixed_ref, total_ref):
    count_of_rows = query_ref.shape[0]
    size = row_tile(count_of_rows)
    scale = HEAD_WIDTH ** (-0.5)
    for start in range(0, count_of_rows, size):
        reach = start + size
        allowed = tile_mask(column_ref, row_ref, start, size)
        outputs, totals = [], []
        for group in range(KEY_VALUE_HEADS):
            lanes = slice(group * HEAD_WIDTH, (group + 1) * HEAD_WIDTH)
            queries = head_stack(query_ref, start, size, group)
            scores = times_transposed(queries, key_ref[:reach, lanes]) * scale
            scores = jnp.where(allowed, scores, masked_fill)
            peak = jnp.max(scores, axis=-1, keepdims=True)
            expo = jnp.exp(scores - peak)
            total = jnp.sum(expo, axis=-1, keepdims=True)
            probs = (expo * (1.0 / total)).astype(jnp.bfloat16)
            mixed = jnp.dot(probs, value_ref[:reach, lanes], preferred_element_type=jnp.float32)
            outputs += head_unstack(mixed, size)
            totals += head_unstack(peak + jnp.log(total), size)
        mixed_ref[start:reach, :] = jnp.concatenate(outputs, axis=1).astype(jnp.bfloat16)
        total_ref[start:reach, :] = jnp.concatenate(totals, axis=1)


def backward_kernel(
    column_ref,
    row_ref,
    query_ref,
    key_ref,
    value_ref,
    total_ref,
    upstream_ref,
    grad_query_ref,
    grad_key_ref,
    grad_value_ref,
):
    count_of_rows = query_ref.shape[0]
    size = row_tile(count_of_rows)
    scale = HEAD_WIDTH ** (-0.5)
    heads = QUERY_HEADS // KEY_VALUE_HEADS
    for start in reversed(range(0, count_of_rows, size)):
        reach = start + size
        allowed = tile_mask(column_ref, row_ref, start, size)
        query_grads, key_grads, value_grads = [], [], []
        for group in range(KEY_VALUE_HEADS):
            lanes = slice(group * HEAD_WIDTH, (group + 1) * HEAD_WIDTH)
            queries = head_stack(query_ref, start, size, group)
            upstream = head_stack(upstream_ref, start, size, group)
            keys = key_ref[:reach, lanes]
            values = value_ref[:reach, lanes]
            totals = total_ref[start:reach, :]
            total = jnp.concatenate(
                [totals[:, group * heads + j : group * heads + j + 1] for j in range(heads)], axis=0
            )
            scores = times_transposed(queries, keys) * scale
            scores = jnp.where(allowed, scores, masked_fill)
            probs_full = jnp.exp(scores - total)
            value_grads.append(dot_rows(probs_full.astype(jnp.bfloat16), upstream))
            grad_probs = times_transposed(upstream, values)
            row_weight = jnp.sum(probs_full * grad_probs, axis=-1, keepdims=True)
            grad_scores = (probs_full * (grad_probs - row_weight)).astype(jnp.bfloat16)
            grad_queries = jnp.dot(grad_scores, keys, preferred_element_type=jnp.float32) * scale
            query_grads += head_unstack(grad_queries, size)
            key_grads.append(dot_rows(grad_scores, queries) * scale)
        grad_query_ref[start:reach, :] = jnp.concatenate(query_grads, axis=1)
        key_grads = jnp.concatenate(key_grads, axis=1)
        value_grads = jnp.concatenate(value_grads, axis=1)
        if reach == count_of_rows:
            grad_key_ref[...] = key_grads
            grad_value_ref[...] = value_grads
        else:
            grad_key_ref[:reach, :] += key_grads
            grad_value_ref[:reach, :] += value_grads


def row_spec(size, width):
    return pl.BlockSpec((size, width), lambda index: (index, 0))


def call_attention(kernel, segment, arrays, outputs):
    size = segment.shape[0] // MICRO
    return pl.pallas_call(
        kernel,
        grid=(MICRO,),
        in_specs=[row_spec(size, 1), pl.BlockSpec((1, 1, size), lambda index: (index, 0, 0))]
        + [row_spec(size, item.shape[1]) for item in arrays],
        out_specs=[row_spec(size, item.shape[1]) for item in outputs],
        out_shape=outputs,
        compiler_params=pltpu.CompilerParams(vmem_limit_bytes=50 * 2**20),
    )(segment.reshape(-1, 1), segment.reshape(MICRO, 1, size), *arrays)


def attend(query_rows, key_rows, value_rows, segment):
    count_of_rows = query_rows.shape[0]
    return call_attention(
        forward_kernel,
        segment,
        (query_rows, key_rows, value_rows),
        [
            jax.ShapeDtypeStruct(query_rows.shape, jnp.bfloat16),
            jax.ShapeDtypeStruct((count_of_rows, QUERY_HEADS), jnp.float32),
        ],
    )


def attend_back(query_rows, key_rows, value_rows, log_total, mixed_gradient, segment):
    return call_attention(
        backward_kernel,
        segment,
        (query_rows, key_rows, value_rows, log_total, mixed_gradient),
        [
            jax.ShapeDtypeStruct(item.shape, jnp.float32)
            for item in (query_rows, key_rows, value_rows)
        ],
    )


def rotate_flat(rotation, rows, cosine_table, sine_values):
    shaped = rows.reshape(rows.shape[0], -1, HEAD_WIDTH)
    return rotation(shaped, cosine_table, sine_values).reshape(rows.shape).astype(jnp.bfloat16)


def layer_forward(residual, attn_params, fetch_feed, gains, layout):
    allowed, active_rows, cosine_table, sine_values = layout
    w_query, key_weight, value_weight, w_out = attn_params
    normed, factor = norm_forward(residual, gains[0])
    normed = normed.astype(jnp.bfloat16)
    query_rows = jnp.dot(normed, w_query, preferred_element_type=jnp.float32)
    key_rows = jnp.dot(normed, key_weight, preferred_element_type=jnp.float32)
    value_rows = jnp.dot(normed, value_weight, preferred_element_type=jnp.float32).astype(
        jnp.bfloat16
    )
    query_rows = rotate_flat(rotary_apply, query_rows, cosine_table, sine_values)
    key_rows = rotate_flat(rotary_apply, key_rows, cosine_table, sine_values)
    mixed, log_total = attend(query_rows, key_rows, value_rows, allowed)
    hidden_state = (
        residual + jnp.dot(mixed, w_out, preferred_element_type=jnp.float32) * active_rows
    )
    gate_weight, up_weight, down_weight = fetch_feed
    normed_feed, factor_mlp = norm_forward(hidden_state, gains[1])
    normed_feed = normed_feed.astype(jnp.bfloat16)
    gate_branch = jnp.dot(normed_feed, gate_weight, preferred_element_type=jnp.float32)
    up_branch = jnp.dot(normed_feed, up_weight, preferred_element_type=jnp.float32)
    inner_product = (jax.nn.silu(gate_branch) * up_branch).astype(jnp.bfloat16)
    output = (
        hidden_state
        + jnp.dot(inner_product, down_weight, preferred_element_type=jnp.float32) * active_rows
    )
    saved = (
        residual,
        normed,
        factor,
        query_rows,
        key_rows,
        value_rows,
        mixed,
        log_total,
        hidden_state,
        normed_feed,
        factor_mlp,
        gate_branch,
        up_branch,
        inner_product,
    )
    return (output, saved)


def contract_rows(left, right):
    return lax.dot_general(
        left, right, (((0,), (0,)), ((), ())), preferred_element_type=jnp.float32
    ).astype(jnp.bfloat16)


def times_transposed(left, right):
    return lax.dot_general(
        left, right, (((1,), (1,)), ((), ())), preferred_element_type=jnp.float32
    )


def feed_backward(saved, feed_params, gain_row, active_rows, upstream):
    hidden_state, normed_feed, factor_mlp, gate_branch, up_branch, inner_product = saved[8:]
    gate_weight, up_weight, down_weight = feed_params
    sigmoid_gate = jax.nn.sigmoid(gate_branch)
    activated = gate_branch * sigmoid_gate
    grad_branch = (upstream * active_rows).astype(jnp.bfloat16)
    grad_inner = times_transposed(grad_branch, down_weight).astype(jnp.bfloat16)
    grad_gate_in = (
        grad_inner * up_branch * sigmoid_gate * (1.0 + gate_branch * (1.0 - sigmoid_gate))
    ).astype(jnp.bfloat16)
    grad_up_in = (grad_inner * activated).astype(jnp.bfloat16)
    grad_down = contract_rows(inner_product, grad_branch)
    grad_gate = contract_rows(normed_feed, grad_gate_in)
    grad_up = contract_rows(normed_feed, grad_up_in)
    grad_normed = times_transposed(grad_gate_in, gate_weight) + times_transposed(
        grad_up_in, up_weight
    )
    through, grad_gain = norm_backward(hidden_state, factor_mlp, gain_row, grad_normed)
    return (through + upstream, grad_gain, (grad_gate, grad_up, grad_down))


def attention_part_backward(saved, attn_params, gain_row, layout, grad_hidden):
    residual, normed, factor, query_rows, key_rows, value_rows, mixed, log_total = saved[:8]
    w_query, key_weight, value_weight, w_out = attn_params
    allowed, active_rows, cosine_table, sine_values = layout
    grad_attn = (grad_hidden * active_rows).astype(jnp.bfloat16)
    grad_out = contract_rows(mixed, grad_attn)
    mixed_gradient = times_transposed(grad_attn, w_out).astype(jnp.bfloat16)
    grad_queries, key_gradient, value_gradient = attend_back(
        query_rows, key_rows, value_rows, log_total, mixed_gradient, allowed
    )
    value_gradient = value_gradient.astype(jnp.bfloat16)
    grad_queries = rotate_flat(rotary_inverse, grad_queries, cosine_table, sine_values)
    key_gradient = rotate_flat(rotary_inverse, key_gradient, cosine_table, sine_values)
    grad_query = contract_rows(normed, grad_queries)
    grad_key = contract_rows(normed, key_gradient)
    grad_value = contract_rows(normed, value_gradient)
    grad_normed = (
        times_transposed(grad_queries, w_query)
        + times_transposed(key_gradient, key_weight)
        + times_transposed(value_gradient, value_weight)
    )
    through, grad_gain = norm_backward(residual, factor, gain_row, grad_normed)
    return (through + grad_hidden, grad_gain, (grad_query, grad_key, grad_value, grad_out))


def blocks_of(rows):
    size = rows.shape[0] // MICRO
    return [rows[index * size : (index + 1) * size] for index in range(MICRO)]


def sum_shards(buffer, last):
    shard = lax.psum_scatter(buffer, "fsdp", scatter_dimension=0, tiled=False)
    if last:
        return lax.psum(shard, "rep")
    rows, width = shard.shape
    copies = lax.axis_size("rep")
    padded = -(-rows // copies) * copies
    if padded != rows:
        shard = jnp.pad(shard, ((0, padded - rows), (0, 0)))
    part = lax.psum_scatter(shard, "rep", scatter_dimension=0, tiled=True)
    return lax.all_gather(part, "rep", axis=0, tiled=True)


def local(
    tokens,
    segment,
    attn_gain,
    w_query,
    key_weight,
    value_weight,
    w_out,
    mlp_gain,
    gate_weight,
    up_weight,
    down_weight,
    cotangent,
):
    devices = lax.axis_size("fsdp")
    rows, ff = gate_weight.shape[1:]
    width = rows * devices
    kv = key_weight.shape[2]
    down_rows = down_weight.shape[1]
    layouts = [geometry(piece) for piece in blocks_of(segment)]
    layout = (segment,) + tuple(
        jnp.concatenate([item[member] for item in layouts]) for member in range(1, 4)
    )
    active_rows = layout[1]

    all_gains = jnp.concatenate([attn_gain, mlp_gain]).reshape(1, 4 * rows)
    all_gains = jnp.pad(all_gains, ((0, 0), (0, 2 * width + 2 * kv - 4 * rows)))
    attn_weights, feed_weights = [], []
    gains = None
    for layer in range(DECODER_LAYERS):
        packed = jnp.concatenate(
            [w_query[layer], key_weight[layer], value_weight[layer], w_out[layer]], axis=1
        )
        if layer == 0:
            packed = jnp.concatenate([packed, all_gains])
        whole = lax.all_gather(packed, "fsdp", axis=0, tiled=False)
        if layer == 0:
            gains = whole[:, rows, : 4 * rows].reshape(devices, 4, rows)
            gains = gains.transpose(1, 0, 2).reshape(4, width).astype(jnp.float32)
        whole = whole[:, :rows].reshape(width, -1)
        attn_weights.append(
            (
                whole[:, :width],
                whole[:, width : width + kv],
                whole[:, width + kv : width + 2 * kv],
                whole[:, width + 2 * kv :],
            )
        )
        packed = jnp.concatenate(
            [gate_weight[layer], up_weight[layer], down_weight[layer].reshape(rows, ff)]
        )
        whole = lax.all_gather(packed, "fsdp", axis=0, tiled=False)
        feed_weights.append(
            (
                whole[:, :rows].reshape(width, ff),
                whole[:, rows : 2 * rows].reshape(width, ff),
                whole[:, 2 * rows :].reshape(ff, width),
            )
        )

    residual = tokens.astype(jnp.float32)
    saved = []
    for layer in range(DECODER_LAYERS):
        residual, kept = layer_forward(
            residual,
            attn_weights[layer],
            feed_weights[layer],
            (gains[layer], gains[DECODER_LAYERS + layer]),
            layout,
        )
        saved.append(kept)
    out_tokens = residual.astype(jnp.bfloat16)

    upstream = cotangent.astype(jnp.float32)
    shards = [None] * DECODER_LAYERS
    for layer in reversed(range(DECODER_LAYERS)):
        grad_hidden, mlp_gain_grad, feed_grads = feed_backward(
            saved[layer],
            feed_weights[layer],
            gains[DECODER_LAYERS + layer],
            active_rows,
            upstream,
        )
        buffer = jnp.concatenate(
            [
                feed_grads[0].reshape(devices, rows, ff),
                feed_grads[1].reshape(devices, rows, ff),
                feed_grads[2].reshape(devices, rows, ff),
            ],
            axis=1,
        )
        feed_shard = sum_shards(buffer, False)
        upstream, attn_gain_grad, attn_grads = attention_part_backward(
            saved[layer], attn_weights[layer], gains[layer], layout, grad_hidden
        )
        gain_grads = jnp.concatenate(
            [attn_gain_grad.reshape(devices, rows), mlp_gain_grad.reshape(devices, rows)], axis=1
        ).astype(jnp.bfloat16)
        gain_grads = jnp.pad(gain_grads, ((0, 0), (0, 2 * width + 2 * kv - 2 * rows)))
        buffer = jnp.concatenate(
            [
                jnp.concatenate(attn_grads, axis=1).reshape(devices, rows, -1),
                gain_grads[:, None],
            ],
            axis=1,
        )
        attn_shard = sum_shards(buffer, layer == 0)
        feed_shard = feed_shard.astype(jnp.float32)
        attn_shard = attn_shard.astype(jnp.float32)
        block = attn_shard[:rows]
        shards[layer] = (
            attn_shard[rows, :rows],
            block[:, :width],
            block[:, width : width + kv],
            block[:, width + kv : width + 2 * kv],
            block[:, width + 2 * kv :],
            attn_shard[rows, rows : 2 * rows],
            feed_shard[:rows],
            feed_shard[rows : 2 * rows],
            feed_shard[2 * rows : 3 * rows].reshape(down_rows, width),
        )
    stacked = tuple(
        jnp.stack([shards[layer][member] for layer in range(DECODER_LAYERS)])
        for member in range(9)
    )
    return (out_tokens, upstream) + stacked


def solution(mesh):
    in_specs = (
        P(("rep", "fsdp"), None),
        P(("rep", "fsdp")),
        P(None, "fsdp"),
        P(None, "fsdp", None),
        P(None, "fsdp", None),
        P(None, "fsdp", None),
        P(None, "fsdp", None),
        P(None, "fsdp"),
        P(None, "fsdp", None),
        P(None, "fsdp", None),
        P(None, "fsdp", None),
        P(("rep", "fsdp"), None),
    )
    out_specs = (
        P(("rep", "fsdp"), None),
        P(("rep", "fsdp"), None),
        P(None, "fsdp"),
        P(None, "fsdp", None),
        P(None, "fsdp", None),
        P(None, "fsdp", None),
        P(None, "fsdp", None),
        P(None, "fsdp"),
        P(None, "fsdp", None),
        P(None, "fsdp", None),
        P(None, "fsdp", None),
    )
    return jax.shard_map(local, mesh=mesh, in_specs=in_specs, out_specs=out_specs, check_vma=False)
```

profile of v0, /device:TPU:0, one launch (start us, length us, event | category | flops | bytes accessed | tf_op | source)
XLA Modules:
  0.0 701.8 jit_solution(5025352950604371224)
XLA Ops:
  22.1 20.2 %all-gather.19.cloned.1.call-done = bf16[8,73,1536]{2,1,0:T(8,128)(2,1)} async-done(((bf16[1,73,1536]{2,1,0:T(8,128)(2,1)}), bf16[8,73,1536]{2,1,0:T(8,128)(2,1)}) %all-gather.19.cloned.1.call-update) | async-done | bytes 1794064 | tf_op jit(solution)/shard_map/all_gather | solution.py:384
  59.5 24.6 %shard_map.203 = (bf16[1536,576]{1,0:T(8,128)(2,1)}, f32[1536,9]{1,0:T(8,128)S(1)}) custom-call(s32[1536,1]{1,0:T(8,128)S(1)} %reshape.454.column_ref, s32[2,1,768]{2,1,0:T(1,128)S(1)} %reshape.403.row_ref, bf16[1536,576]{1,0:T(8,128)(2,1)} %copy.125.query_ref, bf16[1536,192]{1,0:T(8,128)(2,1)S(1)} %copy.126.key_ref, ...), custom_call_target="tpu_custom_call" | custom-call | tf_op jit(solution)/shard_map/pallas_call | solution.py:187
  84.2 5.8 multiply_reduce_fusion.8
  109.4 6.0 fusion.82
  115.5 7.6 %multiply_convert_fusion.1 = (bf16[1536,1536]{1,0:T(8,128)(2,1)S(1)}, f32[1536,1536]{1,0:T(8,128)}) fusion(f32[1536,1536]{1,0:T(8,128)S(1)} %fusion.82, bf16[1536,576]{0,1:T(8,128)(2,1)S(1)} %copy-done.37, bf16[576,1536]{1,0:T(8,128)(2,1)S(1)} %bitcast.185), kind=kOutput, calls=%fused_computation.15 | convolution fusion | flops 2732064768 | bytes 27131904 | tf_op jit(solution)/shard_map/dot_general | solution.py:248
  143.9 24.2 %shard_map.204 = (bf16[1536,576]{1,0:T(8,128)(2,1)}, f32[1536,9]{1,0:T(8,128)S(1)}) custom-call(s32[1536,1]{1,0:T(8,128)S(1)} %reshape.454.column_ref, s32[2,1,768]{2,1,0:T(1,128)S(1)} %reshape.403.row_ref, bf16[1536,576]{1,0:T(8,128)(2,1)} %copy.129.query_ref, bf16[1536,192]{1,0:T(8,128)(2,1)S(1)} %copy.130.key_ref, ...), custom_call_target="tpu_custom_call" | custom-call | tf_op jit(solution)/shard_map/pallas_call | solution.py:187
  168.1 5.7 multiply_reduce_fusion.6
  174.4 11.3 %all-gather.17.cloned.1.call-done = bf16[1728,1536]{1,0:T(8,128)(2,1)} async-done(((bf16[216,1536]{1,0:T(8,128)(2,1)}), bf16[1728,1536]{1,0:T(8,128)(2,1)}) %all-gather.17.cloned.1.call-update) | async-done | bytes 5308432 | tf_op jit(solution)/shard_map/all_gather | solution.py:400
  190.8 5.4 reshape.416
  198.8 6.4 fusion.83
  205.2 5.7 convolution_convert_fusion.1
  210.9 13.1 %fusion.4 = (bf16[1536,1536]{1,0:T(8,128)(2,1)}, bf16[1536,1536]{1,0:T(8,128)(2,1)}, bf16[1536,1536]{1,0:T(8,128)(2,1)S(1)}) fusion(bf16[1536,1536]{1,0:T(8,128)(2,1)} %convolution_convert_fusion.1, f32[1536,1536]{1,0:T(8,128)} %fusion.83, bf16[1536,576]{0,1:T(8,128)(2,1)S(1)} %multiply_convert_fusion.5, bf16[576,1536]{1,0:T(8,128)(2,1)S(1)} %bitcast.191), kind=kOutput, calls=%fused_computation.6 | convolution fusion | flops 2755657728 | bytes 31850496 | tf_op jit(solution)/shard_map/dot_general | solution.py:248
  224.0 6.6 fusion.84
  246.8 33.3 %shard_map.205 = (f32[1536,576]{1,0:T(8,128)}, f32[1536,192]{1,0:T(8,128)}, f32[1536,192]{1,0:T(8,128)}) custom-call(s32[1536,1]{1,0:T(8,128)S(1)} %reshape.454.column_ref, s32[2,1,768]{2,1,0:T(1,128)S(1)} %reshape.403.row_ref, bf16[1536,576]{1,0:T(8,128)(2,1)} %copy.129.query_ref, bf16[1536,192]{1,0:T(8,128)(2,1)S(1)} %copy.130.key_ref, ...), custom_call_target="tpu_custom_call" | custom-call | tf_op jit(solution)/shard_map/pallas_call | solution.py:187
  303.6 14.9 %fusion.9 = (bf16[1536,1536]{1,0:T(8,128)(2,1)}, bf16[1536,1536]{1,0:T(8,128)(2,1)}) fusion(f32[1536,1536]{1,0:T(8,128)} %copy-done.89, f32[1536,1536]{1,0:T(8,128)} %get-tuple-element.131, bf16[1536,576]{1,0:T(8,128)(2,1)S(1)} %copy-done.35, f32[1536,576]{0,1:T(8,128)S(1)} %subtract_add_fusion.1, f32[1536]{0:T(1024)S(1)} %copy-done.79), kind=kOutput, calls=%fused_computation.11 | convolution fusion | flops 2755067904 | bytes 33626112 | tf_op jit(solution)/shard_map/dot_general | solution.py:280
  318.5 5.5 fusion.85
  339.8 33.3 %shard_map.206 = (f32[1536,576]{1,0:T(8,128)}, f32[1536,192]{1,0:T(8,128)}, f32[1536,192]{1,0:T(8,128)}) custom-call(s32[1536,1]{1,0:T(8,128)S(1)} %reshape.454.column_ref, s32[2,1,768]{2,1,0:T(1,128)S(1)} %reshape.403.row_ref, bf16[1536,576]{1,0:T(8,128)(2,1)} %copy.125.query_ref, bf16[1536,192]{1,0:T(8,128)(2,1)S(1)} %copy.126.key_ref, ...), custom_call_target="tpu_custom_call" | custom-call | tf_op jit(solution)/shard_map/pallas_call | solution.py:187
  388.8 5.4 copy.141
  419.2 6.4 convolution_convert_fusion.3
  432.0 7.2 %convolution_convert_fusion.9 = bf16[576,1536]{1,0:T(8,128)(2,1)} fusion(bf16[1536,576]{0,1:T(8,128)(2,1)} %multiply_convert_fusion.7, bf16[1536,1536]{1,0:T(8,128)(2,1)} %get-tuple-element.52), kind=kOutput, calls=%fused_computation.71 | convolution fusion | flops 2718793728 | bytes 8257536 | tf_op jit(solution)/shard_map/dot_general | solution.py:274
  439.2 6.4 convolution_convert_fusion.8
  447.3 10.3 %reduce-scatter.9.cloned.1.call-done = bf16[1,73,1536]{2,1,0:T(8,128)(2,1)} async-done(((bf16[8,73,1536]{2,1,0:T(8,128)(2,1)}), bf16[1,73,1536]{2,1,0:T(8,128)(2,1)}) %reduce-scatter.9.cloned.1.call-update) | async-done | bytes 224272 | tf_op jit(solution)/shard_map/reduce_scatter | solution.py:337
  462.8 5.9 convolution_convert_fusion.2
  475.5 5.9 convolution_convert_fusion.7
  492.1 6.1 fusion.18
  498.3 6.7 add_convert_fusion
  505.8 9.3 %all-gather.5 = bf16[4,19,1536]{2,1,0:T(8,128)(2,1)S(1)} all-gather(bf16[1,19,1536]{2,1,0:T(8,128)(2,1)S(1)} %dynamic-slice_bitcast_fusion.2), channel_id=1, replica_groups=mesh['rep'=4,'fsdp'=8] {'rep'}, dimensions={0}, use_global_device_ids=true | all-gather | bytes 291840 | tf_op jit(solution)/shard_map/all_gather | solution.py:346
  521.0 46.8 %reduce-scatter.13.cloned.1.call-done = bf16[1,216,1536]{2,1,0:T(8,128)(2,1)} async-done(((bf16[8,216,1536]{2,1,0:T(8,128)(2,1)}), bf16[1,216,1536]{2,1,0:T(8,128)(2,1)}) %reduce-scatter.13.cloned.1.call-update) | async-done | bytes 663568 | tf_op jit(solution)/shard_map/reduce_scatter | solution.py:337
  567.7 61.4 %reduce-scatter.15.cloned.1.call-done = bf16[1,216,1536]{2,1,0:T(8,128)(2,1)} async-done(((bf16[8,216,1536]{2,1,0:T(8,128)(2,1)}), bf16[1,216,1536]{2,1,0:T(8,128)(2,1)}) %reduce-scatter.15.cloned.1.call-update) | async-done | bytes 663568 | tf_op jit(solution)/shard_map/reduce_scatter | solution.py:337
  629.1 29.4 %fusion.72 = (bf16[64,1536]{1,0:T(8,128)(2,1)S(1)}, bf16[64,1536]{1,0:T(8,128)(2,1)S(1)}) fusion(bf16[216,1536]{1,0:T(8,128)(2,1)} %bitcast.199, bf16[216,1536]{1,0:T(8,128)(2,1)} %bitcast.198), kind=kCustom, calls=%all-reduce-scatter.2 | all-reduce-scatter fusion | flops 786433 | bytes 1720832
  666.5 11.0 %all-gather.6 = bf16[4,54,1536]{2,1,0:T(8,128)(2,1)S(1)} all-gather(bf16[1,54,1536]{2,1,0:T(8,128)(2,1)S(1)} %dynamic-slice_bitcast_fusion.1), channel_id=1, replica_groups=mesh['rep'=4,'fsdp'=8] {'rep'}, dimensions={0}, use_global_device_ids=true | all-gather | bytes 829440 | tf_op jit(solution)/shard_map/all_gather | solution.py:346
  678.9 9.5 %all-gather.7 = bf16[4,54,1536]{2,1,0:T(8,128)(2,1)S(1)} all-gather(bf16[1,54,1536]{2,1,0:T(8,128)(2,1)S(1)} %dynamic-slice_bitcast_fusion), channel_id=1, replica_groups=mesh['rep'=4,'fsdp'=8] {'rep'}, dimensions={0}, use_global_device_ids=true | all-gather | bytes 829440 | tf_op jit(solution)/shard_map/all_gather | solution.py:346
  (366 shorter events, 227.8 us)
Async XLA Ops:
  7.2 35.1 %all-gather.19.cloned.1.call-start = ((), (), s32[]{:S(2)}) async-start(), calls=%async_computation.11 | async-start | bytes 2211840 | tf_op jit(solution)/shard_map/all_gather | solution.py:384
  11.5 89.2 %all-gather.13.cloned.1.call-start = ((), (), s32[]{:S(2)}) async-start(), calls=%async_computation.8 | async-start | bytes 5971968 | tf_op jit(solution)/shard_map/all_gather | solution.py:400
  15.2 114.2 %all-gather.15.cloned.1.call-start = ((), (), s32[]{:S(2)}) async-start(), calls=%async_computation.9 | async-start | bytes 1990656 | tf_op jit(solution)/shard_map/all_gather | solution.py:384
  17.0 168.8 %all-gather.17.cloned.1.call-start = ((), (), s32[]{:S(2)}) async-start(), calls=%async_computation.10 | async-start | bytes 5971968 | tf_op jit(solution)/shard_map/all_gather | solution.py:400
  18.3 427.3 %reduce-scatter.11.cloned.1.call-start = ((), (), s32[]{:S(2)}) async-start(), calls=%async_computation.5 | async-start | bytes 2211840 | tf_op jit(solution)/shard_map/reduce_scatter | solution.py:337
  19.7 30.0 %copy-start.62 = (f32[1536]{0:T(1024)}, f32[1536]{0:T(1024)S(1)}, u32[]{:S(2)}) copy-start(f32[1536]{0:T(1024)S(1)} %get-tuple-element.109) | copy-start | bytes 18436
  22.1 29.2 %copy-start.13 = (f32[1536,32]{0,1:T(8,128)}, f32[1536,32]{0,1:T(8,128)S(1)}, u32[]{:S(2)}) copy-start(f32[1536,32]{0,1:T(8,128)S(1)} %maximum_bitcast_fusion.1) | copy-start | bytes 589828
  22.1 101.5 %copy-start.76 = (f32[1536]{0:T(1024)}, f32[1536]{0:T(1024)S(1)}, u32[]{:S(2)}) copy-start(f32[1536]{0:T(1024)S(1)} %maximum_reduce_fusion) | copy-start | bytes 18436
  50.8 8.7 %copy-start = (bf16[1536,192]{1,0:T(8,128)(2,1)}, bf16[1536,192]{1,0:T(8,128)(2,1)S(1)}, u32[]{:S(2)}) copy-start(bf16[1536,192]{1,0:T(8,128)(2,1)S(1)} %convolution_convert_fusion.11.value_ref) | copy-start | bytes 1769476
  59.5 24.6 %copy-start.18 = (bf16[1536,576]{0,1:T(8,128)(2,1)S(1)}, bf16[1536,576]{0,1:T(8,128)(2,1)}, u32[]{:S(2)}) copy-start(bf16[1536,576]{0,1:T(8,128)(2,1)} %param.12) | copy-start | bytes 5308420
  90.0 10.7 %copy-start.70 = (f32[576]{0:T(1024)}, f32[576]{0:T(1024)S(1)}, u32[]{:S(2)}) copy-start(f32[576]{0:T(1024)S(1)} %mul.691) | copy-start | bytes 6916
  91.9 8.8 %copy-start.59 = (f32[1536]{0:T(1024)}, f32[1536]{0:T(1024)S(1)}, u32[]{:S(2)}) copy-start(f32[1536]{0:T(1024)S(1)} %get-tuple-element.111) | copy-start | bytes 18436
  115.4 8.2 %copy-start.89 = (f32[1536,1536]{1,0:T(8,128)}, f32[1536,1536]{1,0:T(8,128)S(1)}, u32[]{:S(2)}) copy-start(f32[1536,1536]{1,0:T(8,128)S(1)} %fusion.82) | copy-start | bytes 28311556
  115.5 8.2 %copy-start.23 = (f32[1536,576]{0,1:T(8,128)S(1)}, f32[1536,576]{0,1:T(8,128)}, u32[]{:S(2)}) copy-start(f32[1536,576]{0,1:T(8,128)} %get-tuple-element.129) | copy-start | bytes 10616836
  115.5 8.2 %copy-start.34 = (bf16[1536,576]{1,0:T(8,128)(2,1)S(1)}, bf16[1536,576]{1,0:T(8,128)(2,1)}, u32[]{:S(2)}) copy-start(bf16[1536,576]{1,0:T(8,128)(2,1)} %reshape.410) | copy-start | bytes 5308420
  141.4 26.7 %copy-start.7 = (f32[1536,576]{0,1:T(8,128)S(1)}, f32[1536,576]{0,1:T(8,128)}, u32[]{:S(2)}) copy-start(f32[1536,576]{0,1:T(8,128)} %copy-done.6) | copy-start | bytes 10616836
  141.4 26.7 %copy-start.77 = (f32[1536]{0:T(1024)S(1)}, f32[1536]{0:T(1024)}, u32[]{:S(2)}) copy-start(f32[1536]{0:T(1024)} %copy-done.76) | copy-start | bytes 18436
  198.7 12.2 %copy-start.39 = (bf16[1536,576]{0,1:T(8,128)(2,1)}, bf16[1536,576]{0,1:T(8,128)(2,1)S(1)}, u32[]{:S(2)}) copy-start(bf16[1536,576]{0,1:T(8,128)(2,1)S(1)} %multiply_convert_fusion.5) | copy-start | bytes 5308420
  224.0 6.6 copy-start.87
  224.0 6.6 copy-start.9
  224.0 6.6 copy-start.61
  224.0 6.6 copy-start.69
  302.9 25.5 %copy-start.20 = (f32[1536,576]{0,1:T(8,128)}, f32[1536,576]{0,1:T(8,128)S(1)}, u32[]{:S(2)}) copy-start(f32[1536,576]{0,1:T(8,128)S(1)} %subtract_add_fusion.1) | copy-start | bytes 10616836
  386.9 70.7 %reduce-scatter.9.cloned.1.call-start = ((), (), s32[]{:S(2)}) async-start(), calls=%async_computation.4 | async-start | bytes 2211840 | tf_op jit(solution)/shard_map/reduce_scatter | solution.py:337
  387.0 7.2 %copy-start.29 = (bf16[1536,3,64]{0,2,1:T(8,128)(2,1)}, bf16[1536,3,64]{0,2,1:T(8,128)(2,1)S(1)}, u32[]{:S(2)}) copy-start(bf16[1536,3,64]{0,2,1:T(8,128)(2,1)S(1)} %pad_maximum_fusion.16) | copy-start | bytes 1769476
  419.1 85.8 %all-reduce.13.cloned.1.call-start = ((), (), s32[]{:S(2)}) async-start(), calls=%async_computation.12 | async-start | bytes 983040
  432.0 7.2 %copy-start.38 = (bf16[1536,576]{0,1:T(8,128)(2,1)S(1)}, bf16[1536,576]{0,1:T(8,128)(2,1)}, u32[]{:S(2)}) copy-start(bf16[1536,576]{0,1:T(8,128)(2,1)} %multiply_convert_fusion.7) | copy-start | bytes 5308420
  457.6 110.1 %reduce-scatter.13.cloned.1.call-start = ((), (), s32[]{:S(2)}) async-start(), calls=%async_computation.6 | async-start | bytes 5971968 | tf_op jit(solution)/shard_map/reduce_scatter | solution.py:337
  462.7 166.4 %reduce-scatter.15.cloned.1.call-start = ((), (), s32[]{:S(2)}) async-start(), calls=%async_computation.7 | async-start | bytes 5971968 | tf_op jit(solution)/shard_map/reduce_scatter | solution.py:337
  658.5 8.0 %copy-start.49 = (bf16[64,1536]{1,0:T(8,128)(2,1)}, bf16[64,1536]{1,0:T(8,128)(2,1)S(1)}, u32[]{:S(2)}) copy-start(bf16[64,1536]{1,0:T(8,128)(2,1)S(1)} %get-tuple-element.47) | copy-start | bytes 589828
  658.5 7.6 %collective-permute-start = (bf16[30,1536]{1,0:T(8,128)(2,1)S(1)}, bf16[30,1536]{1,0:T(8,128)(2,1)S(1)}, u32[]{:S(2)}, u32[]{:S(2)}) collective-permute-start(bf16[30,1536]{1,0:T(8,128)(2,1)S(1)} %slice.352), channel_id=1, source_target_pairs={{0,8},{8,16},{16,24},{1,9},{9,17},{17,25},{2,10},{10,18},{18,26},{... | collective-permute-start | bytes 276488
  662.9 15.2 %collective-permute-start.1 = (bf16[30,1536]{1,0:T(8,128)(2,1)}, bf16[30,1536]{1,0:T(8,128)(2,1)S(1)}, u32[]{:S(2)}, u32[]{:S(2)}) collective-permute-start(bf16[30,1536]{1,0:T(8,128)(2,1)} %slice.353), channel_id=1, source_target_pairs={{0,8},{8,16},{16,24},{1,9},{9,17},{17,25},{2,10},{10,18},{18,26},{... | collective-permute-start | bytes 276488
  (70 other events, 259.4 us)
Sparse Core Ops, SparseCore 0:
  11.6 30.7 all-gather.18
  44.5 56.0 all-gather.12
  102.9 25.1 all-gather.14
  129.6 56.1 all-gather.16
  387.0 34.2 reduce-scatter.10
  423.6 33.9 reduce-scatter.8
  461.2 43.5 all-reduce.12
  507.2 60.5 reduce-scatter.12
  570.2 58.8 reduce-scatter.14
where the time goes:
time: 711 us; the launch traced here: 702 us
  matrix products  184 us (26%)
  waiting for transfers between devices  155 us (22%)
  Pallas kernels  115 us (16%)
  local copies, waits for them, and re-layouts  101 us (14%)
  other arithmetic  63 us (9%)
  blocking collectives  59.2 us (8%)
  between operations  16.9 us (2%)
    reduce_scatter x4, waiting for transfers between devices, sum_shards(): shard = lax.psum_scatter(buffer, 'fsdp', scatter_dimension=0, tiled=False)  118 us
    pallas_call x4, Pallas kernels, call_attention(): pl.pallas_call(kernel, grid=(MICRO,), in_specs=[row_spec(size, 1), pl.Blo...  115 us
    dot_general x14, matrix products, times_transposed(): lax.dot_general(left, right, (((1,), (1,)), ((), ())), preferred_element_...  58.4 us
    dot_general x14, matrix products, contract_rows(): lax.dot_general(left, right, (((0,), (0,)), ((), ())), preferred_element_...  57.8 us
    all_gather x4, waiting for transfers between devices, local(): whole = lax.all_gather(packed, 'fsdp', axis=0, tiled=False)  36.7 us
    all_gather x3, blocking collectives, sum_shards(): return lax.all_gather(part, 'rep', axis=0, tiled=True)  29.8 us
    unnamed x1, blocking collectives  29.4 us
    dot_general x2, matrix products, layer_forward(): jnp.dot(normed_feed, up_weight, preferred_element_type=jnp.float32)  20.7 us
  transfers between devices with their start and end apart: 11, of which 6 were waited for; matrix products, arithmetic and copies ran while one was open for 28% of the time, Pallas kernels for 7%

commit v1 on v0

v1 whole, which is shorter than its diff:
```python
import functools

import jax
import jax.numpy as jnp
from jax import lax
from jax.experimental import pallas as pl
from jax.experimental.pallas import tpu as pltpu
from jax.sharding import PartitionSpec as P

QUERY_HEADS = 9
KEY_VALUE_HEADS = 3
HEAD_WIDTH = 64
DECODER_LAYERS = 2
MICRO = 2
GROUP = QUERY_HEADS // KEY_VALUE_HEADS
Q_WIDTH = QUERY_HEADS * HEAD_WIDTH
KV_WIDTH = KEY_VALUE_HEADS * HEAD_WIDTH
QK_WIDTH = Q_WIDTH + KV_WIDTH
LSE_ROWS = 16
SCALE = HEAD_WIDTH ** (-0.5)

epsilon = 1e-05
rope_base = 100000.0
masked_fill = -1e30
f32 = jnp.float32
bf16 = jnp.bfloat16


def nn(left, right):
    return jnp.dot(left, right, preferred_element_type=f32)


def nt(left, right):
    return lax.dot_general(left, right, (((1,), (1,)), ((), ())), preferred_element_type=f32)


def tn(left, right):
    return lax.dot_general(left, right, (((0,), (0,)), ((), ())), preferred_element_type=f32)


def geometry(segment):
    size = segment.shape[0] // MICRO
    seg = segment.reshape(MICRO, size)
    index = jnp.arange(size, dtype=jnp.int32)
    same = seg[:, :, None] == seg[:, None, :]
    earlier = index[None, :] < index[:, None]
    position = jnp.sum(jnp.where(same & earlier, 1, 0).astype(jnp.int32), axis=-1)
    frequency = rope_base ** (-2.0 * jnp.arange(HEAD_WIDTH // 2, dtype=f32) / HEAD_WIDTH)
    angles = position.reshape(-1).astype(f32)[:, None] * frequency
    cosine, sine = jnp.cos(angles), jnp.sin(angles)
    table = jnp.concatenate([cosine] * 4 + [-sine, sine] * 2, axis=1)
    live = jnp.where(segment >= 0, 1.0, 0.0).astype(f32)[:, None]
    return live, table


def swap_halves(rows):
    lane = lax.broadcasted_iota(jnp.int32, rows.shape, 1)
    first = (lane % HEAD_WIDTH) < HEAD_WIDTH // 2
    return jnp.where(
        first, pltpu.roll(rows, 128 - HEAD_WIDTH // 2, 1), pltpu.roll(rows, HEAD_WIDTH // 2, 1)
    )


def rotate(rows, cosine, sine):
    parts = []
    for first in range(0, rows.shape[1], 128):
        slab = rows[:, first : first + 128]
        parts.append(slab * cosine + swap_halves(slab) * sine)
    return jnp.concatenate(parts, axis=1)


def tile_of(rows):
    return 256 if rows % 256 == 0 else rows


def heads_stacked(ref, start, size, group):
    first = group * GROUP * HEAD_WIDTH
    piece = ref[start : start + size, first : first + GROUP * HEAD_WIDTH]
    return jnp.concatenate(
        [piece[:, j * HEAD_WIDTH : (j + 1) * HEAD_WIDTH] for j in range(GROUP)], axis=0
    )


def heads_split(stacked, size):
    turned = stacked.T
    return [turned[j * size : (j + 1) * size] for j in range(GROUP)]


def mask_bias(column_ref, row_ref, start, size):
    reach = start + size
    shape = (reach, size)
    key = lax.broadcasted_iota(jnp.int32, shape, 0)
    query = lax.broadcasted_iota(jnp.int32, shape, 1) + start
    same = column_ref[:reach, :] == row_ref[0, :, start:reach]
    bias = jnp.where(same & (key <= query), 0.0, masked_fill)
    return jnp.concatenate([bias] * GROUP, axis=1)


def norm(rows):
    return lax.rsqrt(jnp.mean(rows * rows, axis=-1, keepdims=True) + epsilon)


def row_line(ref, start, size, group):
    return jnp.concatenate(
        [ref[group * GROUP + j : group * GROUP + j + 1, start : start + size] for j in range(GROUP)],
        axis=1,
    )


def attn_forward_kernel(
    x_ref, column_ref, row_ref, live_ref, table_ref, gain_ref, weight_ref,
    h_ref, qk_ref, v_ref, a_ref, lse_ref,
):
    rows = x_ref.shape[0]
    x = x_ref[...].astype(f32)
    normed = (x * norm(x) * gain_ref[...]).astype(bf16)
    qk = nn(normed, weight_ref[:, :QK_WIDTH])
    v_ref[...] = nn(normed, weight_ref[:, QK_WIDTH + Q_WIDTH :]).astype(bf16)
    qk = rotate(qk, table_ref[:, :128], table_ref[:, 128:]).astype(bf16)
    qk_ref[:, :Q_WIDTH] = qk[:, :Q_WIDTH] * SCALE
    qk_ref[:, Q_WIDTH:] = qk[:, Q_WIDTH:]
    size = tile_of(rows)
    for start in range(0, rows, size):
        reach = start + size
        bias = mask_bias(column_ref, row_ref, start, size)
        outputs = []
        for group in range(KEY_VALUE_HEADS):
            lanes = slice(group * HEAD_WIDTH, (group + 1) * HEAD_WIDTH)
            klanes = slice(Q_WIDTH + group * HEAD_WIDTH, Q_WIDTH + (group + 1) * HEAD_WIDTH)
            queries = heads_stacked(qk_ref, start, size, group)
            scores = nt(qk_ref[:reach, klanes], queries) + bias
            peak = jnp.max(scores, axis=0, keepdims=True)
            expo = jnp.exp(scores - peak)
            total = jnp.sum(expo, axis=0, keepdims=True)
            mixed = tn(v_ref[:reach, lanes], expo.astype(bf16)) * (1.0 / total)
            outputs += heads_split(mixed, size)
            line = peak + jnp.log(total)
            for j in range(GROUP):
                lse_ref[group * GROUP + j : group * GROUP + j + 1, start:reach] = line[
                    :, j * size : (j + 1) * size
                ]
        a_ref[start:reach, :] = jnp.concatenate(outputs, axis=1).astype(bf16)
    out = nn(a_ref[...], weight_ref[:, QK_WIDTH : QK_WIDTH + Q_WIDTH])
    h_ref[...] = x_ref[...].astype(f32) + out * live_ref[...]


def attn_backward_kernel(
    x_ref, dh_ref, column_ref, row_ref, live_ref, table_ref, gain_ref, weight_ref,
    qk_ref, v_ref, a_ref, lse_ref,
    dx_ref, grad_ref, gain_grad_ref,
    n1t_ref, at_ref, c_ref, dqk_ref, dv_ref, da_ref, weight_line_ref, dqk_sum, dv_sum,
):
    step = pl.program_id(0)
    rows = x_ref.shape[0]
    here = pl.ds(pl.multiple_of(step * rows, rows), rows)
    c = (dh_ref[...] * live_ref[...]).astype(bf16)
    c_ref[here, :] = c
    da = nt(c, weight_ref[:, QK_WIDTH : QK_WIDTH + Q_WIDTH]).astype(bf16)
    da_ref[...] = da
    a = a_ref[...]
    at_ref[:, here] = a.T
    product = da.astype(f32) * a.astype(f32)
    high = product.astype(bf16)
    low = (product - high.astype(f32)).astype(bf16)
    pick = (
        lax.broadcasted_iota(jnp.int32, (LSE_ROWS, Q_WIDTH), 1) // HEAD_WIDTH
        == lax.broadcasted_iota(jnp.int32, (LSE_ROWS, Q_WIDTH), 0)
    )
    pick = jnp.where(pick, 1.0, 0.0).astype(bf16)
    weight_line_ref[...] = nt(pick, high) + nt(pick, low)
    size = tile_of(rows)
    for start in reversed(range(0, rows, size)):
        reach = start + size
        bias = mask_bias(column_ref, row_ref, start, size)
        query_grads = []
        for group in range(KEY_VALUE_HEADS):
            lanes = slice(group * HEAD_WIDTH, (group + 1) * HEAD_WIDTH)
            klanes = slice(Q_WIDTH + group * HEAD_WIDTH, Q_WIDTH + (group + 1) * HEAD_WIDTH)
            queries = heads_stacked(qk_ref, start, size, group)
            upstream = heads_stacked(da_ref, start, size, group)
            keys = qk_ref[:reach, klanes]
            values = v_ref[:reach, lanes]
            probs = jnp.exp(nt(keys, queries) + bias - row_line(lse_ref, start, size, group))
            value_grad = nn(probs.astype(bf16), upstream)
            grad_probs = nt(values, upstream)
            grad_scores = (
                probs * (grad_probs - row_line(weight_line_ref, start, size, group))
            ).astype(bf16)
            key_grad = nn(grad_scores, queries)
            query_grads += heads_split(tn(keys, grad_scores) * SCALE, size)
            if reach == rows:
                dqk_sum[:, klanes] = key_grad
                dv_sum[:, lanes] = value_grad
            else:
                dqk_sum[:reach, klanes] += key_grad
                dv_sum[:reach, lanes] += value_grad
        dqk_sum[start:reach, :Q_WIDTH] = jnp.concatenate(query_grads, axis=1)
    dqk = rotate(dqk_sum[...], table_ref[:, :128], -table_ref[:, 128:]).astype(bf16)
    dqk_ref[here, :] = dqk
    dv = dv_sum[...].astype(bf16)
    dv_ref[here, :] = dv
    dn = nt(dqk, weight_ref[:, :QK_WIDTH]) + nt(dv, weight_ref[:, QK_WIDTH + Q_WIDTH :])
    x = x_ref[...].astype(f32)
    factor = norm(x)
    unit = x * factor
    gain = gain_ref[...]
    n1t_ref[:, here] = (unit * gain).astype(bf16).T
    scaled = dn * gain
    dx_ref[...] = dh_ref[...] + factor * (
        scaled - unit * jnp.mean(scaled * unit, axis=-1, keepdims=True)
    )
    gain_part = jnp.sum(dn * unit, axis=0, keepdims=True)

    @pl.when(step == 0)
    def _():
        gain_grad_ref[...] = gain_part

    @pl.when(step > 0)
    def _():
        gain_grad_ref[...] += gain_part

    @pl.when(step == pl.num_programs(0) - 1)
    def _():
        grad_ref[:, :QK_WIDTH] = nn(n1t_ref[...], dqk_ref[...]).astype(bf16)
        grad_ref[:, QK_WIDTH : QK_WIDTH + Q_WIDTH] = nn(at_ref[...], c_ref[...]).astype(bf16)
        grad_ref[:, QK_WIDTH + Q_WIDTH :] = nn(n1t_ref[...], dv_ref[...]).astype(bf16)


def ff_forward_kernel(h_ref, live_ref, gain_ref, wg_ref, wu_ref, wd_ref, y_ref):
    h = h_ref[...]
    normed = (h * norm(h) * gain_ref[...]).astype(bf16)
    gate = nn(normed, wg_ref[...])
    up = nn(normed, wu_ref[...])
    half = 0.5 * gate
    inner = ((half + half * jnp.tanh(half)) * up).astype(bf16)
    y_ref[...] = h + nn(inner, wd_ref[...]) * live_ref[...]


def ff_backward_kernel(
    last, h_ref, dy_ref, live_ref, gain_ref, wg_ref, wu_ref, wd_ref, *rest,
):
    if last:
        y_ref, *rest = rest
    (dh_ref, gg_ref, gu_ref, gd_ref, gain_grad_ref, n2t_ref, et_ref, m_ref, dg_ref, du_ref) = rest
    step = pl.program_id(0)
    rows = h_ref.shape[0]
    here = pl.ds(pl.multiple_of(step * rows, rows), rows)
    h = h_ref[...]
    factor = norm(h)
    unit = h * factor
    gain = gain_ref[...]
    normed = (unit * gain).astype(bf16)
    n2t_ref[:, here] = normed.T
    live = live_ref[...]
    dy = dy_ref[...].astype(f32)
    e = (dy * live).astype(bf16)
    et_ref[:, here] = e.T
    gate = nn(normed, wg_ref[...])
    up = nn(normed, wu_ref[...])
    sig = 0.5 + 0.5 * jnp.tanh(0.5 * gate)
    silu = gate * sig
    inner = (silu * up).astype(bf16)
    m_ref[here, :] = inner
    dm = nt(e, wd_ref[...]).astype(bf16).astype(f32)
    dgate = (dm * up * (sig + silu * (1.0 - sig))).astype(bf16)
    dup = (dm * silu).astype(bf16)
    dg_ref[here, :] = dgate
    du_ref[here, :] = dup
    if last:
        y_ref[...] = (h + nn(inner, wd_ref[...]) * live).astype(bf16)
    dn = nt(dgate, wg_ref[...]) + nt(dup, wu_ref[...])
    scaled = dn * gain
    dh_ref[...] = dy + factor * (scaled - unit * jnp.mean(scaled * unit, axis=-1, keepdims=True))
    gain_part = jnp.sum(dn * unit, axis=0, keepdims=True)

    @pl.when(step == 0)
    def _():
        gain_grad_ref[...] = gain_part

    @pl.when(step > 0)
    def _():
        gain_grad_ref[...] += gain_part

    @pl.when(step == pl.num_programs(0) - 1)
    def _():
        ff = m_ref.shape[1]
        for first in range(0, ff, 512):
            cols = slice(first, first + 512)
            gg_ref[:, cols] = nn(n2t_ref[...], dg_ref[:, cols]).astype(bf16)
            gu_ref[:, cols] = nn(n2t_ref[...], du_ref[:, cols]).astype(bf16)
            gd_ref[cols, :] = nn(et_ref[...], m_ref[:, cols]).astype(bf16).T


def row_spec(size, width):
    return pl.BlockSpec((size, width), lambda i: (i, 0))


def whole_spec(shape):
    return pl.BlockSpec(shape, lambda i: (0,) * len(shape), pipeline_mode=pl.Buffered(1))


def still_spec(shape):
    return pl.BlockSpec(shape, lambda i: (0,) * len(shape))


def shape(dims, dtype):
    return jax.ShapeDtypeStruct(dims, dtype)


def params(mib=60):
    return pltpu.CompilerParams(vmem_limit_bytes=mib * 2**20, dimension_semantics=("arbitrary",))


def cost(flops, *arrays):
    return pl.CostEstimate(
        flops=int(flops),
        bytes_accessed=sum(int(a.size) * a.dtype.itemsize for a in arrays),
        transcendentals=0,
    )


def attn_forward(x, segment, live, table, gain, weight):
    total, width = x.shape
    size = total // MICRO
    outs = [
        shape((total, width), f32),
        shape((total, QK_WIDTH), bf16),
        shape((total, KV_WIDTH), bf16),
        shape((total, Q_WIDTH), bf16),
        shape((LSE_ROWS, total), f32),
    ]
    return pl.pallas_call(
        attn_forward_kernel,
        grid=(MICRO,),
        in_specs=[
            row_spec(size, width),
            row_spec(size, 1),
            pl.BlockSpec((1, 1, size), lambda i: (i, 0, 0)),
            row_spec(size, 1),
            row_spec(size, 256),
            whole_spec(gain.shape),
            whole_spec(weight.shape),
        ],
        out_specs=[row_spec(size, o.shape[1]) for o in outs[:4]]
        + [pl.BlockSpec((LSE_ROWS, size), lambda i: (0, i))],
        out_shape=outs,
        compiler_params=params(),
        cost_estimate=cost(2 * total * (width * 1536 + size * Q_WIDTH * 4), x, weight, *outs),
        name="attn_fwd",
    )(x, segment.reshape(-1, 1), segment.reshape(MICRO, 1, size), live, table, gain, weight)


def attn_backward(x, dh, segment, live, table, gain, weight, saved):
    total, width = x.shape
    size = total // MICRO
    qk, v, a, lse = saved
    outs = [shape((total, width), f32), shape(weight.shape, bf16), shape((1, width), f32)]
    return pl.pallas_call(
        attn_backward_kernel,
        grid=(MICRO,),
        in_specs=[
            row_spec(size, width),
            row_spec(size, width),
            row_spec(size, 1),
            pl.BlockSpec((1, 1, size), lambda i: (i, 0, 0)),
            row_spec(size, 1),
            row_spec(size, 256),
            whole_spec(gain.shape),
            whole_spec(weight.shape),
            row_spec(size, QK_WIDTH),
            row_spec(size, KV_WIDTH),
            row_spec(size, Q_WIDTH),
            pl.BlockSpec((LSE_ROWS, size), lambda i: (0, i)),
        ],
        out_specs=[row_spec(size, width), still_spec(weight.shape), still_spec((1, width))],
        out_shape=outs,
        scratch_shapes=[
            pltpu.VMEM((width, total), bf16),
            pltpu.VMEM((Q_WIDTH, total), bf16),
            pltpu.VMEM((total, width), bf16),
            pltpu.VMEM((total, QK_WIDTH), bf16),
            pltpu.VMEM((total, KV_WIDTH), bf16),
            pltpu.VMEM((size, Q_WIDTH), bf16),
            pltpu.VMEM((LSE_ROWS, size), f32),
            pltpu.VMEM((size, QK_WIDTH), f32),
            pltpu.VMEM((size, KV_WIDTH), f32),
        ],
        compiler_params=params(),
        cost_estimate=cost(2 * total * (width * 3072 + size * Q_WIDTH * 10), x, dh, weight, *outs),
        name="attn_bwd",
    )(
        x, dh, segment.reshape(-1, 1), segment.reshape(MICRO, 1, size), live, table, gain, weight,
        qk, v, a, lse,
    )


def ff_forward(h, live, gain, wg, wu, wd):
    total, width = h.shape
    size = tile_of(total)
    out = shape((total, width), f32)
    return pl.pallas_call(
        ff_forward_kernel,
        grid=(total // size,),
        in_specs=[row_spec(size, width), row_spec(size, 1), whole_spec(gain.shape)]
        + [whole_spec(w.shape) for w in (wg, wu, wd)],
        out_specs=row_spec(size, width),
        out_shape=out,
        compiler_params=params(),
        cost_estimate=cost(6 * total * wg.size, h, wg, wu, wd, out),
        name="ff_fwd",
    )(h, live, gain, wg, wu, wd)


def ff_backward(h, dy, live, gain, wg, wu, wd, last):
    total, width = h.shape
    ff = wg.shape[1]
    size = tile_of(total)
    outs = [
        shape((total, width), f32),
        shape(wg.shape, bf16),
        shape(wu.shape, bf16),
        shape(wd.shape, bf16),
        shape((1, width), f32),
    ]
    specs = [row_spec(size, width)] + [still_spec(o.shape) for o in outs[1:]]
    if last:
        outs = [shape((total, width), bf16)] + outs
        specs = [row_spec(size, width)] + specs
    return pl.pallas_call(
        functools.partial(ff_backward_kernel, last),
        grid=(total // size,),
        in_specs=[row_spec(size, width), row_spec(size, width), row_spec(size, 1)]
        + [whole_spec(gain.shape)]
        + [whole_spec(w.shape) for w in (wg, wu, wd)],
        out_specs=specs,
        out_shape=outs,
        scratch_shapes=[
            pltpu.VMEM((width, total), bf16),
            pltpu.VMEM((width, total), bf16),
            pltpu.VMEM((total, ff), bf16),
            pltpu.VMEM((total, ff), bf16),
            pltpu.VMEM((total, ff), bf16),
        ],
        compiler_params=params(),
        cost_estimate=cost(16 * total * wg.size, h, dy, wg, wu, wd, *outs),
        name="ff_bwd",
    )(h, dy, live, gain, wg, wu, wd)


def sum_shards(buffer):
    shard = lax.psum_scatter(buffer, "fsdp", scatter_dimension=0, tiled=False)
    return lax.psum(shard, "rep").astype(f32)


def local(
    tokens, segment, attn_gain, w_query, key_weight, value_weight, w_out, mlp_gain,
    gate_weight, up_weight, down_weight, cotangent,
):
    devices = lax.axis_size("fsdp")
    rows, ff = gate_weight.shape[1:]
    width = rows * devices
    down_rows = down_weight.shape[1]
    live, table = geometry(segment)

    gains = jnp.concatenate([attn_gain, mlp_gain]).reshape(1, 4 * rows)
    gains = jnp.pad(gains, ((0, 0), (0, QK_WIDTH + Q_WIDTH + KV_WIDTH - 4 * rows)))
    attn_w, feed_w = [], []
    for layer in range(DECODER_LAYERS):
        packed = jnp.concatenate(
            [w_query[layer], key_weight[layer], w_out[layer], value_weight[layer]], axis=1
        )
        if layer == 0:
            packed = jnp.concatenate([packed, gains])
            whole = lax.all_gather(packed, "fsdp", axis=0, tiled=False)
            all_gains = whole[:, rows, : 4 * rows].reshape(devices, 4, rows)
            all_gains = all_gains.transpose(1, 0, 2).reshape(4, 1, width).astype(f32)
            attn_w.append(whole[:, :rows].reshape(width, -1))
        else:
            attn_w.append(lax.all_gather(packed, "fsdp", axis=0, tiled=True))
        packed = jnp.concatenate(
            [gate_weight[layer], up_weight[layer], down_weight[layer].reshape(rows, ff)]
        )
        whole = lax.all_gather(packed, "fsdp", axis=0, tiled=False)
        feed_w.append(
            (
                whole[:, :rows].reshape(width, ff),
                whole[:, rows : 2 * rows].reshape(width, ff),
                whole[:, 2 * rows :].reshape(ff, width),
            )
        )

    h0, *kept0 = attn_forward(tokens, segment, live, table, all_gains[0], attn_w[0])
    x1 = ff_forward(h0, live, all_gains[2], *feed_w[0])
    h1, *kept1 = attn_forward(x1, segment, live, table, all_gains[1], attn_w[1])
    out_tokens, dh1, gg1, gu1, gd1, mg1 = ff_backward(
        h1, cotangent, live, all_gains[3], *feed_w[1], True
    )
    feed1 = sum_shards(
        jnp.concatenate(
            [g.reshape(devices, rows, ff) for g in (gg1, gu1, gd1)], axis=1
        )
    )
    dx1, ga1, ag1 = attn_backward(x1, dh1, segment, live, table, all_gains[1], attn_w[1], kept1)
    dh0, gg0, gu0, gd0, mg0 = ff_backward(h0, dx1, live, all_gains[2], *feed_w[0], False)
    feed0 = sum_shards(
        jnp.concatenate(
            [g.reshape(devices, rows, ff) for g in (gg0, gu0, gd0)], axis=1
        )
    )
    dx0, ga0, ag0 = attn_backward(
        tokens, dh0, segment, live, table, all_gains[0], attn_w[0], kept0
    )
    zero = jnp.zeros((devices, 1, ff - 4 * rows), bf16)
    gain_grads = jnp.concatenate(
        [g.reshape(devices, 1, rows).astype(bf16) for g in (ag0, ag1, mg0, mg1)] + [zero], axis=2
    )
    attn1 = sum_shards(ga1.reshape(devices, rows, ff))
    attn0 = sum_shards(jnp.concatenate([ga0.reshape(devices, rows, ff), gain_grads], axis=1))
    last = attn0[rows]
    attn = jnp.stack([attn0[:rows], attn1])
    feed = jnp.stack([feed0, feed1])
    return (
        out_tokens,
        dx0,
        last[: 2 * rows].reshape(2, rows),
        attn[:, :, :Q_WIDTH],
        attn[:, :, Q_WIDTH:QK_WIDTH],
        attn[:, :, QK_WIDTH + Q_WIDTH :],
        attn[:, :, QK_WIDTH : QK_WIDTH + Q_WIDTH],
        last[2 * rows : 4 * rows].reshape(2, rows),
        feed[:, :rows],
        feed[:, rows : 2 * rows],
        feed[:, 2 * rows :].reshape(2, down_rows, width),
    )


def solution(mesh):
    rows = P(("rep", "fsdp"), None)
    flat, cube = P(None, "fsdp"), P(None, "fsdp", None)
    in_specs = (rows, P(("rep", "fsdp")), flat, cube, cube, cube, cube, flat, cube, cube, cube, rows)
    out_specs = (rows, rows, flat, cube, cube, cube, cube, flat, cube, cube, cube)
    return jax.shard_map(local, mesh=mesh, in_specs=in_specs, out_specs=out_specs, check_vma=False)
```

time: 711 us -> 610 us (0.86)
  matrix products: 184 us -> 0 us
  waiting for transfers between devices: 155 us -> 292 us
  Pallas kernels: 115 us -> 214 us
  blocking collectives: 59.2 us -> 0 us
  local copies, waits for them, and re-layouts: 101 us -> 58.3 us
  other arithmetic: 63 us -> 24.7 us
    dot_general x42 -> x0, matrix products: 184 us -> none  [the longest x14 58.4 us: times_transposed(): lax.dot_general(left, right, (((1,), (1,)), ((), ())), preferred_element_...]
    pallas_call x4 -> x7, Pallas kernels: 115 us -> 214 us  [the longest x2 79.5 us: ff_backward(): pl.pallas_call(functools.partial(ff_backward_kernel, last), grid=(total /...]
    psum x0 -> x1, waiting for transfers between devices: none -> 60 us  [sum_shards(): return lax.psum(shard, 'rep').astype(f32)]
    all_gather x4 -> x3, waiting for transfers between devices: 36.7 us -> 89.6 us  [local(): whole = lax.all_gather(packed, 'fsdp', axis=0, tiled=False)]
    all_gather x3 -> x0, blocking collectives: 29.8 us -> none  [sum_shards(): return lax.all_gather(part, 'rep', axis=0, tiled=True)]
    unnamed x1 -> x0, blocking collectives: 29.4 us -> none
    convert_element_type x16 -> x7, local copies, waits for them, and re-layouts: 23.7 us -> 0.45 us  [the longest x4 0.36 us: local(): g.reshape(devices, 1, rows).astype(bf16)]
    reduce_scatter x4, waiting for transfers between devices: 118 us -> 141 us  [sum_shards(): shard = lax.psum_scatter(buffer, 'fsdp', scatter_dimension=0, tiled=False)]
  transfers between devices with their start and end apart: 11 -> 9, of which waited for: 6 -> 8; matrix products, arithmetic and copies ran while one was open for 28% -> 12% of each run, Pallas kernels for 7% -> 19%
where the time goes in v1:
time: 610 us; the launch traced here: 604 us
  waiting for transfers between devices  292 us (48%)
  Pallas kernels  214 us (35%)
  local copies, waits for them, and re-layouts  58.3 us (10%)
  other arithmetic  24.7 us (4%)
  between operations  14.4 us (2%)
    reduce_scatter x4, waiting for transfers between devices, sum_shards(): shard = lax.psum_scatter(buffer, 'fsdp', scatter_dimension=0, tiled=False)  141 us
    all_gather x3, waiting for transfers between devices, local(): whole = lax.all_gather(packed, 'fsdp', axis=0, tiled=False)  89.6 us
    pallas_call x2, Pallas kernels, ff_backward(): pl.pallas_call(functools.partial(ff_backward_kernel, last), grid=(total /...  79.5 us
    pallas_call x2, Pallas kernels, attn_backward(): pl.pallas_call(attn_backward_kernel, grid=(MICRO,), in_specs=[row_spec(si...  73.2 us
    psum x1, waiting for transfers between devices, sum_shards(): return lax.psum(shard, 'rep').astype(f32)  60 us
    pallas_call x2, Pallas kernels, attn_forward(): pl.pallas_call(attn_forward_kernel, grid=(MICRO,), in_specs=[row_spec(siz...  44.5 us
    pallas_call x1, Pallas kernels, ff_forward(): pl.pallas_call(ff_forward_kernel, grid=(total // size,), in_specs=[row_sp...  17.1 us
    unnamed x32, local copies, waits for them, and re-layouts  12.3 us
  transfers between devices with their start and end apart: 9, of which 8 were waited for; matrix products, arithmetic and copies ran while one was open for 12% of the time, Pallas kernels for 19%

profile of v1, /device:TPU:0, one launch (start us, length us, event | category | flops | bytes accessed | tf_op | source)
XLA Modules:
  0.0 604.0 jit_solution(2016953283747094806)
XLA Ops:
  16.6 1.5 select_reduce_fusion
  19.2 2.3 copy.98.x_ref
  21.5 2.3 copy.104.dy_ref
  23.8 2.8 multiply_sine_fusion
  26.6 3.0 concatenate.33.table_ref
  29.6 12.1 %all-gather.15.cloned.1.call-done = bf16[8,73,1536]{2,1,0:T(8,128)(2,1)} async-done(((bf16[1,73,1536]{2,1,0:T(8,128)(2,1)}), bf16[8,73,1536]{2,1,0:T(8,128)(2,1)}) %all-gather.15.cloned.1.call-update) | async-done | bytes 1794064 | tf_op jit(solution)/shard_map/all_gather | solution.py:474
  45.3 2.8 slice.158
  48.1 22.4 %attn_fwd.2 = (f32[1536,576]{1,0:T(8,128)}, bf16[1536,768]{1,0:T(8,128)(2,1)}, bf16[1536,192]{1,0:T(8,128)(2,1)}, bf16[1536,576]{1,0:T(8,128)(2,1)}, f32[16,1536]{1,0:T(8,128)}) custom-call(bf16[1536,576]{1,0:T(8,128)(2,1)} %copy.98.x_ref, s32[1536,1]{1,0:T(8,128)} %reshape.232.column_ref, s32[2,1,768]{2,1,0:T(1,128)} %reshape.202.row_ref, ...), custom_call_target="tpu_custom_call" | custom-call | flops 8153726976 | bytes 11894784 | tf_op jit(solution)/shard_map/attn_fwd/pallas_call | solution.py:332
  70.5 29.0 %all-gather.11.cloned.1.call-done = bf16[1728,1536]{1,0:T(8,128)(2,1)} async-done(((bf16[216,1536]{1,0:T(8,128)(2,1)}), bf16[1728,1536]{1,0:T(8,128)(2,1)}) %all-gather.11.cloned.1.call-update) | async-done | bytes 5308432 | tf_op jit(solution)/shard_map/all_gather | solution.py:483
  99.6 4.7 fusion.9
  104.3 3.9 reshape.207.wd_ref
  108.1 48.4 %all-gather.13.cloned.1.call-done = bf16[1728,1536]{1,0:T(8,128)(2,1)} async-done(((bf16[216,1536]{1,0:T(8,128)(2,1)}), bf16[1728,1536]{1,0:T(8,128)(2,1)}) %all-gather.13.cloned.1.call-update) | async-done | bytes 5308432 | tf_op jit(solution)/shard_map/all_gather | solution.py:483
  156.6 4.8 fusion.8
  161.4 3.9 reshape.210.wd_ref
  165.3 17.1 %ff_fwd.1.x_ref = f32[1536,576]{1,0:T(8,128)} custom-call(f32[1536,576]{1,0:T(8,128)} %get-tuple-element.38.h_ref, f32[1536,1]{1,0:T(8,128)} %broadcast_in_dim.33.live_ref, f32[1,576]{1,0:T(1,128)} %squeeze.57.gain_ref, bf16[576,1536]{1,0:T(8,128)(2,1)} %bitcast.55, bf16[576,1536]{1,0:T(8,128)(2,1)} %bitcast.53, bf16[1536,576]{1,0:T(8,128)(2,1)} %reshape.207.wd_ref), custom_call_target="tpu_custom_call" | custom-call | flops 8153726976 | bytes 12386304 | tf_op jit(solution)/shard_map/ff_fwd/pallas_call | solution.py:401
  183.8 22.1 %attn_fwd.3 = (f32[1536,576]{1,0:T(8,128)}, bf16[1536,768]{1,0:T(8,128)(2,1)}, bf16[1536,192]{1,0:T(8,128)(2,1)}, bf16[1536,576]{1,0:T(8,128)(2,1)}, f32[16,1536]{1,0:T(8,128)}) custom-call(f32[1536,576]{1,0:T(8,128)} %ff_fwd.1.x_ref, s32[1536,1]{1,0:T(8,128)} %reshape.232.column_ref, s32[2,1,768]{2,1,0:T(1,128)} %reshape.202.row_ref, ...), custom_call_target="tpu_custom_call" | custom-call | flops 8153726976 | bytes 13664256 | tf_op jit(solution)/shard_map/attn_fwd/pallas_call | solution.py:332
  205.9 40.5 %ff_bwd.2 = (bf16[1536,576]{1,0:T(8,128)(2,1)}, f32[1536,576]{1,0:T(8,128)}, bf16[576,1536]{1,0:T(8,128)(2,1)}, bf16[576,1536]{1,0:T(8,128)(2,1)}, bf16[1536,576]{1,0:T(8,128)(2,1)}, /*index=5*/f32[1,576]{1,0:T(1,128)}) custom-call(f32[1536,576]{1,0:T(8,128)} %get-tuple-element.39.h_ref, bf16[1536,576]{1,0:T(8,128)(2,1)} %copy.104.dy_ref, ...), custom_call_target="tpu_custom_call" | custom-call | flops 21743271936 | bytes 21235968 | tf_op jit(solution)/shard_map/ff_bwd/pallas_call | solution.py:429
  246.4 36.9 %attn_bwd.2 = (f32[1536,576]{1,0:T(8,128)}, bf16[576,1536]{1,0:T(8,128)(2,1)}, f32[1,576]{1,0:T(1,128)}) custom-call(f32[1536,576]{1,0:T(8,128)} %ff_fwd.1.x_ref, f32[1536,576]{1,0:T(8,128)} %get-tuple-element.41.dh_ref, s32[1536,1]{1,0:T(8,128)} %reshape.232.column_ref, s32[2,1,768]{2,1,0:T(1,128)} %reshape.202.row_ref, ...), custom_call_target="tpu_custom_call" | custom-call | flops 19025362944 | bytes 14158080 | tf_op jit(solution)/shard_map/attn_bwd/pallas_call | solution.py:358
  283.4 39.0 %ff_bwd.3 = (f32[1536,576]{1,0:T(8,128)}, bf16[576,1536]{1,0:T(8,128)(2,1)}, bf16[576,1536]{1,0:T(8,128)(2,1)}, bf16[1536,576]{1,0:T(8,128)(2,1)}, f32[1,576]{1,0:T(1,128)}) custom-call(f32[1536,576]{1,0:T(8,128)} %get-tuple-element.38.h_ref, f32[1536,576]{1,0:T(8,128)} %get-tuple-element.46.dy_ref, f32[1536,1]{1,0:T(8,128)} %broadcast_in_dim.33.live_ref, ...), custom_call_target="tpu_custom_call" | custom-call | flops 21743271936 | bytes 21235968 | tf_op jit(solution)/shard_map/ff_bwd/pallas_call | solution.py:429
  322.4 36.3 %attn_bwd.3 = (f32[1536,576]{1,0:T(8,128)}, bf16[576,1536]{1,0:T(8,128)(2,1)}, f32[1,576]{1,0:T(1,128)}) custom-call(bf16[1536,576]{1,0:T(8,128)(2,1)} %copy.98.x_ref, f32[1536,576]{1,0:T(8,128)} %get-tuple-element.47.dh_ref, s32[1536,1]{1,0:T(8,128)} %reshape.232.column_ref, s32[2,1,768]{2,1,0:T(1,128)} %reshape.202.row_ref, ...), custom_call_target="tpu_custom_call" | custom-call | flops 19025362944 | bytes 12388608 | tf_op jit(solution)/shard_map/attn_bwd/pallas_call | solution.py:358
  360.2 2.9 pad_maximum_fusion.2
  363.2 4.3 reshape.217
  367.6 4.2 pad_maximum_fusion
  371.9 4.3 reshape.220
  376.2 4.3 pad_maximum_fusion.1
  380.6 17.8 %reduce-scatter.5.cloned.1.call-done = bf16[1,73,1536]{2,1,0:T(8,128)(2,1)} async-done(((bf16[8,73,1536]{2,1,0:T(8,128)(2,1)}), bf16[1,73,1536]{2,1,0:T(8,128)(2,1)}) %reduce-scatter.5.cloned.1.call-update) | async-done | bytes 224272 | tf_op jit(solution)/shard_map/reduce_scatter | solution.py:451
  398.4 61.4 %reduce-scatter.9.cloned.1.call-done = bf16[1,216,1536]{2,1,0:T(8,128)(2,1)} async-done(((bf16[8,216,1536]{2,1,0:T(8,128)(2,1)}), bf16[1,216,1536]{2,1,0:T(8,128)(2,1)}) %reduce-scatter.9.cloned.1.call-update) | async-done | bytes 663568 | tf_op jit(solution)/shard_map/reduce_scatter | solution.py:451
  459.8 61.3 %reduce-scatter.11.cloned.1.call-done = bf16[1,216,1536]{2,1,0:T(8,128)(2,1)} async-done(((bf16[8,216,1536]{2,1,0:T(8,128)(2,1)}), bf16[1,216,1536]{2,1,0:T(8,128)(2,1)}) %reduce-scatter.11.cloned.1.call-update) | async-done | bytes 663568 | tf_op jit(solution)/shard_map/reduce_scatter | solution.py:451
  521.1 5.4 copy.117
  526.6 2.2 copy.116
  528.8 60.0 %all-reduce.4.cloned.1.call-done = (bf16[73,1536]{1,0:T(8,128)(2,1)}, bf16[1,72,1536]{2,1,0:T(8,128)(2,1)}, bf16[1,216,1536]{2,1,0:T(8,128)(2,1)}, bf16[1,216,1536]{2,1,0:T(8,128)(2,1)}) async-done(((bf16[73,1536]{1,0:T(8,128)(2,1)}, bf16[1,72,1536]{2,1,0:T(8,128)(2,1)}, bf16[1,216,1536]{2,1,0:T(8,128)(2,1)}, bf16[1,216,1536]{2,1,0:T(8,128)(2,1)}), (bf16[73,1536]{1,0:T(8,128)(2,1)}, ...) | async-done | bytes 1772560 | tf_op jit(solution)/shard_map/psum | solution.py:452
  594.3 1.6 reshape.221
  (98 shorter events, 23.8 us)
Async XLA Ops:
  7.2 3.7 copy-start.7
  7.2 4.2 copy-start.9
  7.2 4.2 copy-start.8
  7.2 34.5 %all-gather.15.cloned.1.call-start = ((), (), s32[]{:S(2)}) async-start(), calls=%async_computation.11 | async-start | bytes 2211840 | tf_op jit(solution)/shard_map/all_gather | solution.py:474
  10.9 88.7 %all-gather.11.cloned.1.call-start = ((), (), s32[]{:S(2)}) async-start(), calls=%async_computation.9 | async-start | bytes 5971968 | tf_op jit(solution)/shard_map/all_gather | solution.py:483
  12.3 2.5 copy-start.10
  12.4 144.2 %all-gather.13.cloned.1.call-start = ((), (), s32[]{:S(2)}) async-start(), calls=%async_computation.10 | async-start | bytes 5971968 | tf_op jit(solution)/shard_map/all_gather | solution.py:483
  13.7 5.6 copy-start.1
  13.7 170.1 %all-gather.9.cloned.1.call-start = ((), (), s32[]{:S(2)}) async-start(), calls=%async_computation.4 | async-start | bytes 1990656 | tf_op jit(solution)/shard_map/all_gather | solution.py:479
  14.6 366.0 %reduce-scatter.7.cloned.1.call-start = ((), (), s32[]{:S(2)}) async-start(), calls=%async_computation.6 | async-start | bytes 1990656 | tf_op jit(solution)/shard_map/reduce_scatter | solution.py:451
  19.2 2.3 copy-start.2
  283.3 115.0 %reduce-scatter.5.cloned.1.call-start = ((), (), s32[]{:S(2)}) async-start(), calls=%async_computation.5 | async-start | bytes 2211840 | tf_op jit(solution)/shard_map/reduce_scatter | solution.py:451
  322.4 37.2 %copy-start.13 = (f32[1,576]{1,0:T(1,128)S(1)}, f32[1,576]{1,0:T(1,128)}, u32[]{:S(2)}) copy-start(f32[1,576]{1,0:T(1,128)} %get-tuple-element.56) | copy-start | bytes 6916
  322.4 37.3 %copy-start.12 = (f32[1,576]{1,0:T(1,128)S(1)}, f32[1,576]{1,0:T(1,128)}, u32[]{:S(2)}) copy-start(f32[1,576]{1,0:T(1,128)} %get-tuple-element.55) | copy-start | bytes 6916
  322.4 37.4 %copy-start.11 = (f32[1,576]{1,0:T(1,128)S(1)}, f32[1,576]{1,0:T(1,128)}, u32[]{:S(2)}) copy-start(f32[1,576]{1,0:T(1,128)} %get-tuple-element.57) | copy-start | bytes 6916
  363.2 4.4 copy-start.4
  363.2 96.6 %reduce-scatter.9.cloned.1.call-start = ((), (), s32[]{:S(2)}) async-start(), calls=%async_computation.7 | async-start | bytes 5971968 | tf_op jit(solution)/shard_map/reduce_scatter | solution.py:451
  371.8 4.4 copy-start.3
  371.8 149.3 %reduce-scatter.11.cloned.1.call-start = ((), (), s32[]{:S(2)}) async-start(), calls=%async_computation.8 | async-start | bytes 5971968 | tf_op jit(solution)/shard_map/reduce_scatter | solution.py:451
  380.5 208.2 %all-reduce.4.cloned.1.call-start = ((), (), s32[]{:S(2)}) async-start(), calls=%async_computation.12 | async-start | bytes 3588096 | tf_op jit(solution)/shard_map/psum | solution.py:452
  521.1 5.4 copy-start
  589.7 3.0 copy-start.5
  589.7 3.0 copy-start.6
Sparse Core Ops, SparseCore 0:
  11.0 30.7 all-gather.14
  43.4 56.1 all-gather.10
  101.2 55.3 all-gather.12
  158.7 25.1 all-gather.8
  283.5 34.4 reduce-scatter.6
  363.3 35.0 reduce-scatter.4
  400.8 58.9 reduce-scatter.8
  462.2 58.8 reduce-scatter.10
  525.1 63.6 all-reduce.3

commit v2 on v1

--- a/solution.py
+++ b/solution.py
@@ -107,12 +107,303 @@
     )
 
 
+MESH_AXES = ("rep", "fsdp")
+
+
+class Place:
+    def __init__(self):
+        self.copies = lax.axis_size("rep")
+        self.line = lax.axis_size("fsdp") // 2
+        self.r = lax.axis_index("rep")
+        index = lax.axis_index("fsdp")
+        self.z = index // 2
+        self.c = index % 2
+
+    def at(self, r, z, c):
+        return (r, 2 * z + c)
+
+    def partner(self):
+        return self.at(self.r, self.z, 1 - self.c)
+
+    def chip(self, k):
+        return lax.rem(self.z + k, self.line)
+
+    def replica(self, j):
+        return lax.rem(self.r + j, self.copies)
+
+    def greet(self):
+        barrier = pltpu.get_barrier_semaphore()
+        peers = [self.partner()]
+        peers += [self.at(self.r, self.chip(k), self.c) for k in range(1, self.line)]
+        peers += [self.at(self.replica(j), self.z, self.c) for j in range(1, self.copies)]
+        for peer in peers:
+            pl.semaphore_signal(barrier, inc=1, device_id=peer, device_id_type=pl.DeviceIdType.MESH)
+        pl.semaphore_wait(barrier, len(peers))
+
+
+def remote(source, target, send, receive, device):
+    return pltpu.make_async_remote_copy(
+        src_ref=source, dst_ref=target, send_sem=send, recv_sem=receive,
+        device_id=device, device_id_type=pl.DeviceIdType.MESH,
+    )
+
+
+def part_of(dims, parts):
+    rows, cols = dims
+    if cols % (128 * parts) == 0:
+        return 1, cols // parts
+    return 0, rows // parts
+
+
+def can_cut(dims, parts):
+    rows, cols = dims
+    return cols % (128 * parts) == 0 or rows % (16 * parts) == 0
+
+
+def piece(ref, lead, dims, parts, index):
+    axis, size = part_of(dims, parts)
+    if axis == 1:
+        return ref.at[lead, :, pl.ds(pl.multiple_of(index * size, 128), size)]
+    return ref.at[lead, pl.ds(pl.multiple_of(index * size, 16), size), :]
+
+
+def piece_dims(dims, parts):
+    axis, size = part_of(dims, parts)
+    return (dims[0], size) if axis == 1 else (size, dims[1])
+
+
+class Gather:
+    def __init__(self, place, layer, shard, whole, sems):
+        self.p, self.layer, self.shard, self.whole = place, layer, shard, whole
+        self.sems = sems
+        self.dims = shard.shape[1:]
+        self.parts = place.copies
+
+    @staticmethod
+    def semaphores(copies, line):
+        return [
+            pltpu.SemaphoreType.DMA((2, line)),
+            pltpu.SemaphoreType.DMA((2, line, copies)),
+            pltpu.SemaphoreType.DMA((2, line)),
+            pltpu.SemaphoreType.DMA,
+        ]
+
+    def own(self):
+        p = self.p
+        return pltpu.make_async_copy(
+            self.shard.at[self.layer], self.whole.at[2 * p.z + p.c], self.sems[3]
+        )
+
+    def along(self, k):
+        p = self.p
+        return remote(
+            piece(self.shard, self.layer, self.dims, self.parts, p.r),
+            piece(self.whole, 2 * p.z + p.c, self.dims, self.parts, p.r),
+            self.sems[0].at[0, k], self.sems[0].at[1, k], p.at(p.r, p.chip(k), p.c),
+        )
+
+    def across(self, k, j):
+        p = self.p
+        block = piece(
+            self.whole, 2 * p.chip(p.line - k) + p.c, self.dims, self.parts, p.r
+        )
+        return remote(
+            block, block, self.sems[1].at[0, k, j], self.sems[1].at[1, k, j],
+            p.at(p.replica(j), p.z, p.c),
+        )
+
+    def pair(self, k):
+        p = self.p
+        index = 2 * p.chip(p.line - k) + p.c
+        source = self.shard.at[self.layer] if k == 0 else self.whole.at[index]
+        return remote(
+            source, self.whole.at[index], self.sems[2].at[0, k], self.sems[2].at[1, k], p.partner()
+        )
+
+    def start(self):
+        for k in range(1, self.p.line):
+            self.along(k).start()
+        self.own().start()
+        self.pair(0).start()
+
+    def second(self):
+        for k in range(1, self.p.line):
+            self.along(k).wait_recv()
+            for j in range(1, self.p.copies):
+                self.across(k, j).start()
+
+    def third(self):
+        for k in range(1, self.p.line):
+            for j in range(1, self.p.copies):
+                self.across(k, j).wait_recv()
+            self.pair(k).start()
+
+    def finish(self):
+        self.own().wait()
+        for k in range(self.p.line):
+            self.pair(k).wait()
+            if k:
+                self.along(k).wait_send()
+                for j in range(1, self.p.copies):
+                    self.across(k, j).wait_send()
+
+
+class Reduce:
+    def __init__(self, place, source, out, buffers):
+        self.p, self.source, self.out = place, source, out
+        self.dims = source.shape[1:]
+        self.parts = place.copies
+        (self.mine, self.theirs, self.across_in, self.line_out, self.line_in, self.final,
+         self.s0, self.s1, self.s2, self.s3, self.s4) = buffers
+
+    @staticmethod
+    def scratch(dims, copies, line):
+        small = piece_dims(dims, copies)
+        return [
+            pltpu.VMEM((line,) + tuple(dims), bf16),
+            pltpu.VMEM((line,) + tuple(dims), bf16),
+            pltpu.VMEM((copies, line) + small, bf16),
+            pltpu.VMEM((line,) + small, bf16),
+            pltpu.VMEM((line,) + small, bf16),
+            pltpu.VMEM((copies,) + small, bf16),
+            pltpu.SemaphoreType.DMA((2, line)),
+            pltpu.SemaphoreType.DMA((line,)),
+            pltpu.SemaphoreType.DMA((2, copies, line)),
+            pltpu.SemaphoreType.DMA((2, line)),
+            pltpu.SemaphoreType.DMA((2, copies)),
+        ]
+
+    def pair(self, z):
+        p = self.p
+        return remote(
+            self.source.at[2 * z + 1 - p.c], self.theirs.at[z],
+            self.s0.at[0, z], self.s0.at[1, z], p.partner(),
+        )
+
+    def load(self, z):
+        return pltpu.make_async_copy(
+            self.source.at[2 * z + self.p.c], self.mine.at[z], self.s1.at[z]
+        )
+
+    def across(self, j, z):
+        p = self.p
+        return remote(
+            piece(self.mine, z, self.dims, self.parts, p.replica(j)), self.across_in.at[j, z],
+            self.s2.at[0, j, z], self.s2.at[1, j, z], p.at(p.replica(j), p.z, p.c),
+        )
+
+    def along(self, k):
+        p = self.p
+        return remote(
+            self.line_out.at[p.chip(k)], self.line_in.at[k],
+            self.s3.at[0, k], self.s3.at[1, k], p.at(p.r, p.chip(k), p.c),
+        )
+
+    def spread(self, j):
+        p = self.p
+        return remote(
+            self.final.at[p.r], self.final.at[p.r],
+            self.s4.at[0, j], self.s4.at[1, j], p.at(p.replica(j), p.z, p.c),
+        )
+
+    def start(self):
+        for z in range(self.p.line):
+            self.pair(z).start()
+            self.load(z).start()
+
+    def second(self):
+        for z in range(self.p.line):
+            self.load(z).wait()
+            self.pair(z).wait_recv()
+            self.mine[z] = (self.mine[z].astype(f32) + self.theirs[z].astype(f32)).astype(bf16)
+            for j in range(1, self.p.copies):
+                self.across(j, z).start()
+
+    def third(self):
+        for z in range(self.p.line):
+            total = piece(self.mine, z, self.dims, self.parts, self.p.r)[...].astype(f32)
+            for j in range(1, self.p.copies):
+                self.across(j, z).wait_recv()
+                total += self.across_in[j, z].astype(f32)
+            self.line_out[z] = total.astype(bf16)
+        for k in range(1, self.p.line):
+            self.along(k).start()
+
+    def fourth(self):
+        total = self.line_out[self.p.z].astype(f32)
+        for k in range(1, self.p.line):
+            self.along(k).wait_recv()
+            total += self.line_in[k].astype(f32)
+        self.final[self.p.r] = total.astype(bf16)
+        for j in range(1, self.p.copies):
+            self.spread(j).start()
+
+    def finish(self):
+        for j in range(1, self.p.copies):
+            self.spread(j).wait()
+        axis, size = part_of(self.dims, self.parts)
+        for index in range(self.parts):
+            here = slice(index * size, (index + 1) * size)
+            if axis == 1:
+                self.out[:, here] = self.final[index].astype(f32)
+            else:
+                self.out[here, :] = self.final[index].astype(f32)
+        for z in range(self.p.line):
+            self.pair(z).wait_send()
+            for j in range(1, self.p.copies):
+                self.across(j, z).wait_send()
+        for k in range(1, self.p.line):
+            self.along(k).wait_send()
+
+
+class Plan:
+    def __init__(self, step, steps):
+        self.step, self.steps, self.at = step, steps, {}
+
+    def put(self, when, point, *acts):
+        self.at.setdefault((when, point), []).extend(acts)
+
+    def run(self, point):
+        for when in range(self.steps):
+            acts = self.at.get((when, point), [])
+            if acts:
+                @pl.when(self.step == when)
+                def _(acts=acts):
+                    for act in acts:
+                        act()
+
+
 def attn_forward_kernel(
-    x_ref, column_ref, row_ref, live_ref, table_ref, gain_ref, weight_ref,
-    h_ref, qk_ref, v_ref, a_ref, lse_ref,
+    layer, count, turned, x_ref, column_ref, row_ref, live_ref, table_ref, gain_ref, weight_ref,
+    *rest
 ):
-    rows = x_ref.shape[0]
-    x = x_ref[...].astype(f32)
+    shards, rest = rest[:count], rest[count:]
+    h_ref, qk_ref, v_ref, a_ref, lse_ref, *rest = rest
+    wholes, sems = rest[:count], rest[count:]
+    plan = Plan(pl.program_id(0), MICRO)
+    if count:
+        place = Place()
+        moves = [
+            Gather(place, layer, shards[i], wholes[i], sems[4 * i : 4 * i + 4])
+            for i in range(count)
+        ]
+        plan.put(0, "start", place.greet, *[move.start for move in moves])
+        if count == 1:
+            plan.put(0, 6, moves[0].second)
+            plan.put(1, 6, moves[0].third)
+        else:
+            one, two, three = moves
+            plan.put(0, 4, one.second)
+            plan.put(0, "end", two.second)
+            plan.put(1, 2, one.third)
+            plan.put(1, 3, three.second)
+            plan.put(1, 7, two.third)
+            plan.put(1, "end", three.third)
+        plan.put(1, "end", *[move.finish for move in moves])
+    plan.run("start")
+    x = (x_ref[...].T if turned else x_ref[...]).astype(f32)
+    rows = x.shape[0]
+    h_ref[...] = x
     normed = (x * norm(x) * gain_ref[...]).astype(bf16)
     qk = nn(normed, weight_ref[:, :QK_WIDTH])
     v_ref[...] = nn(normed, weight_ref[:, QK_WIDTH + Q_WIDTH :]).astype(bf16)
@@ -120,7 +411,9 @@
     qk_ref[:, :Q_WIDTH] = qk[:, :Q_WIDTH] * SCALE
     qk_ref[:, Q_WIDTH:] = qk[:, Q_WIDTH:]
     size = tile_of(rows)
-    for start in range(0, rows, size):
+    tiles = rows // size
+    for tile in range(tiles):
+        start = tile * size
         reach = start + size
         bias = mask_bias(column_ref, row_ref, start, size)
         outputs = []
@@ -139,19 +432,46 @@
                 lse_ref[group * GROUP + j : group * GROUP + j + 1, start:reach] = line[
                     :, j * size : (j + 1) * size
                 ]
+            plan.run(tile * KEY_VALUE_HEADS + group)
         a_ref[start:reach, :] = jnp.concatenate(outputs, axis=1).astype(bf16)
     out = nn(a_ref[...], weight_ref[:, QK_WIDTH : QK_WIDTH + Q_WIDTH])
-    h_ref[...] = x_ref[...].astype(f32) + out * live_ref[...]
+    h_ref[...] = h_ref[...] + out * live_ref[...]
+    for point in range(tiles * KEY_VALUE_HEADS, 9):
+        plan.run(point)
+    plan.run("end")
 
 
 def attn_backward_kernel(
-    x_ref, dh_ref, column_ref, row_ref, live_ref, table_ref, gain_ref, weight_ref,
-    qk_ref, v_ref, a_ref, lse_ref,
-    dx_ref, grad_ref, gain_grad_ref,
-    n1t_ref, at_ref, c_ref, dqk_ref, dv_ref, da_ref, weight_line_ref, dqk_sum, dv_sum,
+    count, turned, x_ref, dh_ref, column_ref, row_ref, live_ref, table_ref, gain_ref, weight_ref,
+    qk_ref, v_ref, a_ref, lse_ref, *rest
 ):
+    sources, rest = rest[:count], rest[count:]
+    dx_ref, grad_ref, gain_grad_ref, *rest = rest
+    results, rest = rest[:count], rest[count:]
+    (n1t_ref, at_ref, c_ref, dqk_ref, dv_ref, da_ref, weight_line_ref, dqk_sum, dv_sum) = rest[:9]
+    buffers = rest[9:]
     step = pl.program_id(0)
-    rows = x_ref.shape[0]
+    plan = Plan(step, MICRO)
+    if count:
+        place = Place()
+        moves = [
+            Reduce(place, sources[i], results[i], buffers[11 * i : 11 * i + 11])
+            for i in range(count)
+        ]
+        plan.put(0, "start", place.greet, *[move.start for move in moves])
+        one, two = moves[:2]
+        plan.put(0, 0, one.second, two.second)
+        plan.put(0, 6, one.third)
+        plan.put(1, 0, one.fourth)
+        plan.put(1, 1, two.third)
+        plan.put(1, 4, two.fourth)
+        if count == 3:
+            plan.put(0, 1, moves[2].second)
+            plan.put(1, 8, moves[2].third)
+            plan.put(1, "end", moves[2].fourth)
+        plan.put(1, "end", *[move.finish for move in moves])
+    plan.run("start")
+    rows = dh_ref.shape[0]
     here = pl.ds(pl.multiple_of(step * rows, rows), rows)
     c = (dh_ref[...] * live_ref[...]).astype(bf16)
     c_ref[here, :] = c
@@ -169,7 +489,9 @@
     pick = jnp.where(pick, 1.0, 0.0).astype(bf16)
     weight_line_ref[...] = nt(pick, high) + nt(pick, low)
     size = tile_of(rows)
-    for start in reversed(range(0, rows, size)):
+    tiles = rows // size
+    for tile in reversed(range(tiles)):
+        start = tile * size
         reach = start + size
         bias = mask_bias(column_ref, row_ref, start, size)
         query_grads = []
@@ -194,21 +516,25 @@
             else:
                 dqk_sum[:reach, klanes] += key_grad
                 dv_sum[:reach, lanes] += value_grad
+            plan.run((tiles - 1 - tile) * KEY_VALUE_HEADS + group)
         dqk_sum[start:reach, :Q_WIDTH] = jnp.concatenate(query_grads, axis=1)
+    for point in range(tiles * KEY_VALUE_HEADS, 9):
+        plan.run(point)
     dqk = rotate(dqk_sum[...], table_ref[:, :128], -table_ref[:, 128:]).astype(bf16)
     dqk_ref[here, :] = dqk
     dv = dv_sum[...].astype(bf16)
     dv_ref[here, :] = dv
     dn = nt(dqk, weight_ref[:, :QK_WIDTH]) + nt(dv, weight_ref[:, QK_WIDTH + Q_WIDTH :])
-    x = x_ref[...].astype(f32)
+    x = (x_ref[...].T if turned else x_ref[...]).astype(f32)
     factor = norm(x)
     unit = x * factor
     gain = gain_ref[...]
     n1t_ref[:, here] = (unit * gain).astype(bf16).T
     scaled = dn * gain
-    dx_ref[...] = dh_ref[...] + factor * (
+    dx = dh_ref[...] + factor * (
         scaled - unit * jnp.mean(scaled * unit, axis=-1, keepdims=True)
     )
+    dx_ref[...] = dx.T if turned else dx
     gain_part = jnp.sum(dn * unit, axis=0, keepdims=True)
 
     @pl.when(step == 0)
@@ -225,8 +551,27 @@
         grad_ref[:, QK_WIDTH : QK_WIDTH + Q_WIDTH] = nn(at_ref[...], c_ref[...]).astype(bf16)
         grad_ref[:, QK_WIDTH + Q_WIDTH :] = nn(n1t_ref[...], dv_ref[...]).astype(bf16)
 
-
-def ff_forward_kernel(h_ref, live_ref, gain_ref, wg_ref, wu_ref, wd_ref, y_ref):
+    plan.run("end")
+
+
+def ff_forward_kernel(
+    layer, count, steps, h_ref, live_ref, gain_ref, wg_ref, wu_ref, wd_ref, *rest
+):
+    shards, (y_ref, *rest) = rest[:count], rest[count:]
+    wholes, sems = rest[:count], rest[count:]
+    plan = Plan(pl.program_id(0), steps)
+    if count:
+        place = Place()
+        moves = [
+            Gather(place, layer, shards[i], wholes[i], sems[4 * i : 4 * i + 4])
+            for i in range(count)
+        ]
+        for move in moves:
+            plan.put(steps * 2 // 6, "start", move.second)
+            plan.put(steps * 5 // 6, "start", move.third)
+            plan.put(steps - 1, "end", move.finish)
+        plan.put(0, "start", place.greet, *[move.start for move in moves])
+    plan.run("start")
     h = h_ref[...]
     normed = (h * norm(h) * gain_ref[...]).astype(bf16)
     gate = nn(normed, wg_ref[...])
@@ -234,15 +579,33 @@
     half = 0.5 * gate
     inner = ((half + half * jnp.tanh(half)) * up).astype(bf16)
     y_ref[...] = h + nn(inner, wd_ref[...]) * live_ref[...]
+    plan.run("end")
 
 
 def ff_backward_kernel(
-    last, h_ref, dy_ref, live_ref, gain_ref, wg_ref, wu_ref, wd_ref, *rest,
+    last, count, steps, h_ref, dy_ref, live_ref, gain_ref, wg_ref, wu_ref, wd_ref, *rest,
 ):
+    sources, rest = rest[:count], rest[count:]
     if last:
         y_ref, *rest = rest
-    (dh_ref, gg_ref, gu_ref, gd_ref, gain_grad_ref, n2t_ref, et_ref, m_ref, dg_ref, du_ref) = rest
+    dh_ref, gg_ref, gu_ref, gd_ref, gain_grad_ref, *rest = rest
+    results, rest = rest[:count], rest[count:]
+    n2t_ref, et_ref, m_ref, dg_ref, du_ref, *buffers = rest
     step = pl.program_id(0)
+    plan = Plan(step, steps)
+    if count:
+        place = Place()
+        moves = [
+            Reduce(place, sources[i], results[i], buffers[11 * i : 11 * i + 11])
+            for i in range(count)
+        ]
+        plan.put(0, "start", place.greet, *[move.start for move in moves])
+        for move in moves:
+            plan.put(steps * 1 // 6, "start", move.second)
+            plan.put(steps * 4 // 6, "start", move.third)
+            plan.put(steps * 5 // 6, "end", move.fourth)
+            plan.put(steps - 1, "last", move.finish)
+    plan.run("start")
     rows = h_ref.shape[0]
     here = pl.ds(pl.multiple_of(step * rows, rows), rows)
     h = h_ref[...]
@@ -252,7 +615,7 @@
     normed = (unit * gain).astype(bf16)
     n2t_ref[:, here] = normed.T
     live = live_ref[...]
-    dy = dy_ref[...].astype(f32)
+    dy = (dy_ref[...].T if last else dy_ref[...]).astype(f32)
     e = (dy * live).astype(bf16)
     et_ref[:, here] = e.T
     gate = nn(normed, wg_ref[...])
@@ -267,11 +630,13 @@
     dg_ref[here, :] = dgate
     du_ref[here, :] = dup
     if last:
-        y_ref[...] = (h + nn(inner, wd_ref[...]) * live).astype(bf16)
+        y_ref[...] = (h + nn(inner, wd_ref[...]) * live).astype(bf16).T
     dn = nt(dgate, wg_ref[...]) + nt(dup, wu_ref[...])
     scaled = dn * gain
     dh_ref[...] = dy + factor * (scaled - unit * jnp.mean(scaled * unit, axis=-1, keepdims=True))
     gain_part = jnp.sum(dn * unit, axis=0, keepdims=True)
+
+    plan.run("end")
 
     @pl.when(step == 0)
     def _():
@@ -290,6 +655,8 @@
             gu_ref[:, cols] = nn(n2t_ref[...], du_ref[:, cols]).astype(bf16)
             gd_ref[cols, :] = nn(et_ref[...], m_ref[:, cols]).astype(bf16).T
 
+    plan.run("last")
+
 
 def row_spec(size, width):
     return pl.BlockSpec((size, width), lambda i: (i, 0))
@@ -299,6 +666,10 @@
     return pl.BlockSpec(shape, lambda i: (0,) * len(shape), pipeline_mode=pl.Buffered(1))
 
 
+def turned_spec(size, width):
+    return pl.BlockSpec((width, size), lambda i: (0, i))
+
+
 def still_spec(shape):
     return pl.BlockSpec(shape, lambda i: (0,) * len(shape))
 
@@ -307,8 +678,17 @@
     return jax.ShapeDtypeStruct(dims, dtype)
 
 
-def params(mib=60):
-    return pltpu.CompilerParams(vmem_limit_bytes=mib * 2**20, dimension_semantics=("arbitrary",))
+def params(collective_id=None, mib=62):
+    extra = {}
+    if collective_id is not None:
+        extra = {"collective_id": collective_id, "has_side_effects": True}
+    return pltpu.CompilerParams(
+        vmem_limit_bytes=mib * 2**20, dimension_semantics=("arbitrary",), **extra
+    )
+
+
+def any_spec():
+    return pl.BlockSpec(memory_space=pl.ANY)
 
 
 def cost(flops, *arrays):
@@ -319,8 +699,15 @@
     )
 
 
-def attn_forward(x, segment, live, table, gain, weight):
-    total, width = x.shape
+def attn_forward(
+    x, segment, live, table, gain, weight, turned, collective_id=None, layer=None, shards=()
+):
+    total, width = x.shape[::-1] if turned else x.shape
+    copies, devices = lax.axis_size("rep"), lax.axis_size("fsdp")
+    wholes = [shape((devices,) + w.shape[1:], bf16) for w in shards]
+    sems = []
+    for _ in shards:
+        sems += Gather.semaphores(copies, devices // 2)
     size = total // MICRO
     outs = [
         shape((total, width), f32),
@@ -330,36 +717,47 @@
         shape((LSE_ROWS, total), f32),
     ]
     return pl.pallas_call(
-        attn_forward_kernel,
+        functools.partial(attn_forward_kernel, layer, len(shards), turned),
         grid=(MICRO,),
         in_specs=[
-            row_spec(size, width),
+            turned_spec(size, width) if turned else row_spec(size, width),
             row_spec(size, 1),
             pl.BlockSpec((1, 1, size), lambda i: (i, 0, 0)),
             row_spec(size, 1),
             row_spec(size, 256),
             whole_spec(gain.shape),
             whole_spec(weight.shape),
-        ],
+        ]
+        + [any_spec() for _ in shards],
         out_specs=[row_spec(size, o.shape[1]) for o in outs[:4]]
-        + [pl.BlockSpec((LSE_ROWS, size), lambda i: (0, i))],
-        out_shape=outs,
-        compiler_params=params(),
+        + [pl.BlockSpec((LSE_ROWS, size), lambda i: (0, i))]
+        + [any_spec() for _ in shards],
+        out_shape=outs + wholes,
+        scratch_shapes=sems,
+        compiler_params=params(collective_id),
         cost_estimate=cost(2 * total * (width * 1536 + size * Q_WIDTH * 4), x, weight, *outs),
         name="attn_fwd",
-    )(x, segment.reshape(-1, 1), segment.reshape(MICRO, 1, size), live, table, gain, weight)
-
-
-def attn_backward(x, dh, segment, live, table, gain, weight, saved):
-    total, width = x.shape
+    )(x, segment.reshape(-1, 1), segment.reshape(MICRO, 1, size), live, table, gain, weight, *shards)
+
+
+def attn_backward(
+    x, dh, segment, live, table, gain, weight, saved, turned, collective_id=None, sources=()
+):
+    total, width = dh.shape
+    copies, devices = lax.axis_size("rep"), lax.axis_size("fsdp")
+    sums = [shape(g.shape[1:], f32) for g in sources]
+    buffers = []
+    for g in sources:
+        buffers += Reduce.scratch(g.shape[1:], copies, devices // 2)
     size = total // MICRO
     qk, v, a, lse = saved
-    outs = [shape((total, width), f32), shape(weight.shape, bf16), shape((1, width), f32)]
+    outs = [shape(x.shape, f32), shape(weight.shape, bf16), shape((1, width), f32)]
+    x_spec = turned_spec(size, width) if turned else row_spec(size, width)
     return pl.pallas_call(
-        attn_backward_kernel,
+        functools.partial(attn_backward_kernel, len(sources), turned),
         grid=(MICRO,),
         in_specs=[
-            row_spec(size, width),
+            x_spec,
             row_spec(size, width),
             row_spec(size, 1),
             pl.BlockSpec((1, 1, size), lambda i: (i, 0, 0)),
@@ -371,9 +769,11 @@
             row_spec(size, KV_WIDTH),
             row_spec(size, Q_WIDTH),
             pl.BlockSpec((LSE_ROWS, size), lambda i: (0, i)),
-        ],
-        out_specs=[row_spec(size, width), still_spec(weight.shape), still_spec((1, width))],
-        out_shape=outs,
+        ]
+        + [any_spec() for _ in sources],
+        out_specs=[x_spec, whole_spec(weight.shape), still_spec((1, width))]
+        + [whole_spec(o.shape) for o in sums],
+        out_shape=outs + sums,
         scratch_shapes=[
             pltpu.VMEM((width, total), bf16),
             pltpu.VMEM((Q_WIDTH, total), bf16),
@@ -384,34 +784,72 @@
             pltpu.VMEM((LSE_ROWS, size), f32),
             pltpu.VMEM((size, QK_WIDTH), f32),
             pltpu.VMEM((size, KV_WIDTH), f32),
-        ],
-        compiler_params=params(),
+        ]
+        + buffers,
+        compiler_params=params(collective_id),
         cost_estimate=cost(2 * total * (width * 3072 + size * Q_WIDTH * 10), x, dh, weight, *outs),
         name="attn_bwd",
     )(
         x, dh, segment.reshape(-1, 1), segment.reshape(MICRO, 1, size), live, table, gain, weight,
-        qk, v, a, lse,
-    )
-
-
-def ff_forward(h, live, gain, wg, wu, wd):
+        qk, v, a, lse, *sources,
+    )
+
+
+def reduce_kernel(count, *refs):
+    sources, results, buffers = refs[:count], refs[count : 2 * count], refs[2 * count :]
+    place = Place()
+    moves = [
+        Reduce(place, sources[i], results[i], buffers[11 * i : 11 * i + 11]) for i in range(count)
+    ]
+    place.greet()
+    for stage in ("start", "second", "third", "fourth", "finish"):
+        for move in moves:
+            getattr(move, stage)()
+
+
+def reduce_alone(collective_id, *sources):
+    copies, devices = lax.axis_size("rep"), lax.axis_size("fsdp")
+    buffers = []
+    for g in sources:
+        buffers += Reduce.scratch(g.shape[1:], copies, devices // 2)
+    return pl.pallas_call(
+        functools.partial(reduce_kernel, len(sources)),
+        in_specs=[any_spec() for _ in sources],
+        out_specs=[pl.BlockSpec(memory_space=pltpu.VMEM) for _ in sources],
+        out_shape=[shape(g.shape[1:], f32) for g in sources],
+        scratch_shapes=buffers,
+        compiler_params=pltpu.CompilerParams(
+            vmem_limit_bytes=32 * 2**20, collective_id=collective_id, has_side_effects=True
+        ),
+        name="reduce",
+    )(*sources)
+
+
+def ff_forward(h, live, gain, wg, wu, wd, collective_id=None, layer=None, shards=()):
     total, width = h.shape
+    copies, devices = lax.axis_size("rep"), lax.axis_size("fsdp")
+    wholes = [shape((devices,) + w.shape[1:], bf16) for w in shards]
+    sems = []
+    for _ in shards:
+        sems += Gather.semaphores(copies, devices // 2)
     size = tile_of(total)
     out = shape((total, width), f32)
     return pl.pallas_call(
-        ff_forward_kernel,
+        functools.partial(ff_forward_kernel, layer, len(shards), total // size),
         grid=(total // size,),
         in_specs=[row_spec(size, width), row_spec(size, 1), whole_spec(gain.shape)]
-        + [whole_spec(w.shape) for w in (wg, wu, wd)],
-        out_specs=row_spec(size, width),
-        out_shape=out,
-        compiler_params=params(),
+        + [whole_spec(w.shape) for w in (wg, wu, wd)]
+        + [any_spec() for _ in shards],
+        out_specs=[row_spec(size, width)] + [any_spec() for _ in shards],
+        out_shape=[out] + wholes,
+        scratch_shapes=sems,
+        compiler_params=params(collective_id),
         cost_estimate=cost(6 * total * wg.size, h, wg, wu, wd, out),
         name="ff_fwd",
-    )(h, live, gain, wg, wu, wd)
-
-
-def ff_backward(h, dy, live, gain, wg, wu, wd, last):
+    )(h, live, gain, wg, wu, wd, *shards)
+
+
+def ff_backward(h, dy, live, gain, wg, wu, wd, last, collective_id=None, sources=()):
     total, width = h.shape
     ff = wg.shape[1]
     size = tile_of(total)
@@ -422,16 +860,25 @@
         shape(wd.shape, bf16),
         shape((1, width), f32),
     ]
-    specs = [row_spec(size, width)] + [still_spec(o.shape) for o in outs[1:]]
+    copies, devices = lax.axis_size("rep"), lax.axis_size("fsdp")
+    sums = [shape(g.shape[1:], f32) for g in sources]
+    buffers = []
+    for g in sources:
+        buffers += Reduce.scratch(g.shape[1:], copies, devices // 2)
+    outs += sums
+    specs = [row_spec(size, width)] + [whole_spec(o.shape) for o in outs[1:]]
+    dy_spec = row_spec(size, width)
     if last:
-        outs = [shape((total, width), bf16)] + outs
-        specs = [row_spec(size, width)] + specs
+        outs = [shape((width, total), bf16)] + outs
+        dy_spec = turned_spec(size, width)
+        specs = [dy_spec] + specs
     return pl.pallas_call(
-        functools.partial(ff_backward_kernel, last),
+        functools.partial(ff_backward_kernel, last, len(sources), total // size),
         grid=(total // size,),
-        in_specs=[row_spec(size, width), row_spec(size, width), row_spec(size, 1)]
+        in_specs=[row_spec(size, width), dy_spec, row_spec(size, 1)]
         + [whole_spec(gain.shape)]
-        + [whole_spec(w.shape) for w in (wg, wu, wd)],
+        + [whole_spec(w.shape) for w in (wg, wu, wd)]
+        + [any_spec() for _ in sources],
         out_specs=specs,
         out_shape=outs,
         scratch_shapes=[
@@ -440,11 +887,12 @@
             pltpu.VMEM((total, ff), bf16),
             pltpu.VMEM((total, ff), bf16),
             pltpu.VMEM((total, ff), bf16),
-        ],
-        compiler_params=params(),
+        ]
+        + buffers,
+        compiler_params=params(collective_id),
         cost_estimate=cost(16 * total * wg.size, h, dy, wg, wu, wd, *outs),
         name="ff_bwd",
-    )(h, dy, live, gain, wg, wu, wd)
+    )(h, dy, live, gain, wg, wu, wd, *sources)
 
 
 def sum_shards(buffer):
@@ -464,7 +912,10 @@
 
     gains = jnp.concatenate([attn_gain, mlp_gain]).reshape(1, 4 * rows)
     gains = jnp.pad(gains, ((0, 0), (0, QK_WIDTH + Q_WIDTH + KV_WIDTH - 4 * rows)))
-    attn_w, feed_w = [], []
+    shards = (gate_weight, up_weight, down_weight)
+    copies = lax.axis_size("rep")
+    direct = all(can_cut(w.shape[1:], copies) for w in shards)
+    attn_w = []
     for layer in range(DECODER_LAYERS):
         packed = jnp.concatenate(
             [w_query[layer], key_weight[layer], w_out[layer], value_weight[layer]], axis=1
@@ -477,60 +928,84 @@
             attn_w.append(whole[:, :rows].reshape(width, -1))
         else:
             attn_w.append(lax.all_gather(packed, "fsdp", axis=0, tiled=True))
-        packed = jnp.concatenate(
-            [gate_weight[layer], up_weight[layer], down_weight[layer].reshape(rows, ff)]
-        )
-        whole = lax.all_gather(packed, "fsdp", axis=0, tiled=False)
-        feed_w.append(
-            (
-                whole[:, :rows].reshape(width, ff),
-                whole[:, rows : 2 * rows].reshape(width, ff),
-                whole[:, 2 * rows :].reshape(ff, width),
-            )
-        )
-
-    h0, *kept0 = attn_forward(tokens, segment, live, table, all_gains[0], attn_w[0])
-    x1 = ff_forward(h0, live, all_gains[2], *feed_w[0])
-    h1, *kept1 = attn_forward(x1, segment, live, table, all_gains[1], attn_w[1])
+
+    def whole(shard):
+        gathered = lax.all_gather(shard, "fsdp", axis=0, tiled=False)
+        return gathered
+
+    def feed_of(gathered):
+        gate, up, down = gathered
+        return gate.reshape(width, ff), up.reshape(width, ff), down.reshape(ff, width)
+
+    def split(grads):
+        dims = ((rows, ff), (rows, ff), (down_rows, width))
+        return [g.reshape((devices,) + d) for g, d in zip(grads, dims)]
+
+    tokens, cotangent = tokens.T, cotangent.T
+    args0 = (tokens, segment, live, table, all_gains[0], attn_w[0], True)
+    if direct:
+        down1 = whole(down_weight[1])
+        h0, *kept0 = attn_forward(*args0, 0, 0, shards)
+        kept0, feed0 = kept0[:4], feed_of(kept0[4:])
+        x1, gate1 = ff_forward(h0, live, all_gains[2], *feed0, 1, 1, shards[:1])
+    else:
+        h0, *kept0 = attn_forward(*args0)
+        feed0 = feed_of([whole(w[0]) for w in shards])
+        x1 = ff_forward(h0, live, all_gains[2], *feed0)[0]
+    args1 = (x1, segment, live, table, all_gains[1], attn_w[1], False)
+    if direct:
+        h1, *kept1 = attn_forward(*args1, 2, 1, shards[1:2])
+        kept1, feed1 = kept1[:4], feed_of([gate1, kept1[4], down1])
+    else:
+        h1, *kept1 = attn_forward(*args1)
+        feed1 = feed_of([whole(w[1]) for w in shards])
     out_tokens, dh1, gg1, gu1, gd1, mg1 = ff_backward(
-        h1, cotangent, live, all_gains[3], *feed_w[1], True
-    )
-    feed1 = sum_shards(
-        jnp.concatenate(
-            [g.reshape(devices, rows, ff) for g in (gg1, gu1, gd1)], axis=1
-        )
-    )
-    dx1, ga1, ag1 = attn_backward(x1, dh1, segment, live, table, all_gains[1], attn_w[1], kept1)
-    dh0, gg0, gu0, gd0, mg0 = ff_backward(h0, dx1, live, all_gains[2], *feed_w[0], False)
-    feed0 = sum_shards(
-        jnp.concatenate(
-            [g.reshape(devices, rows, ff) for g in (gg0, gu0, gd0)], axis=1
-        )
-    )
-    dx0, ga0, ag0 = attn_backward(
-        tokens, dh0, segment, live, table, all_gains[0], attn_w[0], kept0
-    )
-    zero = jnp.zeros((devices, 1, ff - 4 * rows), bf16)
+        h1, cotangent, live, all_gains[3], *feed1, True
+    )
+    grads1 = split((gg1, gu1, gd1))
+    args1 = (x1, dh1, segment, live, table, all_gains[1], attn_w[1], kept1, False)
+    if direct:
+        dx1, ga1, ag1, *sums1 = attn_backward(*args1, 3, grads1[:2])
+    else:
+        dx1, ga1, ag1 = attn_backward(*args1)
+    ga1 = ga1.reshape(devices, rows, ff)
+    args0 = (h0, dx1, live, all_gains[2], *feed0, False)
+    if direct:
+        dh0, gg0, gu0, gd0, mg0, down1, attn1 = ff_backward(*args0, 4, (grads1[2], ga1))
+        sums1.append(down1)
+    else:
+        sums1, attn1 = [sum_shards(g) for g in grads1], sum_shards(ga1)
+        dh0, gg0, gu0, gd0, mg0 = ff_backward(*args0)
+    grads0 = split((gg0, gu0, gd0))
+    args0 = (tokens, dh0, segment, live, table, all_gains[0], attn_w[0], kept0, True)
+    if direct:
+        dx0, ga0, ag0, *sums0 = attn_backward(*args0, 5, grads0)
+    else:
+        dx0, ga0, ag0 = attn_backward(*args0)
+        sums0 = [sum_shards(g) for g in grads0]
+    ga0 = ga0.reshape(devices, rows, ff)
+    room = 512 * -(-4 * rows // 512)
     gain_grads = jnp.concatenate(
-        [g.reshape(devices, 1, rows).astype(bf16) for g in (ag0, ag1, mg0, mg1)] + [zero], axis=2
-    )
-    attn1 = sum_shards(ga1.reshape(devices, rows, ff))
-    attn0 = sum_shards(jnp.concatenate([ga0.reshape(devices, rows, ff), gain_grads], axis=1))
-    last = attn0[rows]
-    attn = jnp.stack([attn0[:rows], attn1])
-    feed = jnp.stack([feed0, feed1])
+        [g.reshape(devices, 1, rows).astype(bf16) for g in (ag0, ag1, mg0, mg1)], axis=2
+    )
+    gain_grads = jnp.pad(gain_grads, ((0, 0), (0, 15), (0, room - 4 * rows)))
+    if direct:
+        attn0, last = reduce_alone(6, ga0, gain_grads)
+    else:
+        attn0, last = sum_shards(ga0), sum_shards(gain_grads)
+    last = last[0]
+    attn = jnp.stack([attn0, attn1])
+    feed = [jnp.stack(pair) for pair in zip(sums0, sums1)]
     return (
-        out_tokens,
-        dx0,
+        out_tokens.T,
+        dx0.T,
         last[: 2 * rows].reshape(2, rows),
         attn[:, :, :Q_WIDTH],
         attn[:, :, Q_WIDTH:QK_WIDTH],
         attn[:, :, QK_WIDTH + Q_WIDTH :],
         attn[:, :, QK_WIDTH : QK_WIDTH + Q_WIDTH],
         last[2 * rows : 4 * rows].reshape(2, rows),
-        feed[:, :rows],
-        feed[:, rows : 2 * rows],
-        feed[:, 2 * rows :].reshape(2, down_rows, width),
+        *feed,
     )
 
 

time: 610 us -> 405 us (0.66)
  waiting for transfers between devices: 292 us -> 18.9 us
  Pallas kernels: 214 us -> 334 us
  local copies, waits for them, and re-layouts: 58.3 us -> 20.9 us
  other arithmetic: 24.7 us -> 12.3 us
    reduce_scatter x4 -> x0, waiting for transfers between devices: 141 us -> none  [sum_shards(): shard = lax.psum_scatter(buffer, 'fsdp', scatter_dimension=0, tiled=False)]
    pallas_call x7 -> x8, Pallas kernels: 214 us -> 334 us  [the longest x2 110 us: attn_backward(): pl.pallas_call(functools.partial(attn_backward_kernel, len(sources), turn...]
    all_gather x3 -> x1, waiting for transfers between devices: 89.6 us -> 18.8 us  [local(): whole = lax.all_gather(packed, 'fsdp', axis=0, tiled=False)]
    psum x1 -> x0, waiting for transfers between devices: 60 us -> none  [sum_shards(): return lax.psum(shard, 'rep').astype(f32)]
    reshape x5 -> x0, local copies, waits for them, and re-layouts: 18.1 us -> none  [the longest x2 8.65 us: local(): g.reshape(devices, rows, ff)]
    concatenate x5 -> x1, other arithmetic: 13.2 us -> 0.11 us  [local(): jnp.concatenate([g.reshape(devices, 1, rows).astype(bf16) for g in (ag0,...]
    slice x4 -> x1, local copies, waits for them, and re-layouts: 10.9 us -> 0.72 us  [local(): down1 = whole(down_weight[1])]
    unnamed x32 -> x29, local copies, waits for them, and re-layouts: 12.3 us -> 4 us
  transfers between devices with their start and end apart: 9 -> 3, of which waited for: 8 -> 1; matrix products, arithmetic and copies ran while one was open for 12% -> 5% of each run, Pallas kernels for 19% -> 26%
where the time goes in v2:
time: 405 us; the launch traced here: 400 us
  Pallas kernels  334 us (82%)
  local copies, waits for them, and re-layouts  20.9 us (5%)
  waiting for transfers between devices  18.9 us (5%)
  between operations  14.2 us (4%)
  other arithmetic  12.3 us (3%)
    pallas_call x2, Pallas kernels, attn_backward(): pl.pallas_call(functools.partial(attn_backward_kernel, len(sources), turn...  110 us
    pallas_call x2, Pallas kernels, ff_backward(): pl.pallas_call(functools.partial(ff_backward_kernel, last, len(sources),...  91.5 us
    pallas_call x2, Pallas kernels, attn_forward(): pl.pallas_call(functools.partial(attn_forward_kernel, layer, len(shards),...  77.8 us
    pallas_call x1, Pallas kernels, ff_forward(): pl.pallas_call(functools.partial(ff_forward_kernel, layer, len(shards), t...  28.1 us
    pallas_call x1, Pallas kernels, reduce_alone(): pl.pallas_call(functools.partial(reduce_kernel, len(sources)), in_specs=[...  26.2 us
    all_gather x1, waiting for transfers between devices, local(): whole = lax.all_gather(packed, 'fsdp', axis=0, tiled=False)  18.8 us
  transfers between devices with their start and end apart: 3, of which 1 were waited for; matrix products, arithmetic and copies ran while one was open for 5% of the time, Pallas kernels for 26%

profile of v2, /device:TPU:0, one launch (start us, length us, event | category | flops | bytes accessed | tf_op | source)
XLA Modules:
  0.0 400.2 jit_solution(9242548791415540262)
XLA Ops:
  7.2 0.7 pad_maximum_fusion.4
  8.1 0.8 slice_bitcast_fusion.4
  8.9 1.1 slice_bitcast_fusion
  10.1 0.7 fusion.9
  10.9 0.8 concatenate.22
  11.7 0.7 slice.89
  13.3 1.1 reshape.223.column_ref
  14.5 1.4 select_reduce_fusion
  15.9 1.1 broadcast_in_dim.29.live_ref
  17.1 2.8 multiply_sine_fusion
  19.9 3.0 concatenate.18.table_ref
  22.9 18.8 %all-gather.10.cloned.1.call-done = bf16[8,73,1536]{2,1,0:T(8,128)(2,1)} async-done(((bf16[1,73,1536]{2,1,0:T(8,128)(2,1)}), bf16[8,73,1536]{2,1,0:T(8,128)(2,1)}) %all-gather.10.cloned.1.call-update) | async-done | bytes 1794064 | tf_op jit(solution)/shard_map/all_gather | solution.py:925
  41.7 0.8 fusion.19
  43.3 0.7 squeeze.46.gain_ref
  45.3 2.9 slice.98
  48.2 46.4 %attn_fwd.2 = (f32[1536,576]{1,0:T(8,128)}, bf16[1536,768]{1,0:T(8,128)(2,1)}, bf16[1536,192]{1,0:T(8,128)(2,1)}, bf16[1536,576]{1,0:T(8,128)(2,1)}, f32[16,1536...) custom-call(bf16[576,1536]{1,0:T(8,128)(2,1)} %bitcast.65, ...), custom_call_target="tpu_custom_call" | custom-call | flops 8153726976 | bytes 11894784 | tf_op jit(solution)/shard_map/attn_fwd/pallas_call | solution.py:719
  94.6 28.1 %ff_fwd.1 = (f32[1536,576]{1,0:T(8,128)}, bf16[8,72,1536]{2,1,0:T(8,128)(2,1)}) custom-call(f32[1536,576]{1,0:T(8,128)} %get-tuple-element.53.h_ref, f32[1536,1]{1,0:T(8,128)} %broadcast_in_dim.29.live_ref, f32[1,576]{1,0:T(1,128)} %squeeze.45.gain_ref, bf16[576,1536]{1,0:T(8,128)(2,1)} %bitcast.72, bf16[576,1536]{1,0:T(8,128)(2,1)} %bitcast.74, ...), custom_call_target="tpu_custom_call" | custom-call | flops 8153726976 | bytes 12386304 | tf_op jit(solution)/shard_map/ff_fwd/pallas_call | solution.py:837
  122.7 31.4 %attn_fwd.3 = (f32[1536,576]{1,0:T(8,128)}, bf16[1536,768]{1,0:T(8,128)(2,1)}, bf16[1536,192]{1,0:T(8,128)(2,1)}, bf16[1536,576]{1,0:T(8,128)(2,1)}, f32[16,1536]{1,0:T(8,128)}, /*index=5*/bf16[8,72,1536]{2,1,0:T(8,128)(2,1)}) custom-call(f32[1536,576]{1,0:T(8,128)} %get-tuple-element.57.x_ref, s32[1536,1]{1,0:T(8,128)} %reshape.223.column_ref, ...), custom_call_target="tpu_custom_call" | custom-call | flops 8153726976 | bytes 13664256 | tf_op jit(solution)/shard_map/attn_fwd/pallas_call | solution.py:719
  154.2 40.4 %ff_bwd.2 = (bf16[576,1536]{1,0:T(8,128)(2,1)}, f32[1536,576]{1,0:T(8,128)}, bf16[576,1536]{1,0:T(8,128)(2,1)}, bf16[576,1536]{1,0:T(8,128)(2,1)}, bf16[1536,576]{1,0:T(8,128)(2,1)}, /*index=5*/f32[1,576]{1,0:T(1,128)}) custom-call(f32[1536,576]{1,0:T(8,128)} %get-tuple-element.58.h_ref, bf16[576,1536]{1,0:T(8,128)(2,1)} %bitcast.64, ...), custom_call_target="tpu_custom_call" | custom-call | flops 21743271936 | bytes 21235968 | tf_op jit(solution)/shard_map/ff_bwd/pallas_call | solution.py:875
  194.5 50.5 %attn_bwd.2 = (f32[1536,576]{1,0:T(8,128)}, bf16[576,1536]{1,0:T(8,128)(2,1)}, f32[1,576]{1,0:T(1,128)}, f32[72,1536]{1,0:T(8,128)}, f32[72,1536]{1,0:T(8,128)}) custom-call(f32[1536,576]{1,0:T(8,128)} %get-tuple-element.57.x_ref, f32[1536,576]{1,0:T(8,128)} %get-tuple-element.62.dh_ref, s32[1536,1]{1,0:T(8,128)} %reshape.223.column_ref, ...), custom_call_target="tpu_custom_call" | custom-call | flops 19025362944 | bytes 14158080 | tf_op jit(solution)/shard_map/attn_bwd/pallas_call | solution.py:756
  245.0 51.1 %ff_bwd.3 = (f32[1536,576]{1,0:T(8,128)}, bf16[576,1536]{1,0:T(8,128)(2,1)}, bf16[576,1536]{1,0:T(8,128)(2,1)}, bf16[1536,576]{1,0:T(8,128)(2,1)}, f32[1,576]{1,...) custom-call(f32[1536,576]{1,0:T(8,128)} %get-tuple-element.53.h_ref, f32[1536,576]{1,0:T(8,128)} %get-tuple-element.69.dy_ref, ...), custom_call_target="tpu_custom_call" | custom-call | flops 21743271936 | bytes 22120704 | tf_op jit(solution)/shard_map/ff_bwd/pallas_call | solution.py:875
  296.2 59.7 %attn_bwd.3 = (f32[576,1536]{1,0:T(8,128)}, bf16[576,1536]{1,0:T(8,128)(2,1)}, f32[1,576]{1,0:T(1,128)}, f32[72,1536]{1,0:T(8,128)}, f32[72,1536]{1,0:T(8,128)}, /*index=5*/f32[192,576]{1,0:T(8,128)}) custom-call(bf16[576,1536]{1,0:T(8,128)(2,1)} %bitcast.66, f32[1536,576]{1,0:T(8,128)} %get-tuple-element.72.dh_ref, s32[1536,1]{1,0:T(8,128)} %reshape.223.column_ref, ...), custom_call_target="tpu_custom_call" | custom-call | flops 19025362944 | bytes 12388608 | tf_op jit(solution)/shard_map/attn_bwd/pallas_call | solution.py:756
  355.9 0.7 convert_reduce_fusion.3
  357.2 1.5 copy-done
  358.7 26.2 %reduce.19 = (f32[72,1536]{1,0:T(8,128)S(1)}, f32[16,512]{1,0:T(8,128)S(1)}) custom-call(bf16[8,72,1536]{2,1,0:T(8,128)(2,1)S(1)} %bitcast.50, bf16[8,16,512]{2,1,0:T(8,128)(2,1)S(1)} %fusion.15.refs_1_), custom_call_target="tpu_custom_call" | custom-call | tf_op jit(solution)/shard_map/reduce/pallas_call | solution.py:815
  384.9 0.9 fusion.10
  385.8 0.9 pad_maximum_fusion.3
  388.0 1.0 pad_maximum_fusion.1
  389.0 1.0 pad_maximum_fusion.2
  390.0 1.0 pad_maximum_fusion
  391.0 0.7 copy-done.1
  391.7 1.8 copy.92
  (60 shorter events, 5.3 us)
Async XLA Ops:
  7.2 4.6 %copy-start.10 = (bf16[2,192,576]{2,1,0:T(8,128)(2,1)S(1)}, bf16[2,192,576]{2,1,0:T(8,128)(2,1)}, u32[]{:S(2)}) copy-start(bf16[2,192,576]{2,1,0:T(8,128)(2,1)} %rest_2_.1) | copy-start | bytes 1327108
  7.2 5.3 %copy-start.9 = (s32[1536]{0:T(1024)S(1)}, s32[1536]{0:T(1024)}, u32[]{:S(2)}) copy-start(s32[1536]{0:T(1024)} %param.13) | copy-start | bytes 18436
  7.2 34.5 %all-gather.10.cloned.1.call-start = ((), (), s32[]{:S(2)}) async-start(), calls=%async_computation.2 | async-start | bytes 2211840 | tf_op jit(solution)/shard_map/all_gather | solution.py:925
  10.8 111.9 %all-gather.6.cloned.1.call-start = ((), (), s32[]{:S(2)}) async-start(), calls=%async_computation | async-start | bytes 1990656 | tf_op jit(solution)/shard_map/all_gather | solution.py:930
  11.7 142.5 %all-gather.8.cloned.1.call-start = ((), (), s32[]{:S(2)}) async-start(), calls=%async_computation.1 | async-start | bytes 2211840 | tf_op jit(solution)/shard_map/all_gather | solution.py:933
  296.2 60.6 %copy-start.13 = (f32[1,576]{1,0:T(1,128)S(1)}, f32[1,576]{1,0:T(1,128)}, u32[]{:S(2)}) copy-start(f32[1,576]{1,0:T(1,128)} %get-tuple-element.84) | copy-start | bytes 6916
  296.2 60.7 %copy-start.12 = (f32[1,576]{1,0:T(1,128)S(1)}, f32[1,576]{1,0:T(1,128)}, u32[]{:S(2)}) copy-start(f32[1,576]{1,0:T(1,128)} %get-tuple-element.83) | copy-start | bytes 6916
  296.2 60.8 %copy-start.11 = (f32[1,576]{1,0:T(1,128)S(1)}, f32[1,576]{1,0:T(1,128)}, u32[]{:S(2)}) copy-start(f32[1,576]{1,0:T(1,128)} %get-tuple-element.85) | copy-start | bytes 6916
  296.2 88.7 %copy-start.2 = (f32[72,1536]{1,0:T(8,128)S(1)}, f32[72,1536]{1,0:T(8,128)}, u32[]{:S(2)}) copy-start(f32[72,1536]{1,0:T(8,128)} %get-tuple-element.88) | copy-start | bytes 1327108
  357.2 1.5 copy-start
  358.7 29.4 %copy-start.6 = (f32[72,1536]{1,0:T(8,128)S(1)}, f32[72,1536]{1,0:T(8,128)}, u32[]{:S(2)}) copy-start(f32[72,1536]{1,0:T(8,128)} %get-tuple-element.90) | copy-start | bytes 1327108
  358.7 29.4 %copy-start.8 = (f32[72,1536]{1,0:T(8,128)S(1)}, f32[72,1536]{1,0:T(8,128)}, u32[]{:S(2)}) copy-start(f32[72,1536]{1,0:T(8,128)} %get-tuple-element.89) | copy-start | bytes 1327108
  385.7 3.3 copy-start.5
  385.7 3.3 copy-start.7
  386.7 3.3 copy-start.3
  386.7 3.3 copy-start.4
  389.0 2.7 copy-start.1
Sparse Core Ops, SparseCore 0:
  10.9 30.7 all-gather.9
  43.9 40.2 all-gather.5
  86.4 32.8 all-gather.7

commit v3 on v2

--- a/solution.py
+++ b/solution.py
@@ -38,21 +38,6 @@
     return lax.dot_general(left, right, (((0,), (0,)), ((), ())), preferred_element_type=f32)
 
 
-def geometry(segment):
-    size = segment.shape[0] // MICRO
-    seg = segment.reshape(MICRO, size)
-    index = jnp.arange(size, dtype=jnp.int32)
-    same = seg[:, :, None] == seg[:, None, :]
-    earlier = index[None, :] < index[:, None]
-    position = jnp.sum(jnp.where(same & earlier, 1, 0).astype(jnp.int32), axis=-1)
-    frequency = rope_base ** (-2.0 * jnp.arange(HEAD_WIDTH // 2, dtype=f32) / HEAD_WIDTH)
-    angles = position.reshape(-1).astype(f32)[:, None] * frequency
-    cosine, sine = jnp.cos(angles), jnp.sin(angles)
-    table = jnp.concatenate([cosine] * 4 + [-sine, sine] * 2, axis=1)
-    live = jnp.where(segment >= 0, 1.0, 0.0).astype(f32)[:, None]
-    return live, table
-
-
 def swap_halves(rows):
     lane = lax.broadcasted_iota(jnp.int32, rows.shape, 1)
     first = (lane % HEAD_WIDTH) < HEAD_WIDTH // 2
@@ -173,10 +158,9 @@
 
 
 class Gather:
-    def __init__(self, place, layer, shard, whole, sems):
-        self.p, self.layer, self.shard, self.whole = place, layer, shard, whole
-        self.sems = sems
-        self.dims = shard.shape[1:]
+    def __init__(self, place, shard, whole, sems):
+        self.p, self.shard, self.whole, self.sems = place, shard, whole, sems
+        self.dims = whole.shape[1:]
         self.parts = place.copies
 
     @staticmethod
@@ -191,22 +175,20 @@
     def own(self):
         p = self.p
         return pltpu.make_async_copy(
-            self.shard.at[self.layer], self.whole.at[2 * p.z + p.c], self.sems[3]
+            self.shard[0].at[self.shard[1]], self.whole.at[2 * p.z + p.c], self.sems[3]
         )
 
     def along(self, k):
         p = self.p
         return remote(
-            piece(self.shard, self.layer, self.dims, self.parts, p.r),
+            piece(self.shard[0], self.shard[1], self.dims, self.parts, p.r),
             piece(self.whole, 2 * p.z + p.c, self.dims, self.parts, p.r),
             self.sems[0].at[0, k], self.sems[0].at[1, k], p.at(p.r, p.chip(k), p.c),
         )
 
     def across(self, k, j):
         p = self.p
-        block = piece(
-            self.whole, 2 * p.chip(p.line - k) + p.c, self.dims, self.parts, p.r
-        )
+        block = piece(self.whole, 2 * p.chip(p.line - k) + p.c, self.dims, self.parts, p.r)
         return remote(
             block, block, self.sems[1].at[0, k, j], self.sems[1].at[1, k, j],
             p.at(p.replica(j), p.z, p.c),
@@ -214,44 +196,67 @@
 
     def pair(self, k):
         p = self.p
-        index = 2 * p.chip(p.line - k) + p.c
-        source = self.shard.at[self.layer] if k == 0 else self.whole.at[index]
-        return remote(
-            source, self.whole.at[index], self.sems[2].at[0, k], self.sems[2].at[1, k], p.partner()
-        )
-
-    def start(self):
+        block = self.whole.at[2 * p.chip(p.line - k) + p.c]
+        return remote(block, block, self.sems[2].at[0, k], self.sems[2].at[1, k], p.partner())
+
+    def others(self):
+        return [(k, j) for k in range(1, self.p.line) for j in range(1, self.p.copies)]
+
+    def line_start(self):
         for k in range(1, self.p.line):
             self.along(k).start()
         self.own().start()
-        self.pair(0).start()
-
-    def second(self):
+
+    def line_end(self):
         for k in range(1, self.p.line):
             self.along(k).wait_recv()
-            for j in range(1, self.p.copies):
-                self.across(k, j).start()
-
-    def third(self):
+
+    def across_start(self):
+        for k, j in self.others():
+            self.across(k, j).start()
+
+    def across_end(self):
+        for k, j in self.others():
+            self.across(k, j).wait_recv()
+
+    def pair_start(self):
+        for k in range(self.p.line):
+            self.pair(k).start()
+
+    def line_done(self):
+        self.own().wait()
         for k in range(1, self.p.line):
-            for j in range(1, self.p.copies):
-                self.across(k, j).wait_recv()
-            self.pair(k).start()
-
-    def finish(self):
-        self.own().wait()
+            self.along(k).wait_send()
+
+    def across_done(self):
+        for k, j in self.others():
+            self.across(k, j).wait_send()
+
+    def pair_done(self):
         for k in range(self.p.line):
             self.pair(k).wait()
-            if k:
-                self.along(k).wait_send()
-                for j in range(1, self.p.copies):
-                    self.across(k, j).wait_send()
+
+
+def gathers(place, shards, wholes, sems):
+    return [
+        Gather(place, shards[i] if shards else None, wholes[i], sems[4 * i : 4 * i + 4])
+        for i in range(len(wholes))
+    ]
+
+
+def gather_semaphores(count):
+    copies, devices = lax.axis_size("rep"), lax.axis_size("fsdp")
+    sems = []
+    for _ in range(count):
+        sems += Gather.semaphores(copies, devices // 2)
+    return sems
 
 
 class Reduce:
-    def __init__(self, place, source, out, buffers):
-        self.p, self.source, self.out = place, source, out
-        self.dims = source.shape[1:]
+    def __init__(self, place, source, out, buffers, first=0, width=None):
+        self.p, self.out, self.first = place, out, first
+        self.source = source
+        self.dims = (source.shape[1], width or source.shape[2])
         self.parts = place.copies
         (self.mine, self.theirs, self.across_in, self.line_out, self.line_in, self.final,
          self.s0, self.s1, self.s2, self.s3, self.s4) = buffers
@@ -273,16 +278,21 @@
             pltpu.SemaphoreType.DMA((2, copies)),
         ]
 
+    def shard(self, index):
+        if self.dims[1] == self.source.shape[2]:
+            return self.source.at[index]
+        return self.source.at[index, :, pl.ds(self.first, self.dims[1])]
+
     def pair(self, z):
         p = self.p
         return remote(
-            self.source.at[2 * z + 1 - p.c], self.theirs.at[z],
+            self.shard(2 * z + 1 - p.c), self.theirs.at[z],
             self.s0.at[0, z], self.s0.at[1, z], p.partner(),
         )
 
     def load(self, z):
         return pltpu.make_async_copy(
-            self.source.at[2 * z + self.p.c], self.mine.at[z], self.s1.at[z]
+            self.shard(2 * z + self.p.c), self.mine.at[z], self.s1.at[z]
         )
 
     def across(self, j, z):
@@ -339,21 +349,112 @@
             self.spread(j).start()
 
     def finish(self):
-        for j in range(1, self.p.copies):
-            self.spread(j).wait()
-        axis, size = part_of(self.dims, self.parts)
-        for index in range(self.parts):
-            here = slice(index * size, (index + 1) * size)
-            if axis == 1:
-                self.out[:, here] = self.final[index].astype(f32)
-            else:
-                self.out[here, :] = self.final[index].astype(f32)
+        self.write()
         for z in range(self.p.line):
             self.pair(z).wait_send()
             for j in range(1, self.p.copies):
                 self.across(j, z).wait_send()
         for k in range(1, self.p.line):
             self.along(k).wait_send()
+
+    def write(self):
+        for j in range(1, self.p.copies):
+            self.spread(j).wait()
+        axis, size = part_of(self.dims, self.parts)
+        for index in range(self.parts):
+            here = index * size
+            if axis == 1:
+                here += self.first
+                self.out[:, here : here + size] = self.final[index].astype(f32)
+            else:
+                self.out[here : here + size, :] = self.final[index].astype(f32)
+
+
+class LineReduce(Reduce):
+    @staticmethod
+    def scratch(dims, copies, line):
+        small = piece_dims(dims, copies)
+        return [
+            pltpu.VMEM((line,) + tuple(dims), bf16),
+            pltpu.VMEM((line,) + tuple(dims), bf16),
+            pltpu.VMEM((copies,) + small, bf16),
+            pltpu.VMEM((1,) + tuple(dims), bf16),
+            pltpu.VMEM((line,) + tuple(dims), bf16),
+            pltpu.VMEM((copies,) + small, bf16),
+            pltpu.SemaphoreType.DMA((2, line)),
+            pltpu.SemaphoreType.DMA((line,)),
+            pltpu.SemaphoreType.DMA((2, copies)),
+            pltpu.SemaphoreType.DMA((2, line)),
+            pltpu.SemaphoreType.DMA((2, copies)),
+        ]
+
+    def along(self, k):
+        p = self.p
+        return remote(
+            self.mine.at[p.chip(k)], self.line_in.at[k],
+            self.s3.at[0, k], self.s3.at[1, k], p.at(p.r, p.chip(k), p.c),
+        )
+
+    def across(self, j):
+        p = self.p
+        return remote(
+            piece(self.line_out, 0, self.dims, self.parts, p.replica(j)), self.across_in.at[j],
+            self.s2.at[0, j], self.s2.at[1, j], p.at(p.replica(j), p.z, p.c),
+        )
+
+    def second(self):
+        for z in range(self.p.line):
+            self.load(z).wait()
+            self.pair(z).wait_recv()
+            self.mine[z] = (self.mine[z].astype(f32) + self.theirs[z].astype(f32)).astype(bf16)
+        for k in range(1, self.p.line):
+            self.along(k).start()
+
+    def third(self):
+        total = self.mine[self.p.z].astype(f32)
+        for k in range(1, self.p.line):
+            self.along(k).wait_recv()
+            total += self.line_in[k].astype(f32)
+        self.line_out[0] = total.astype(bf16)
+        for j in range(1, self.p.copies):
+            self.across(j).start()
+
+    def fourth(self):
+        total = piece(self.line_out, 0, self.dims, self.parts, self.p.r)[...].astype(f32)
+        for j in range(1, self.p.copies):
+            self.across(j).wait_recv()
+            total += self.across_in[j].astype(f32)
+        self.final[self.p.r] = total.astype(bf16)
+        for j in range(1, self.p.copies):
+            self.spread(j).start()
+
+    def finish(self):
+        self.write()
+        for z in range(self.p.line):
+            self.pair(z).wait_send()
+        for k in range(1, self.p.line):
+            self.along(k).wait_send()
+        for j in range(1, self.p.copies):
+            self.across(j).wait_send()
+
+
+def kinds_of(count):
+    return [Reduce, Reduce, LineReduce][:count]
+
+
+def reduce_buffers(sources):
+    copies, devices = lax.axis_size("rep"), lax.axis_size("fsdp")
+    buffers = []
+    for kind, g in zip(kinds_of(len(sources)), sources):
+        buffers += kind.scratch(g.shape[1:], copies, devices // 2)
+    return buffers
+
+
+def reduces(place, sources, results, buffers):
+    return [
+        kind(place, sources[i], results[i], buffers[11 * i : 11 * i + 11])
+        for i, kind in enumerate(kinds_of(len(sources)))
+    ]
 
 
 class Plan:
@@ -373,38 +474,111 @@
                         act()
 
 
+def feed_line(plan, points, moves):
+    gate, up, down = moves
+    (one, two), last = points[0], points[1]
+    plan.put(one, two, gate.line_end, gate.across_start)
+    plan.put(*last, up.line_end, down.line_end, gate.across_end, gate.across_done)
+    plan.put(*last, *[move.line_done for move in moves])
+
+
+def prepare_kernel(counts, column_ref, row_ref, frequency_ref, *refs):
+    attn_count, feed_count = counts
+    total = attn_count + feed_count
+    shards, refs = refs[:total], refs[total:]
+    live_ref, table_ref, *refs = refs
+    wholes, sems = refs[:total], refs[total:]
+    if total:
+        place = Place()
+        moves = gathers(place, [(ref, 0) for ref in shards], wholes, sems)
+        first, feed = moves[:attn_count], moves[attn_count:]
+        place.greet()
+        for move in moves:
+            move.line_start()
+    size = row_ref.shape[2]
+    live_ref[...] = jnp.where(column_ref[...] >= 0, 1.0, 0.0).astype(f32)
+    key = lax.broadcasted_iota(jnp.int32, (size, size), 1)
+    query = lax.broadcasted_iota(jnp.int32, (size, size), 0)
+    positions = []
+    for block in range(MICRO):
+        same = column_ref[block * size : (block + 1) * size, :] == row_ref[block]
+        earlier = jnp.where(same & (key < query), 1.0, 0.0)
+        positions.append(jnp.sum(earlier, axis=1, keepdims=True))
+    if total:
+        for move in first:
+            move.line_end()
+            move.across_start()
+    lane = lax.broadcasted_iota(jnp.int32, (size, 128), 1)
+    sign = jnp.where(lane % HEAD_WIDTH < HEAD_WIDTH // 2, -1.0, 1.0)
+    for block in range(MICRO):
+        angles = positions[block] * frequency_ref[...]
+        here = slice(block * size, (block + 1) * size)
+        table_ref[here, :128] = jnp.cos(angles)
+        table_ref[here, 128:] = jnp.sin(angles) * sign
+    if total:
+        gate = feed[0]
+        gate.line_end()
+        gate.across_start()
+        for move in first:
+            move.across_end()
+            move.own().wait()
+            move.pair_start()
+        for move in feed[1:]:
+            move.line_end()
+        gate.across_end()
+        gate.across_done()
+        for move in feed:
+            move.line_done()
+        for move in first:
+            for k in range(1, place.line):
+                move.along(k).wait_send()
+            move.across_done()
+            move.pair_done()
+
+
+def prepare(segment, shards=(), feed=(), collective_id=None):
+    rows = segment.shape[0]
+    size = rows // MICRO
+    devices = lax.axis_size("fsdp")
+    frequency = rope_base ** (-2.0 * jnp.arange(HEAD_WIDTH // 2, dtype=f32) / HEAD_WIDTH)
+    frequency = jnp.concatenate([frequency] * 4)[None]
+    everything = tuple(shards) + tuple(feed)
+    wholes = [shape((devices,) + w.shape[1:], bf16) for w in everything]
+    vmem = pl.BlockSpec(memory_space=pltpu.VMEM)
+    extra = {}
+    if everything:
+        extra = {"collective_id": collective_id, "has_side_effects": True}
+    return pl.pallas_call(
+        functools.partial(prepare_kernel, (len(shards), len(feed))),
+        in_specs=[vmem] * 3 + [any_spec() for _ in everything],
+        out_specs=[vmem] * 2 + [any_spec() for _ in everything],
+        out_shape=[shape((rows, 1), f32), shape((rows, 256), f32)] + wholes,
+        scratch_shapes=gather_semaphores(len(everything)),
+        compiler_params=pltpu.CompilerParams(vmem_limit_bytes=62 * 2**20, **extra),
+        name="prepare",
+    )(segment.reshape(-1, 1), segment.reshape(MICRO, 1, size), frequency, *everything)
+
+
 def attn_forward_kernel(
-    layer, count, turned, x_ref, column_ref, row_ref, live_ref, table_ref, gain_ref, weight_ref,
+    row, count, turned, x_ref, column_ref, row_ref, live_ref, table_ref, gain_ref, weight_ref,
     *rest
 ):
-    shards, rest = rest[:count], rest[count:]
-    h_ref, qk_ref, v_ref, a_ref, lse_ref, *rest = rest
+    h_ref, qk_ref, v_ref, a_ref, lse_ref, *rest = rest[count:]
     wholes, sems = rest[:count], rest[count:]
     plan = Plan(pl.program_id(0), MICRO)
     if count:
         place = Place()
-        moves = [
-            Gather(place, layer, shards[i], wholes[i], sems[4 * i : 4 * i + 4])
-            for i in range(count)
-        ]
-        plan.put(0, "start", place.greet, *[move.start for move in moves])
-        if count == 1:
-            plan.put(0, 6, moves[0].second)
-            plan.put(1, 6, moves[0].third)
-        else:
-            one, two, three = moves
-            plan.put(0, 4, one.second)
-            plan.put(0, "end", two.second)
-            plan.put(1, 2, one.third)
-            plan.put(1, 3, three.second)
-            plan.put(1, 7, two.third)
-            plan.put(1, "end", three.third)
-        plan.put(1, "end", *[move.finish for move in moves])
+        gate, up, down = gathers(place, (), wholes, sems)
+        plan.put(0, "start", place.greet, up.across_start, down.across_start, gate.pair_start)
+        plan.put(0, "end", up.across_end, up.pair_start)
+        plan.put(1, 6, down.across_end, down.pair_start)
+        plan.put(1, "end", gate.pair_done, up.across_done, up.pair_done)
+        plan.put(1, "end", down.across_done, down.pair_done)
     plan.run("start")
     x = (x_ref[...].T if turned else x_ref[...]).astype(f32)
     rows = x.shape[0]
     h_ref[...] = x
-    normed = (x * norm(x) * gain_ref[...]).astype(bf16)
+    normed = (x * norm(x) * gain_ref[row : row + 1, :]).astype(bf16)
     qk = nn(normed, weight_ref[:, :QK_WIDTH])
     v_ref[...] = nn(normed, weight_ref[:, QK_WIDTH + Q_WIDTH :]).astype(bf16)
     qk = rotate(qk, table_ref[:, :128], table_ref[:, 128:]).astype(bf16)
@@ -442,7 +616,7 @@
 
 
 def attn_backward_kernel(
-    count, turned, x_ref, dh_ref, column_ref, row_ref, live_ref, table_ref, gain_ref, weight_ref,
+    row, count, turned, x_ref, dh_ref, column_ref, row_ref, live_ref, table_ref, gain_ref, weight_ref,
     qk_ref, v_ref, a_ref, lse_ref, *rest
 ):
     sources, rest = rest[:count], rest[count:]
@@ -454,21 +628,19 @@
     plan = Plan(step, MICRO)
     if count:
         place = Place()
-        moves = [
-            Reduce(place, sources[i], results[i], buffers[11 * i : 11 * i + 11])
-            for i in range(count)
-        ]
+        moves = reduces(place, sources, results, buffers)
         plan.put(0, "start", place.greet, *[move.start for move in moves])
         one, two = moves[:2]
         plan.put(0, 0, one.second, two.second)
-        plan.put(0, 6, one.third)
-        plan.put(1, 0, one.fourth)
-        plan.put(1, 1, two.third)
-        plan.put(1, 4, two.fourth)
+        plan.put(0, 8, one.third)
+        plan.put(1, 2, two.third)
         if count == 3:
-            plan.put(0, 1, moves[2].second)
-            plan.put(1, 8, moves[2].third)
-            plan.put(1, "end", moves[2].fourth)
+            plan.put(0, 0, moves[2].second)
+            plan.put(1, 3, moves[2].third, one.fourth)
+            plan.put(1, 6, moves[2].fourth)
+        else:
+            plan.put(1, 1, one.fourth)
+        plan.put(1, "grads", two.fourth)
         plan.put(1, "end", *[move.finish for move in moves])
     plan.run("start")
     rows = dh_ref.shape[0]
@@ -528,7 +700,7 @@
     x = (x_ref[...].T if turned else x_ref[...]).astype(f32)
     factor = norm(x)
     unit = x * factor
-    gain = gain_ref[...]
+    gain = gain_ref[row : row + 1, :]
     n1t_ref[:, here] = (unit * gain).astype(bf16).T
     scaled = dn * gain
     dx = dh_ref[...] + factor * (
@@ -545,6 +717,8 @@
     def _():
         gain_grad_ref[...] += gain_part
 
+    plan.run("grads")
+
     @pl.when(step == pl.num_programs(0) - 1)
     def _():
         grad_ref[:, :QK_WIDTH] = nn(n1t_ref[...], dqk_ref[...]).astype(bf16)
@@ -555,25 +729,19 @@
 
 
 def ff_forward_kernel(
-    layer, count, steps, h_ref, live_ref, gain_ref, wg_ref, wu_ref, wd_ref, *rest
+    row, layer, count, steps, h_ref, live_ref, gain_ref, wg_ref, wu_ref, wd_ref, *rest
 ):
     shards, (y_ref, *rest) = rest[:count], rest[count:]
     wholes, sems = rest[:count], rest[count:]
     plan = Plan(pl.program_id(0), steps)
     if count:
         place = Place()
-        moves = [
-            Gather(place, layer, shards[i], wholes[i], sems[4 * i : 4 * i + 4])
-            for i in range(count)
-        ]
-        for move in moves:
-            plan.put(steps * 2 // 6, "start", move.second)
-            plan.put(steps * 5 // 6, "start", move.third)
-            plan.put(steps - 1, "end", move.finish)
-        plan.put(0, "start", place.greet, *[move.start for move in moves])
+        moves = gathers(place, [(ref, layer) for ref in shards], wholes, sems)
+        plan.put(0, "start", place.greet, *[move.line_start for move in moves])
+        feed_line(plan, ((steps * 2 // 6, "end"), (steps - 1, "end")), moves)
     plan.run("start")
     h = h_ref[...]
-    normed = (h * norm(h) * gain_ref[...]).astype(bf16)
+    normed = (h * norm(h) * gain_ref[row : row + 1, :]).astype(bf16)
     gate = nn(normed, wg_ref[...])
     up = nn(normed, wu_ref[...])
     half = 0.5 * gate
@@ -583,7 +751,7 @@
 
 
 def ff_backward_kernel(
-    last, count, steps, h_ref, dy_ref, live_ref, gain_ref, wg_ref, wu_ref, wd_ref, *rest,
+    row, last, count, steps, h_ref, dy_ref, live_ref, gain_ref, wg_ref, wu_ref, wd_ref, *rest,
 ):
     sources, rest = rest[:count], rest[count:]
     if last:
@@ -595,23 +763,20 @@
     plan = Plan(step, steps)
     if count:
         place = Place()
-        moves = [
-            Reduce(place, sources[i], results[i], buffers[11 * i : 11 * i + 11])
-            for i in range(count)
-        ]
-        plan.put(0, "start", place.greet, *[move.start for move in moves])
-        for move in moves:
-            plan.put(steps * 1 // 6, "start", move.second)
-            plan.put(steps * 4 // 6, "start", move.third)
-            plan.put(steps * 5 // 6, "end", move.fourth)
-            plan.put(steps - 1, "last", move.finish)
+        one, two = reduces(place, sources, results, buffers)
+        plan.put(0, "start", place.greet, one.start, two.start)
+        plan.put(0, "middle", one.second, two.second)
+        plan.put(steps * 3 // 6, "middle", one.third)
+        plan.put(steps * 4 // 6, "end", one.fourth, two.third)
+        plan.put(steps - 1, "half", two.fourth)
+        plan.put(steps - 1, "last", one.finish, two.finish)
     plan.run("start")
     rows = h_ref.shape[0]
     here = pl.ds(pl.multiple_of(step * rows, rows), rows)
     h = h_ref[...]
     factor = norm(h)
     unit = h * factor
-    gain = gain_ref[...]
+    gain = gain_ref[row : row + 1, :]
     normed = (unit * gain).astype(bf16)
     n2t_ref[:, here] = normed.T
     live = live_ref[...]
@@ -624,6 +789,7 @@
     silu = gate * sig
     inner = (silu * up).astype(bf16)
     m_ref[here, :] = inner
+    plan.run("middle")
     dm = nt(e, wd_ref[...]).astype(bf16).astype(f32)
     dgate = (dm * up * (sig + silu * (1.0 - sig))).astype(bf16)
     dup = (dm * silu).astype(bf16)
@@ -646,14 +812,24 @@
     def _():
         gain_grad_ref[...] += gain_part
 
-    @pl.when(step == pl.num_programs(0) - 1)
+    def weight_grads(first):
+        cols = slice(first, first + 512)
+        gg_ref[:, cols] = nn(n2t_ref[...], dg_ref[:, cols]).astype(bf16)
+        gu_ref[:, cols] = nn(n2t_ref[...], du_ref[:, cols]).astype(bf16)
+        gd_ref[cols, :] = nn(et_ref[...], m_ref[:, cols]).astype(bf16).T
+
+    ff = m_ref.shape[1]
+
+    @pl.when(step == steps - 1)
     def _():
-        ff = m_ref.shape[1]
-        for first in range(0, ff, 512):
-            cols = slice(first, first + 512)
-            gg_ref[:, cols] = nn(n2t_ref[...], dg_ref[:, cols]).astype(bf16)
-            gu_ref[:, cols] = nn(n2t_ref[...], du_ref[:, cols]).astype(bf16)
-            gd_ref[cols, :] = nn(et_ref[...], m_ref[:, cols]).astype(bf16).T
+        weight_grads(0)
+
+    plan.run("half")
+
+    @pl.when(step == steps - 1)
+    def _():
+        for first in range(512, ff, 512):
+            weight_grads(first)
 
     plan.run("last")
 
@@ -700,14 +876,9 @@
 
 
 def attn_forward(
-    x, segment, live, table, gain, weight, turned, collective_id=None, layer=None, shards=()
+    x, segment, live, table, gain, weight, row, turned, collective_id=None, halves=()
 ):
     total, width = x.shape[::-1] if turned else x.shape
-    copies, devices = lax.axis_size("rep"), lax.axis_size("fsdp")
-    wholes = [shape((devices,) + w.shape[1:], bf16) for w in shards]
-    sems = []
-    for _ in shards:
-        sems += Gather.semaphores(copies, devices // 2)
     size = total // MICRO
     outs = [
         shape((total, width), f32),
@@ -717,7 +888,7 @@
         shape((LSE_ROWS, total), f32),
     ]
     return pl.pallas_call(
-        functools.partial(attn_forward_kernel, layer, len(shards), turned),
+        functools.partial(attn_forward_kernel, row, len(halves), turned),
         grid=(MICRO,),
         in_specs=[
             turned_spec(size, width) if turned else row_spec(size, width),
@@ -728,33 +899,31 @@
             whole_spec(gain.shape),
             whole_spec(weight.shape),
         ]
-        + [any_spec() for _ in shards],
+        + [any_spec() for _ in halves],
         out_specs=[row_spec(size, o.shape[1]) for o in outs[:4]]
         + [pl.BlockSpec((LSE_ROWS, size), lambda i: (0, i))]
-        + [any_spec() for _ in shards],
-        out_shape=outs + wholes,
-        scratch_shapes=sems,
+        + [any_spec() for _ in halves],
+        out_shape=outs + [shape(w.shape, bf16) for w in halves],
+        scratch_shapes=gather_semaphores(len(halves)),
+        input_output_aliases={7 + k: 5 + k for k in range(len(halves))},
         compiler_params=params(collective_id),
         cost_estimate=cost(2 * total * (width * 1536 + size * Q_WIDTH * 4), x, weight, *outs),
         name="attn_fwd",
-    )(x, segment.reshape(-1, 1), segment.reshape(MICRO, 1, size), live, table, gain, weight, *shards)
+    )(x, segment.reshape(-1, 1), segment.reshape(MICRO, 1, size), live, table, gain, weight, *halves)
 
 
 def attn_backward(
-    x, dh, segment, live, table, gain, weight, saved, turned, collective_id=None, sources=()
+    x, dh, segment, live, table, gain, weight, saved, row, turned, collective_id=None, sources=()
 ):
     total, width = dh.shape
-    copies, devices = lax.axis_size("rep"), lax.axis_size("fsdp")
     sums = [shape(g.shape[1:], f32) for g in sources]
-    buffers = []
-    for g in sources:
-        buffers += Reduce.scratch(g.shape[1:], copies, devices // 2)
+    buffers = reduce_buffers(sources)
     size = total // MICRO
     qk, v, a, lse = saved
     outs = [shape(x.shape, f32), shape(weight.shape, bf16), shape((1, width), f32)]
     x_spec = turned_spec(size, width) if turned else row_spec(size, width)
     return pl.pallas_call(
-        functools.partial(attn_backward_kernel, len(sources), turned),
+        functools.partial(attn_backward_kernel, row, len(sources), turned),
         grid=(MICRO,),
         in_specs=[
             x_spec,
@@ -795,11 +964,19 @@
     )
 
 
+CHUNK = 512
+
+
+def windows(sources):
+    return [(i, first) for i, g in enumerate(sources) for first in range(0, g.shape[2], CHUNK)]
+
+
 def reduce_kernel(count, *refs):
     sources, results, buffers = refs[:count], refs[count : 2 * count], refs[2 * count :]
     place = Place()
     moves = [
-        Reduce(place, sources[i], results[i], buffers[11 * i : 11 * i + 11]) for i in range(count)
+        Reduce(place, sources[i], results[i], buffers[11 * n : 11 * n + 11], first, CHUNK)
+        for n, (i, first) in enumerate(windows(sources))
     ]
     place.greet()
     for stage in ("start", "second", "third", "fourth", "finish"):
@@ -810,8 +987,8 @@
 def reduce_alone(collective_id, *sources):
     copies, devices = lax.axis_size("rep"), lax.axis_size("fsdp")
     buffers = []
-    for g in sources:
-        buffers += Reduce.scratch(g.shape[1:], copies, devices // 2)
+    for i, _ in windows(sources):
+        buffers += Reduce.scratch((sources[i].shape[1], CHUNK), copies, devices // 2)
     return pl.pallas_call(
         functools.partial(reduce_kernel, len(sources)),
         in_specs=[any_spec() for _ in sources],
@@ -825,31 +1002,28 @@
     )(*sources)
 
 
-def ff_forward(h, live, gain, wg, wu, wd, collective_id=None, layer=None, shards=()):
+def ff_forward(h, live, gain, wg, wu, wd, row, collective_id=None, layer=None, shards=()):
     total, width = h.shape
-    copies, devices = lax.axis_size("rep"), lax.axis_size("fsdp")
+    devices = lax.axis_size("fsdp")
     wholes = [shape((devices,) + w.shape[1:], bf16) for w in shards]
-    sems = []
-    for _ in shards:
-        sems += Gather.semaphores(copies, devices // 2)
     size = tile_of(total)
     out = shape((total, width), f32)
     return pl.pallas_call(
-        functools.partial(ff_forward_kernel, layer, len(shards), total // size),
+        functools.partial(ff_forward_kernel, row, layer, len(shards), total // size),
         grid=(total // size,),
         in_specs=[row_spec(size, width), row_spec(size, 1), whole_spec(gain.shape)]
         + [whole_spec(w.shape) for w in (wg, wu, wd)]
         + [any_spec() for _ in shards],
         out_specs=[row_spec(size, width)] + [any_spec() for _ in shards],
         out_shape=[out] + wholes,
-        scratch_shapes=sems,
+        scratch_shapes=gather_semaphores(len(shards)),
         compiler_params=params(collective_id),
         cost_estimate=cost(6 * total * wg.size, h, wg, wu, wd, out),
         name="ff_fwd",
     )(h, live, gain, wg, wu, wd, *shards)
 
 
-def ff_backward(h, dy, live, gain, wg, wu, wd, last, collective_id=None, sources=()):
+def ff_backward(h, dy, live, gain, wg, wu, wd, row, last, collective_id=None, sources=()):
     total, width = h.shape
     ff = wg.shape[1]
     size = tile_of(total)
@@ -860,11 +1034,8 @@
         shape(wd.shape, bf16),
         shape((1, width), f32),
     ]
-    copies, devices = lax.axis_size("rep"), lax.axis_size("fsdp")
     sums = [shape(g.shape[1:], f32) for g in sources]
-    buffers = []
-    for g in sources:
-        buffers += Reduce.scratch(g.shape[1:], copies, devices // 2)
+    buffers = reduce_buffers(sources)
     outs += sums
     specs = [row_spec(size, width)] + [whole_spec(o.shape) for o in outs[1:]]
     dy_spec = row_spec(size, width)
@@ -873,7 +1044,7 @@
         dy_spec = turned_spec(size, width)
         specs = [dy_spec] + specs
     return pl.pallas_call(
-        functools.partial(ff_backward_kernel, last, len(sources), total // size),
+        functools.partial(ff_backward_kernel, row, last, len(sources), total // size),
         grid=(total // size,),
         in_specs=[row_spec(size, width), dy_spec, row_spec(size, 1)]
         + [whole_spec(gain.shape)]
@@ -908,30 +1079,19 @@
     rows, ff = gate_weight.shape[1:]
     width = rows * devices
     down_rows = down_weight.shape[1]
-    live, table = geometry(segment)
-
-    gains = jnp.concatenate([attn_gain, mlp_gain]).reshape(1, 4 * rows)
-    gains = jnp.pad(gains, ((0, 0), (0, QK_WIDTH + Q_WIDTH + KV_WIDTH - 4 * rows)))
+    copies = lax.axis_size("rep")
     shards = (gate_weight, up_weight, down_weight)
-    copies = lax.axis_size("rep")
-    direct = all(can_cut(w.shape[1:], copies) for w in shards)
-    attn_w = []
-    for layer in range(DECODER_LAYERS):
-        packed = jnp.concatenate(
-            [w_query[layer], key_weight[layer], w_out[layer], value_weight[layer]], axis=1
-        )
-        if layer == 0:
-            packed = jnp.concatenate([packed, gains])
-            whole = lax.all_gather(packed, "fsdp", axis=0, tiled=False)
-            all_gains = whole[:, rows, : 4 * rows].reshape(devices, 4, rows)
-            all_gains = all_gains.transpose(1, 0, 2).reshape(4, 1, width).astype(f32)
-            attn_w.append(whole[:, :rows].reshape(width, -1))
-        else:
-            attn_w.append(lax.all_gather(packed, "fsdp", axis=0, tiled=True))
+    packed_gains = jnp.concatenate([attn_gain, mlp_gain]).reshape(1, 4 * rows)
+    room = CHUNK * -(-4 * rows // CHUNK)
+    packed_gains = jnp.pad(packed_gains, ((0, 15), (0, room - 4 * rows)))[None]
+    packed = [
+        jnp.concatenate([w_query[i], key_weight[i], w_out[i], value_weight[i]], axis=1)[None]
+        for i in range(DECODER_LAYERS)
+    ]
+    direct = all(can_cut(w.shape[1:], copies) for w in shards) and can_cut((16, CHUNK), copies)
 
     def whole(shard):
-        gathered = lax.all_gather(shard, "fsdp", axis=0, tiled=False)
-        return gathered
+        return lax.all_gather(shard, "fsdp", axis=0, tiled=True)
 
     def feed_of(gathered):
         gate, up, down = gathered
@@ -942,55 +1102,64 @@
         return [g.reshape((devices,) + d) for g, d in zip(grads, dims)]
 
     tokens, cotangent = tokens.T, cotangent.T
-    args0 = (tokens, segment, live, table, all_gains[0], attn_w[0], True)
     if direct:
-        down1 = whole(down_weight[1])
-        h0, *kept0 = attn_forward(*args0, 0, 0, shards)
+        live, table, weight0, gains, *feed0 = prepare(
+            segment, (packed[0], packed_gains), shards, 0
+        )
+        packed[1], live = lax.optimization_barrier((packed[1], live))
+    else:
+        live, table = prepare(segment)
+        weight0, gains = whole(packed[0]), whole(packed_gains)
+    attn_w = [weight0.reshape(width, ff), whole(packed[1]).reshape(width, ff)]
+    gains = gains[:, 0, : 4 * rows].reshape(devices, 4, rows)
+    gains = gains.transpose(1, 0, 2).reshape(4, width).astype(f32)
+    args0 = (tokens, segment, live, table, gains, attn_w[0], 0, True)
+    if direct:
+        h0, *kept0 = attn_forward(*args0, 1, feed0)
         kept0, feed0 = kept0[:4], feed_of(kept0[4:])
-        x1, gate1 = ff_forward(h0, live, all_gains[2], *feed0, 1, 1, shards[:1])
+        x1, *feed1 = ff_forward(h0, live, gains, *feed0, 2, 2, 1, shards)
     else:
         h0, *kept0 = attn_forward(*args0)
         feed0 = feed_of([whole(w[0]) for w in shards])
-        x1 = ff_forward(h0, live, all_gains[2], *feed0)[0]
-    args1 = (x1, segment, live, table, all_gains[1], attn_w[1], False)
+        x1 = ff_forward(h0, live, gains, *feed0, 2)[0]
+    args1 = (x1, segment, live, table, gains, attn_w[1], 1, False)
     if direct:
-        h1, *kept1 = attn_forward(*args1, 2, 1, shards[1:2])
-        kept1, feed1 = kept1[:4], feed_of([gate1, kept1[4], down1])
+        h1, *kept1 = attn_forward(*args1, 3, feed1)
+        kept1, feed1 = kept1[:4], feed_of(kept1[4:])
     else:
         h1, *kept1 = attn_forward(*args1)
         feed1 = feed_of([whole(w[1]) for w in shards])
     out_tokens, dh1, gg1, gu1, gd1, mg1 = ff_backward(
-        h1, cotangent, live, all_gains[3], *feed1, True
+        h1, cotangent, live, gains, *feed1, 3, True
     )
     grads1 = split((gg1, gu1, gd1))
-    args1 = (x1, dh1, segment, live, table, all_gains[1], attn_w[1], kept1, False)
+    args1 = (x1, dh1, segment, live, table, gains, attn_w[1], kept1, 1, False)
     if direct:
-        dx1, ga1, ag1, *sums1 = attn_backward(*args1, 3, grads1[:2])
+        dx1, ga1, ag1, *sums1 = attn_backward(*args1, 4, grads1[:2])
     else:
         dx1, ga1, ag1 = attn_backward(*args1)
     ga1 = ga1.reshape(devices, rows, ff)
-    args0 = (h0, dx1, live, all_gains[2], *feed0, False)
+    args0 = (h0, dx1, live, gains, *feed0, 2, False)
     if direct:
-        dh0, gg0, gu0, gd0, mg0, down1, attn1 = ff_backward(*args0, 4, (grads1[2], ga1))
+        dh0, gg0, gu0, gd0, mg0, down1, attn1 = ff_backward(*args0, 5, (grads1[2], ga1))
         sums1.append(down1)
     else:
         sums1, attn1 = [sum_shards(g) for g in grads1], sum_shards(ga1)
         dh0, gg0, gu0, gd0, mg0 = ff_backward(*args0)
     grads0 = split((gg0, gu0, gd0))
-    args0 = (tokens, dh0, segment, live, table, all_gains[0], attn_w[0], kept0, True)
+    args0 = (tokens, dh0, segment, live, table, gains, attn_w[0], kept0, 0, True)
     if direct:
-        dx0, ga0, ag0, *sums0 = attn_backward(*args0, 5, grads0)
+        dx0, ga0, ag0, *sums0 = attn_backward(*args0, 6, grads0)
     else:
         dx0, ga0, ag0 = attn_backward(*args0)
         sums0 = [sum_shards(g) for g in grads0]
     ga0 = ga0.reshape(devices, rows, ff)
-    room = 512 * -(-4 * rows // 512)
     gain_grads = jnp.concatenate(
         [g.reshape(devices, 1, rows).astype(bf16) for g in (ag0, ag1, mg0, mg1)], axis=2
     )
     gain_grads = jnp.pad(gain_grads, ((0, 0), (0, 15), (0, room - 4 * rows)))
     if direct:
-        attn0, last = reduce_alone(6, ga0, gain_grads)
+        attn0, last = reduce_alone(7, ga0, gain_grads)
     else:
         attn0, last = sum_shards(ga0), sum_shards(gain_grads)
     last = last[0]

time: 405 us -> 387 us (0.956)
  waiting for transfers between devices: 18.9 us -> 0.04 us
  Pallas kernels: 334 us -> 346 us
  local copies, waits for them, and re-layouts: 20.9 us -> 13.9 us
  other arithmetic: 12.3 us -> 7.69 us
    all_gather x3 -> x1, waiting for transfers between devices: 18.8 us -> 0.02 us  [whole(): return lax.all_gather(shard, 'fsdp', axis=0, tiled=True)]
    pallas_call x7 -> x8, Pallas kernels: 308 us -> 320 us  [the longest x2 108 us: attn_backward(): pl.pallas_call(functools.partial(attn_backward_kernel, row, len(sources),...]
  transfers between devices with their start and end apart: 3 -> 1, of which waited for: 1 -> 0; matrix products, arithmetic and copies ran while one was open for 5% -> 0% of each run, Pallas kernels for 26% -> 15%
where the time goes in v3:
time: 387 us; the launch traced here: 382 us
  Pallas kernels  346 us (89%)
  between operations  14.5 us (4%)
  local copies, waits for them, and re-layouts  13.9 us (4%)
  other arithmetic  7.69 us (2%)
    pallas_call x2, Pallas kernels, attn_backward(): pl.pallas_call(functools.partial(attn_backward_kernel, row, len(sources),...  108 us
    pallas_call x2, Pallas kernels, ff_backward(): pl.pallas_call(functools.partial(ff_backward_kernel, row, last, len(sourc...  86.4 us
    pallas_call x2, Pallas kernels, attn_forward(): pl.pallas_call(functools.partial(attn_forward_kernel, row, len(halves), t...  56.9 us
    pallas_call x1, Pallas kernels, prepare(): pl.pallas_call(functools.partial(prepare_kernel, (len(shards), len(feed))...  39.1 us
    pallas_call x1, Pallas kernels, ff_forward(): pl.pallas_call(functools.partial(ff_forward_kernel, row, layer, len(shard...  29.2 us
    pallas_call x1, Pallas kernels, reduce_alone(): pl.pallas_call(functools.partial(reduce_kernel, len(sources)), in_specs=[...  25.7 us
  transfers between devices with their start and end apart: 1, of which 0 were waited for; matrix products, arithmetic and copies ran while one was open for 0% of the time, Pallas kernels for 15%

profile of v3, /device:TPU:0, one launch (start us, length us, event | category | flops | bytes accessed | tf_op | source)
XLA Modules:
  0.0 381.7 jit_solution(135688203813185750)
XLA Ops:
  7.2 1.3 reshape.159.row_ref
  8.5 1.8 reshape.181.column_ref
  10.4 0.6 maximum_bitcast_fusion.frequency_ref
  11.0 0.7 pad_maximum_fusion.4
  11.7 0.6 pad_bitcast_fusion.refs_1_
  12.4 0.8 slice_bitcast_fusion.4
  13.2 1.1 slice_bitcast_fusion
  14.3 0.8 concatenate.17
  15.1 0.8 concatenate.15
  15.8 39.1 %prepare.1 = (f32[1536,1]{1,0:T(8,128)}, f32[1536,256]{1,0:T(8,128)}, bf16[8,72,1536]{2,1,0:T(8,128)(2,1)}, bf16[8,16,512]{2,1,0:T(8,128)(2,1)}, bf16[8,72,1536]...) custom-call(s32[1536,1]{1,0:T(8,128)} %reshape.181.column_ref, ...), custom_call_target="tpu_custom_call" | custom-call | tf_op jit(solution)/shard_map/prepare/pallas_call | solution.py:551
  54.9 0.8 convert_reduce_fusion
  55.9 0.7 reshape.179.gain_ref
  56.6 28.6 %attn_fwd.2 = (f32[1536,576]{1,0:T(8,128)}, bf16[1536,768]{1,0:T(8,128)(2,1)}, bf16[1536,192]{1,0:T(8,128)(2,1)}, bf16[1536,576]{1,0:T(8,128)(2,1)}, f32[16,1536...) custom-call(bf16[576,1536]{1,0:T(8,128)(2,1)} %bitcast.71, ...), custom_call_target="tpu_custom_call", output_to_operand_aliasing={{5}: (7, {}), {6}: (8, {}), {7}: (9, {})} | custom-call | flops 8153726976 | bytes 11894784 | tf_op jit(solution)/shard_map/attn_fwd/pallas_call | solution.py:890
  85.1 29.2 %ff_fwd.1 = (f32[1536,576]{1,0:T(8,128)}, bf16[8,72,1536]{2,1,0:T(8,128)(2,1)}, bf16[8,72,1536]{2,1,0:T(8,128)(2,1)}, bf16[8,192,576]{2,1,0:T(8,128)(2,1)}) custom-call(f32[1536,576]{1,0:T(8,128)} %get-tuple-element.74.h_ref, f32[1536,1]{1,0:T(8,128)} %get-tuple-element.67.live_ref, f32[4,576]{1,0:T(4,128)} %reshape.179.gain_ref, ...), custom_call_target="tpu_custom_call" | custom-call | flops 8153726976 | bytes 12386304 | tf_op jit(solution)/shard_map/ff_fwd/pallas_call | solution.py:1011
  114.3 28.3 %attn_fwd.3 = (f32[1536,576]{1,0:T(8,128)}, bf16[1536,768]{1,0:T(8,128)(2,1)}, bf16[1536,192]{1,0:T(8,128)(2,1)}, bf16[1536,576]{1,0:T(8,128)(2,1)}, f32[16,1536...) custom-call(f32[1536,576]{1,0:T(8,128)} %get-tuple-element.78.x_ref,, ...), custom_call_target="tpu_custom_call", output_to_operand_aliasing={{5}: (7, {}), {6}: (8, {}), {7}: (9, {})} | custom-call | flops 8153726976 | bytes 13664256 | tf_op jit(solution)/shard_map/attn_fwd/pallas_call | solution.py:890
  142.7 39.9 %ff_bwd.2 = (bf16[576,1536]{1,0:T(8,128)(2,1)}, f32[1536,576]{1,0:T(8,128)}, bf16[576,1536]{1,0:T(8,128)(2,1)}, bf16[576,1536]{1,0:T(8,128)(2,1)}, bf16[1536,576]{1,0:T(8,128)(2,1)}, /*index=5*/f32[1,576]{1,0:T(1,128)}) custom-call(f32[1536,576]{1,0:T(8,128)} %get-tuple-element.83.h_ref, bf16[576,1536]{1,0:T(8,128)(2,1)} %bitcast.70, ...), custom_call_target="tpu_custom_call" | custom-call | flops 21743271936 | bytes 21235968 | tf_op jit(solution)/shard_map/ff_bwd/pallas_call | solution.py:1046
  182.6 49.6 %attn_bwd.2 = (f32[1536,576]{1,0:T(8,128)}, bf16[576,1536]{1,0:T(8,128)(2,1)}, f32[1,576]{1,0:T(1,128)}, f32[72,1536]{1,0:T(8,128)}, f32[72,1536]{1,0:T(8,128)}) custom-call(f32[1536,576]{1,0:T(8,128)} %get-tuple-element.78.x_ref, f32[1536,576]{1,0:T(8,128)} %get-tuple-element.88.dh_ref, s32[1536,1]{1,0:T(8,128)} %reshape.181.column_ref, ...), custom_call_target="tpu_custom_call" | custom-call | flops 19025362944 | bytes 14158080 | tf_op jit(solution)/shard_map/attn_bwd/pallas_call | solution.py:925
  232.3 46.4 %ff_bwd.3 = (f32[1536,576]{1,0:T(8,128)}, bf16[576,1536]{1,0:T(8,128)(2,1)}, bf16[576,1536]{1,0:T(8,128)(2,1)}, bf16[1536,576]{1,0:T(8,128)(2,1)}, f32[1,576]{1,...) custom-call(f32[1536,576]{1,0:T(8,128)} %get-tuple-element.74.h_ref, f32[1536,576]{1,0:T(8,128)} %get-tuple-element.95.dy_ref, ...), custom_call_target="tpu_custom_call" | custom-call | flops 21743271936 | bytes 22120704 | tf_op jit(solution)/shard_map/ff_bwd/pallas_call | solution.py:1046
  278.7 58.7 %attn_bwd.3 = (f32[576,1536]{1,0:T(8,128)}, bf16[576,1536]{1,0:T(8,128)(2,1)}, f32[1,576]{1,0:T(1,128)}, f32[72,1536]{1,0:T(8,128)}, f32[72,1536]{1,0:T(8,128)}, /*index=5*/f32[192,576]{1,0:T(8,128)}) custom-call(bf16[576,1536]{1,0:T(8,128)(2,1)} %bitcast.72, f32[1536,576]{1,0:T(8,128)} %get-tuple-element.98.dh_ref, s32[1536,1]{1,0:T(8,128)} %reshape.181.column_ref, ...), custom_call_target="tpu_custom_call" | custom-call | flops 19025362944 | bytes 12388608 | tf_op jit(solution)/shard_map/attn_bwd/pallas_call | solution.py:925
  337.5 0.7 convert_reduce_fusion.4
  338.6 0.1 fusion.11.refs_1_
  338.8 1.5 copy-done
  340.2 25.7 %reduce.19 = (f32[72,1536]{1,0:T(8,128)S(1)}, f32[16,512]{1,0:T(8,128)S(1)}) custom-call(bf16[8,72,1536]{2,1,0:T(8,128)(2,1)S(1)} %bitcast.55, bf16[8,16,512]{2,1,0:T(8,128)(2,1)S(1)} %fusion.11.refs_1_), custom_call_target="tpu_custom_call" | custom-call | tf_op jit(solution)/shard_map/reduce/pallas_call | solution.py:992
  366.0 0.9 fusion.6
  366.8 0.9 pad_maximum_fusion.3
  367.8 0.6 reshape.178
  368.5 0.6 reshape.177
  369.1 1.0 pad_maximum_fusion.1
  370.1 1.0 pad_maximum_fusion.2
  371.1 1.0 pad_maximum_fusion
  372.1 0.8 copy-done.1
  372.9 1.8 copy.59
  (37 shorter events, 0.8 us)
Async XLA Ops:
  7.2 107.2 %all-gather.2.cloned.1.call-start = ((), (), s32[]{:S(2)}) async-start(), calls=%async_computation | async-start | bytes 1990656 | tf_op jit(solution)/shard_map/all_gather | solution.py:1094
  278.7 59.6 %copy-start.11 = (f32[1,576]{1,0:T(1,128)S(1)}, f32[1,576]{1,0:T(1,128)}, u32[]{:S(2)}) copy-start(f32[1,576]{1,0:T(1,128)} %get-tuple-element.110) | copy-start | bytes 6916
  278.7 59.7 %copy-start.10 = (f32[1,576]{1,0:T(1,128)S(1)}, f32[1,576]{1,0:T(1,128)}, u32[]{:S(2)}) copy-start(f32[1,576]{1,0:T(1,128)} %get-tuple-element.109) | copy-start | bytes 6916
  278.7 59.8 %copy-start.9 = (f32[1,576]{1,0:T(1,128)S(1)}, f32[1,576]{1,0:T(1,128)}, u32[]{:S(2)}) copy-start(f32[1,576]{1,0:T(1,128)} %get-tuple-element.111) | copy-start | bytes 6916
  278.7 87.2 %copy-start.2 = (f32[72,1536]{1,0:T(8,128)S(1)}, f32[72,1536]{1,0:T(8,128)}, u32[]{:S(2)}) copy-start(f32[72,1536]{1,0:T(8,128)} %get-tuple-element.114) | copy-start | bytes 1327108
  338.7 1.5 copy-start
  365.9 3.2 copy-start.6
  366.0 3.2 copy-start.8
  366.8 3.3 copy-start.5
  366.8 3.3 copy-start.7
  369.1 2.0 copy-start.3
  369.1 2.0 copy-start.4
  370.1 2.8 copy-start.1
Sparse Core Ops, SparseCore 0:
  55.1 24.6 all-gather.1

commit v4 on v3

--- a/solution.py
+++ b/solution.py
@@ -477,7 +477,7 @@
 def feed_line(plan, points, moves):
     gate, up, down = moves
     (one, two), last = points[0], points[1]
-    plan.put(one, two, gate.line_end, gate.across_start)
+    plan.put(one, two, gate.line_end, gate.across_start, up.line_start, down.line_start)
     plan.put(*last, up.line_end, down.line_end, gate.across_end, gate.across_done)
     plan.put(*last, *[move.line_done for move in moves])
 
@@ -493,7 +493,7 @@
         moves = gathers(place, [(ref, 0) for ref in shards], wholes, sems)
         first, feed = moves[:attn_count], moves[attn_count:]
         place.greet()
-        for move in moves:
+        for move in first:
             move.line_start()
     size = row_ref.shape[2]
     live_ref[...] = jnp.where(column_ref[...] >= 0, 1.0, 0.0).astype(f32)
@@ -508,6 +508,7 @@
         for move in first:
             move.line_end()
             move.across_start()
+        feed[0].line_start()
     lane = lax.broadcasted_iota(jnp.int32, (size, 128), 1)
     sign = jnp.where(lane % HEAD_WIDTH < HEAD_WIDTH // 2, -1.0, 1.0)
     for block in range(MICRO):
@@ -519,6 +520,8 @@
         gate = feed[0]
         gate.line_end()
         gate.across_start()
+        for move in feed[1:]:
+            move.line_start()
         for move in first:
             move.across_end()
             move.own().wait()
@@ -569,9 +572,10 @@
     if count:
         place = Place()
         gate, up, down = gathers(place, (), wholes, sems)
-        plan.put(0, "start", place.greet, up.across_start, down.across_start, gate.pair_start)
+        plan.put(0, "start", place.greet, up.across_start, gate.pair_start)
+        plan.put(0, 7, down.across_start)
         plan.put(0, "end", up.across_end, up.pair_start)
-        plan.put(1, 6, down.across_end, down.pair_start)
+        plan.put(1, 7, down.across_end, down.pair_start)
         plan.put(1, "end", gate.pair_done, up.across_done, up.pair_done)
         plan.put(1, "end", down.across_done, down.pair_done)
     plan.run("start")
@@ -631,13 +635,15 @@
         moves = reduces(place, sources, results, buffers)
         plan.put(0, "start", place.greet, *[move.start for move in moves])
         one, two = moves[:2]
-        plan.put(0, 0, one.second, two.second)
+        plan.put(0, 0, one.second)
+        plan.put(0, 4, two.second)
         plan.put(0, 8, one.third)
         plan.put(1, 2, two.third)
         if count == 3:
             plan.put(0, 0, moves[2].second)
-            plan.put(1, 3, moves[2].third, one.fourth)
-            plan.put(1, 6, moves[2].fourth)
+            plan.put(1, 3, one.fourth)
+            plan.put(1, 4, moves[2].third)
+            plan.put(1, 7, moves[2].fourth)
         else:
             plan.put(1, 1, one.fourth)
         plan.put(1, "grads", two.fourth)
@@ -737,7 +743,7 @@
     if count:
         place = Place()
         moves = gathers(place, [(ref, layer) for ref in shards], wholes, sems)
-        plan.put(0, "start", place.greet, *[move.line_start for move in moves])
+        plan.put(0, "start", place.greet, moves[0].line_start)
         feed_line(plan, ((steps * 2 // 6, "end"), (steps - 1, "end")), moves)
     plan.run("start")
     h = h_ref[...]
@@ -765,7 +771,8 @@
         place = Place()
         one, two = reduces(place, sources, results, buffers)
         plan.put(0, "start", place.greet, one.start, two.start)
-        plan.put(0, "middle", one.second, two.second)
+        plan.put(0, "middle", one.second)
+        plan.put(steps * 2 // 6, "middle", two.second)
         plan.put(steps * 3 // 6, "middle", one.third)
         plan.put(steps * 4 // 6, "end", one.fourth, two.third)
         plan.put(steps - 1, "half", two.fourth)

time: 387 us -> 390 us (level)
  no operation moved by 1% of the time
where the time goes in v4:
time: 390 us; the launch traced here: 385 us
  Pallas kernels  349 us (89%)
  between operations  14.5 us (4%)
  local copies, waits for them, and re-layouts  13.9 us (4%)
  other arithmetic  7.69 us (2%)
    pallas_call x2, Pallas kernels, attn_backward(): pl.pallas_call(functools.partial(attn_backward_kernel, row, len(sources),...  111 us
    pallas_call x2, Pallas kernels, ff_backward(): pl.pallas_call(functools.partial(ff_backward_kernel, row, last, len(sourc...  86.5 us
    pallas_call x2, Pallas kernels, attn_forward(): pl.pallas_call(functools.partial(attn_forward_kernel, row, len(halves), t...  57.6 us
    pallas_call x1, Pallas kernels, prepare(): pl.pallas_call(functools.partial(prepare_kernel, (len(shards), len(feed))...  39.1 us
    pallas_call x1, Pallas kernels, ff_forward(): pl.pallas_call(functools.partial(ff_forward_kernel, row, layer, len(shard...  28.9 us
    pallas_call x1, Pallas kernels, reduce_alone(): pl.pallas_call(functools.partial(reduce_kernel, len(sources)), in_specs=[...  25.7 us
  transfers between devices with their start and end apart: 1, of which 0 were waited for; matrix products, arithmetic and copies ran while one was open for 0% of the time, Pallas kernels for 15%

profile of v4, /device:TPU:0, one launch (start us, length us, event | category | flops | bytes accessed | tf_op | source)
XLA Modules:
  0.0 384.9 jit_solution(15233660653308687391)
XLA Ops:
  7.2 1.3 reshape.159.row_ref
  8.5 1.8 reshape.181.column_ref
  10.4 0.6 maximum_bitcast_fusion.frequency_ref
  11.0 0.7 pad_maximum_fusion.4
  11.7 0.6 pad_bitcast_fusion.refs_1_
  12.4 0.8 slice_bitcast_fusion.4
  13.2 1.1 slice_bitcast_fusion
  14.3 0.8 concatenate.17
  15.1 0.8 concatenate.15
  15.8 39.1 %prepare.1 = (f32[1536,1]{1,0:T(8,128)}, f32[1536,256]{1,0:T(8,128)}, bf16[8,72,1536]{2,1,0:T(8,128)(2,1)}, bf16[8,16,512]{2,1,0:T(8,128)(2,1)}, bf16[8,72,1536]...) custom-call(s32[1536,1]{1,0:T(8,128)} %reshape.181.column_ref, ...), custom_call_target="tpu_custom_call" | custom-call | tf_op jit(solution)/shard_map/prepare/pallas_call | solution.py:554
  55.0 0.8 convert_reduce_fusion
  55.9 0.7 reshape.179.gain_ref
  56.6 29.0 %attn_fwd.2 = (f32[1536,576]{1,0:T(8,128)}, bf16[1536,768]{1,0:T(8,128)(2,1)}, bf16[1536,192]{1,0:T(8,128)(2,1)}, bf16[1536,576]{1,0:T(8,128)(2,1)}, f32[16,1536...) custom-call(bf16[576,1536]{1,0:T(8,128)(2,1)} %bitcast.71, ...), custom_call_target="tpu_custom_call", output_to_operand_aliasing={{5}: (7, {}), {6}: (8, {}), {7}: (9, {})} | custom-call | flops 8153726976 | bytes 11894784 | tf_op jit(solution)/shard_map/attn_fwd/pallas_call | solution.py:897
  85.6 28.9 %ff_fwd.1 = (f32[1536,576]{1,0:T(8,128)}, bf16[8,72,1536]{2,1,0:T(8,128)(2,1)}, bf16[8,72,1536]{2,1,0:T(8,128)(2,1)}, bf16[8,192,576]{2,1,0:T(8,128)(2,1)}) custom-call(f32[1536,576]{1,0:T(8,128)} %get-tuple-element.74.h_ref, f32[1536,1]{1,0:T(8,128)} %get-tuple-element.67.live_ref, f32[4,576]{1,0:T(4,128)} %reshape.179.gain_ref, ...), custom_call_target="tpu_custom_call" | custom-call | flops 8153726976 | bytes 12386304 | tf_op jit(solution)/shard_map/ff_fwd/pallas_call | solution.py:1018
  114.5 28.6 %attn_fwd.3 = (f32[1536,576]{1,0:T(8,128)}, bf16[1536,768]{1,0:T(8,128)(2,1)}, bf16[1536,192]{1,0:T(8,128)(2,1)}, bf16[1536,576]{1,0:T(8,128)(2,1)}, f32[16,1536...) custom-call(f32[1536,576]{1,0:T(8,128)} %get-tuple-element.78.x_ref,, ...), custom_call_target="tpu_custom_call", output_to_operand_aliasing={{5}: (7, {}), {6}: (8, {}), {7}: (9, {})} | custom-call | flops 8153726976 | bytes 13664256 | tf_op jit(solution)/shard_map/attn_fwd/pallas_call | solution.py:897
  143.1 39.9 %ff_bwd.2 = (bf16[576,1536]{1,0:T(8,128)(2,1)}, f32[1536,576]{1,0:T(8,128)}, bf16[576,1536]{1,0:T(8,128)(2,1)}, bf16[576,1536]{1,0:T(8,128)(2,1)}, bf16[1536,576]{1,0:T(8,128)(2,1)}, /*index=5*/f32[1,576]{1,0:T(1,128)}) custom-call(f32[1536,576]{1,0:T(8,128)} %get-tuple-element.83.h_ref, bf16[576,1536]{1,0:T(8,128)(2,1)} %bitcast.70, ...), custom_call_target="tpu_custom_call" | custom-call | flops 21743271936 | bytes 21235968 | tf_op jit(solution)/shard_map/ff_bwd/pallas_call | solution.py:1053
  183.0 49.8 %attn_bwd.2 = (f32[1536,576]{1,0:T(8,128)}, bf16[576,1536]{1,0:T(8,128)(2,1)}, f32[1,576]{1,0:T(1,128)}, f32[72,1536]{1,0:T(8,128)}, f32[72,1536]{1,0:T(8,128)}) custom-call(f32[1536,576]{1,0:T(8,128)} %get-tuple-element.78.x_ref, f32[1536,576]{1,0:T(8,128)} %get-tuple-element.88.dh_ref, s32[1536,1]{1,0:T(8,128)} %reshape.181.column_ref, ...), custom_call_target="tpu_custom_call" | custom-call | flops 19025362944 | bytes 14158080 | tf_op jit(solution)/shard_map/attn_bwd/pallas_call | solution.py:932
  232.9 46.6 %ff_bwd.3 = (f32[1536,576]{1,0:T(8,128)}, bf16[576,1536]{1,0:T(8,128)(2,1)}, bf16[576,1536]{1,0:T(8,128)(2,1)}, bf16[1536,576]{1,0:T(8,128)(2,1)}, f32[1,576]{1,...) custom-call(f32[1536,576]{1,0:T(8,128)} %get-tuple-element.74.h_ref, f32[1536,576]{1,0:T(8,128)} %get-tuple-element.95.dy_ref, ...), custom_call_target="tpu_custom_call" | custom-call | flops 21743271936 | bytes 22120704 | tf_op jit(solution)/shard_map/ff_bwd/pallas_call | solution.py:1053
  279.5 61.2 %attn_bwd.3 = (f32[576,1536]{1,0:T(8,128)}, bf16[576,1536]{1,0:T(8,128)(2,1)}, f32[1,576]{1,0:T(1,128)}, f32[72,1536]{1,0:T(8,128)}, f32[72,1536]{1,0:T(8,128)}, /*index=5*/f32[192,576]{1,0:T(8,128)}) custom-call(bf16[576,1536]{1,0:T(8,128)(2,1)} %bitcast.72, f32[1536,576]{1,0:T(8,128)} %get-tuple-element.98.dh_ref, s32[1536,1]{1,0:T(8,128)} %reshape.181.column_ref, ...), custom_call_target="tpu_custom_call" | custom-call | flops 19025362944 | bytes 12388608 | tf_op jit(solution)/shard_map/attn_bwd/pallas_call | solution.py:932
  340.7 0.7 convert_reduce_fusion.4
  341.8 0.1 fusion.11.refs_1_
  341.9 1.5 copy-done
  343.4 25.7 %reduce.19 = (f32[72,1536]{1,0:T(8,128)S(1)}, f32[16,512]{1,0:T(8,128)S(1)}) custom-call(bf16[8,72,1536]{2,1,0:T(8,128)(2,1)S(1)} %bitcast.55, bf16[8,16,512]{2,1,0:T(8,128)(2,1)S(1)} %fusion.11.refs_1_), custom_call_target="tpu_custom_call" | custom-call | tf_op jit(solution)/shard_map/reduce/pallas_call | solution.py:999
  369.1 0.9 fusion.6
  370.0 0.9 pad_maximum_fusion.3
  371.0 0.6 reshape.178
  371.6 0.6 reshape.177
  372.3 1.0 pad_maximum_fusion.1
  373.3 1.0 pad_maximum_fusion.2
  374.3 1.0 pad_maximum_fusion
  375.3 0.8 copy-done.1
  376.0 1.8 copy.59
  (37 shorter events, 0.8 us)
Async XLA Ops:
  7.2 107.3 %all-gather.2.cloned.1.call-start = ((), (), s32[]{:S(2)}) async-start(), calls=%async_computation | async-start | bytes 1990656 | tf_op jit(solution)/shard_map/all_gather | solution.py:1101
  279.5 62.0 %copy-start.11 = (f32[1,576]{1,0:T(1,128)S(1)}, f32[1,576]{1,0:T(1,128)}, u32[]{:S(2)}) copy-start(f32[1,576]{1,0:T(1,128)} %get-tuple-element.110) | copy-start | bytes 6916
  279.5 62.1 %copy-start.10 = (f32[1,576]{1,0:T(1,128)S(1)}, f32[1,576]{1,0:T(1,128)}, u32[]{:S(2)}) copy-start(f32[1,576]{1,0:T(1,128)} %get-tuple-element.109) | copy-start | bytes 6916
  279.5 62.2 %copy-start.9 = (f32[1,576]{1,0:T(1,128)S(1)}, f32[1,576]{1,0:T(1,128)}, u32[]{:S(2)}) copy-start(f32[1,576]{1,0:T(1,128)} %get-tuple-element.111) | copy-start | bytes 6916
  279.5 89.6 %copy-start.2 = (f32[72,1536]{1,0:T(8,128)S(1)}, f32[72,1536]{1,0:T(8,128)}, u32[]{:S(2)}) copy-start(f32[72,1536]{1,0:T(8,128)} %get-tuple-element.114) | copy-start | bytes 1327108
  341.9 1.5 copy-start
  369.1 3.2 copy-start.6
  369.1 3.2 copy-start.8
  370.0 3.3 copy-start.5
  370.0 3.3 copy-start.7
  372.3 2.0 copy-start.3
  372.3 2.0 copy-start.4
  373.3 2.8 copy-start.1
Sparse Core Ops, SparseCore 0:
  55.1 25.5 all-gather.1
